TPU v7x, 32 devices: a whole 2x2x4 slice. The times are simulated.
32 devices in a mesh: wide: 8 (over z, y), narrow: 4 (over x, core).
Axes of the slice: x: 2, y: 2, z: 4, core: 2. Of those that a mesh axis runs over, the one named last changes fastest.
Arguments:
- stored_features: bfloat16 [64, 16, 16, 128], P(None, 'wide', 'narrow'), may hold values from -127 to 127
- channel_scale: float32 [64], replicated, may hold values from 0.005 to 0.05
- channel_shift: float32 [64], replicated, may hold values from -0.5 to 0.5
- first_weight: bfloat16 [64, 1728], replicated, may hold values from -0.21875 to 0.21875
- second_weight: bfloat16 [128, 1728], replicated, may hold values from -0.21875 to 0.21875
- third_weight: bfloat16 [256, 3456], P('narrow'), may hold values from -0.15625 to 0.15625
Outputs:
- coarse_features: bfloat16 [256, 8, 512], P('narrow', 'wide')
All inputs are finite; a program needn't handle non-finite values.
Results may differ from a plain program's by a relative error of at most 0.0057.
Values may be sent and summed in bfloat16 or wider, within the bound.
No kernel may reach another device: no remote copies, remote signals or barrier semaphores. Data moves between devices by JAX's collectives and lax.ppermute only.
A program may use at most 64 MiB of HBM per device.

v0:
```python
import jax
import jax.numpy as jnp
from jax import lax
from jax.sharding import PartitionSpec as P


def with_halo(block, sides, width):
    for axis, dim in sides:
        count = lax.axis_size(axis)
        forward = [(i, i + 1) for i in range(count - 1)]
        backward = [(target, source) for source, target in forward]
        low = lax.ppermute(
            lax.slice_in_dim(block, block.shape[dim] - width, None, axis=dim), axis, forward
        )
        high = lax.ppermute(lax.slice_in_dim(block, 0, width, axis=dim), axis, backward)
        block = jnp.concatenate([low, block, high], axis=dim)
    return block


def convolve(padded, weight, depth_rows, height_rows):
    channels = padded.shape[0]
    width_cells = padded.shape[3]
    padded_width = jnp.pad(padded, ((0, 0), (0, 0), (0, 0), (1, 1)))
    accumulated = None
    for depth_off in range(3):
        for height_off in range(3):
            stacked = jnp.concatenate(
                [
                    padded_width[
                        :,
                        depth_off : depth_off + depth_rows,
                        height_off : height_off + height_rows,
                        width_off : width_off + width_cells,
                    ]
                    for width_off in range(3)
                ],
                axis=0,
            )
            stacked = stacked.reshape(3 * channels, -1)
            column_start = (depth_off * 3 + height_off) * 3 * channels
            weight_block = weight[:, column_start : column_start + 3 * channels]
            product = jnp.dot(weight_block, stacked, preferred_element_type=jnp.float32)
            accumulated = product if accumulated is None else accumulated + product
    return accumulated.reshape(weight.shape[0], depth_rows, height_rows, width_cells)


def body(stored_features, channel_scale, channel_shift, first_weight, second_weight, third_weight):
    depth_rows = stored_features.shape[1]
    height_rows = stored_features.shape[2]
    features = (
        stored_features.astype(jnp.float32) * channel_scale[:, None, None, None]
        + channel_shift[:, None, None, None]
    ).astype(jnp.bfloat16)
    padded = with_halo(features, (("wide", 1), ("narrow", 2)), 1)
    first_hidden = jnp.maximum(convolve(padded, first_weight, depth_rows, height_rows), 0.0).astype(
        jnp.bfloat16
    )
    padded_hidden = with_halo(first_hidden, (("wide", 1), ("narrow", 2)), 1)
    second_hidden = jnp.maximum(
        convolve(padded_hidden, second_weight, depth_rows, height_rows), 0.0
    ).astype(jnp.bfloat16)
    channels, _, _, width_cells = second_hidden.shape
    pooled = second_hidden.reshape(
        channels, depth_rows // 2, 2, height_rows // 2, 2, width_cells // 2, 2
    ).max(axis=(2, 4, 6))
    whole_height = lax.all_gather(pooled, "narrow", axis=2, tiled=True)
    slab = with_halo(whole_height, (("wide", 1),), 1)
    slab = jnp.pad(slab, ((0, 0), (0, 0), (1, 1), (0, 0)))
    coarse = jnp.maximum(
        convolve(slab, third_weight, depth_rows // 2, whole_height.shape[2]), 0.0
    ).astype(jnp.bfloat16)
    return coarse.reshape(coarse.shape[0], coarse.shape[1], -1)


def solution(mesh):
    in_specs = (P(None, "wide", "narrow", None), P(), P(), P(), P(), P("narrow", None))
    out_specs = P("narrow", "wide", None)
    return jax.shard_map(body, mesh=mesh, in_specs=in_specs, out_specs=out_specs, check_vma=False)
```

profile of v0, /device:TPU:0, one launch (start us, length us, event | category | flops | bytes accessed | tf_op | source)
XLA Modules:
  0.0 100.6 jit_solution(10894273282007639314)
XLA Ops:
  0.0 1.1 %add_convert_fusion = bf16[64,2,4,128]{3,2,1,0:T(4,128)(2,1)S(1)} fusion(bf16[64,2,4,128]{3,2,1,0:T(4,128)(2,1)} %param.6, f32[64]{0:T(128)} %param.8, f32[64]{0:T(128)} %param.7), kind=kLoop, calls=%fused_computation.126 | loop fusion | flops 262144 | bytes 262656 | tf_op jit(solution)/shard_map/convert_element_type | solution.py:53
  1.2 4.9 %collective-permute-start = (bf16[64,1,4,128]{3,2,1,0:T(4,128)(2,1)S(1)}, bf16[64,1,4,128]{3,2,1,0:T(4,128)(2,1)S(1)}, u32[]{:S(2)}, u32[]{:S(2)}) collective-permute-start(bf16[64,1,4,128]{3,2,1,0:T(4,128)(2,1)S(1)} %get-tuple-element.89), channel_id=1, source_target_pairs={{0,4},{4,8},{8,12},{12,16},{16,20},{20,24},{24,28},{1,5},{5,9},{9,... | collective-permute-start | bytes 196616 | tf_op jit(solution)/shard_map/ppermute | solution.py:12
  6.1 1.3 %collective-permute-start.1 = (bf16[64,1,4,128]{3,2,1,0:T(4,128)(2,1)S(1)}, bf16[64,1,4,128]{3,2,1,0:T(4,128)(2,1)S(1)}, u32[]{:S(2)}, u32[]{:S(2)}) collective-permute-start(bf16[64,1,4,128]{3,2,1,0:T(4,128)(2,1)S(1)} %get-tuple-element.90), channel_id=1, source_target_pairs={{4,0},{8,4},{12,8},{16,12},{20,16},{24,20},{28,24},{5,1},{9,5},{13... | collective-permute-start | bytes 196616 | tf_op jit(solution)/shard_map/ppermute | solution.py:15
  7.4 0.6 collective-permute-done
  8.0 4.3 %collective-permute-done.1 = bf16[64,1,4,128]{3,2,1,0:T(4,128)(2,1)S(1)} collective-permute-done((bf16[64,1,4,128]{3,2,1,0:T(4,128)(2,1)S(1)}, bf16[64,1,4,128]{3,2,1,0:T(4,128)(2,1)S(1)}, u32[]{:S(2)}, u32[]{:S(2)}) %collective-permute-start.1) | collective-permute-done | bytes 65568 | tf_op jit(solution)/shard_map/ppermute | solution.py:15
  12.6 1.3 %collective-permute-start.3 = (bf16[64,4,1,128]{3,2,1,0:T(2,128)(2,1)S(1)}, bf16[64,4,1,128]{3,2,1,0:T(2,128)(2,1)S(1)}, u32[]{:S(2)}, u32[]{:S(2)}) collective-permute-start(bf16[64,4,1,128]{3,2,1,0:T(2,128)(2,1)S(1)} %get-tuple-element.79), channel_id=1, source_target_pairs={{1,0},{2,1},{3,2},{5,4},{6,5},{7,6},{9,8},{10,9},{11,10},{13,12},{... | collective-permute-start | bytes 196616 | tf_op jit(solution)/shard_map/ppermute | solution.py:15
  13.9 3.0 %collective-permute-start.2 = (bf16[64,4,1,128]{3,2,1,0:T(2,128)(2,1)S(1)}, bf16[64,4,1,128]{3,2,1,0:T(2,128)(2,1)S(1)}, u32[]{:S(2)}, u32[]{:S(2)}) collective-permute-start(bf16[64,4,1,128]{3,2,1,0:T(2,128)(2,1)S(1)} %get-tuple-element.80), channel_id=1, source_target_pairs={{0,1},{1,2},{2,3},{4,5},{5,6},{6,7},{8,9},{9,10},{10,11},{12,13},{... | collective-permute-start | bytes 196616 | tf_op jit(solution)/shard_map/ppermute | solution.py:12
  17.0 1.0 collective-permute-done.2
  17.9 1.8 %fusion.15 = bf16[64,4,6,130]{3,2,1,0:T(8,128)(2,1)S(1)} fusion(bf16[64,4,1,128]{3,2,1,0:T(2,128)(2,1)S(1)} %collective-permute-done.3, bf16[64,4,1,128]{3,2,1,0:T(2,128)(2,1)S(1)} %collective-permute-done.2, bf16[64,1,4,128]{3,2,1,0:T(4,128)(2,1)S(1)} %collective-permute-done.1, bf16[64,2,4,128]{3,2,1,0:T(4,128)(2,1)S(1)} %add_convert_fusion, ...), kind=kLoop, calls=%fused_computation.45 | loop fusion | flops 3594240 | bytes 792576 | tf_op jit(solution)/shard_map/concatenate | solution.py:16
  19.7 2.2 %fusion.87 = (bf16[64,2,4,128]{3,2,1,0:T(4,128)(2,1)S(1)}, bf16[64,2,4,128]{3,2,1,0:T(4,128)(2,1)S(1)}, bf16[64,2,4,128]{3,2,1,0:T(4,128)(2,1)}, bf16[64,2,4,128...) fusion(bf16[64,4,6,130]{3,2,1,0:T(8,128)(2,1)S(1)} %fusion.15), kind=kLoop, calls=%fused_computation.179 | loop fusion | bytes 4718592 | tf_op jit(solution)/shard_map/slice | solution.py:29
  22.0 1.6 %fusion.41 = (bf16[192,2,4,128]{3,2,1,0:T(4,128)(2,1)S(1)}, bf16[192,2,4,128]{3,2,1,0:T(4,128)(2,1)S(1)}, bf16[192,2,4,128]{3,2,1,0:T(4,128)(2,1)S(1)}) fusion(bf16[64,4,1,128]{3,2,1,0:T(2,128)(2,1)S(1)} %collective-permute-done.3, bf16[64,1,4,128]{3,2,1,0:T(4,128)(2,1)S(1)} %collective-permute-done.1, bf16[64,2,4,128]{3,2,1,0:T(4,128)(2,1)S(1)} %add_convert_fusion, ...), kind=kLoop, calls=%fused_computation.80 | loop fusion | flops 7077888 | bytes 2293760 | tf_op jit(solution)/shard_map/concatenate | solution.py:27
  23.6 0.3 reshape.124
  23.8 0.3 reshape.121
  24.1 0.3 reshape.118
  24.4 2.4 %fusion.45 = (bf16[192,2,4,128]{3,2,1,0:T(4,128)(2,1)S(1)}, bf16[192,2,4,128]{3,2,1,0:T(4,128)(2,1)S(1)}, bf16[192,2,4,128]{3,2,1,0:T(4,128)(2,1)S(1)}) fusion(bf16[64,4,1,128]{3,2,1,0:T(2,128)(2,1)S(1)} %collective-permute-done.2, bf16[64,1,4,128]{3,2,1,0:T(4,128)(2,1)S(1)} %collective-permute-done.1, bf16[64,2,4,128]{3,2,1,0:T(4,128)(2,1)S(1)} %add_convert_fusion, ...), kind=kLoop, calls=%fused_computation.88 | loop fusion | flops 7077888 | bytes 2293760 | tf_op jit(solution)/shard_map/concatenate | solution.py:27
  26.7 0.3 reshape.122
  27.0 2.9 %fusion.43 = (bf16[192,2,4,128]{3,2,1,0:T(4,128)(2,1)}, bf16[192,2,4,128]{3,2,1,0:T(4,128)(2,1)S(1)}, bf16[192,2,4,128]{3,2,1,0:T(4,128)(2,1)}) fusion(bf16[64,1,4,128]{3,2,1,0:T(4,128)(2,1)S(1)} %collective-permute-done.1, bf16[64,2,4,128]{3,2,1,0:T(4,128)(2,1)S(1)} %add_convert_fusion, bf16[64,2,4,128]{3,2,1,0:T(4,128)(2,1)S(1)} %get-tuple-element.24, ...), kind=kLoop, calls=%fused_computation.85 | loop fusion | flops 1572864 | bytes 2228224 | tf_op jit(solution)/shard_map/concatenate | solution.py:27
  29.9 1.3 %reshape.123 = bf16[192,1024]{1,0:T(8,128)(2,1)S(1)} reshape(bf16[192,2,4,128]{3,2,1,0:T(4,128)(2,1)} %get-tuple-element.86) | data formatting | bytes 786432 | tf_op jit(solution)/shard_map/reshape | solution.py:39
  31.2 1.0 %reshape.117 = bf16[192,1024]{1,0:T(8,128)(2,1)} reshape(bf16[192,2,4,128]{3,2,1,0:T(4,128)(2,1)S(1)} %get-tuple-element.87) | data formatting | bytes 786432 | tf_op jit(solution)/shard_map/reshape | solution.py:39
  32.2 1.3 %reshape.120 = bf16[192,1024]{1,0:T(8,128)(2,1)S(1)} reshape(bf16[192,2,4,128]{3,2,1,0:T(4,128)(2,1)} %get-tuple-element.88) | data formatting | bytes 786432 | tf_op jit(solution)/shard_map/reshape | solution.py:39
  33.5 1.0 %reshape.119 = bf16[192,1024]{1,0:T(8,128)(2,1)} reshape(bf16[192,2,4,128]{3,2,1,0:T(4,128)(2,1)S(1)} %get-tuple-element.75) | data formatting | bytes 786432 | tf_op jit(solution)/shard_map/reshape | solution.py:39
  34.5 1.0 %reshape.116 = bf16[192,1024]{1,0:T(8,128)(2,1)} reshape(bf16[192,2,4,128]{3,2,1,0:T(4,128)(2,1)S(1)} %get-tuple-element.76) | data formatting | bytes 786432 | tf_op jit(solution)/shard_map/reshape | solution.py:39
  35.5 1.2 %fusion.84 = f32[1024,64]{0,1:T(8,128)S(1)} fusion(bf16[192,1024]{1,0:T(8,128)(2,1)} %reshape.116, bf16[64,1728]{1,0:T(8,128)(2,1)S(1)} %copy-done.6), kind=kOutput, calls=%fused_computation.155 | convolution fusion | flops 25165824 | bytes 688128 | tf_op jit(solution)/shard_map/dot_general | solution.py:42
  37.2 0.5 copy-done
  38.9 1.0 fusion.5
  40.0 4.3 %collective-permute-start.4 = (bf16[64,1,4,128]{3,2,1,0:T(4,128)(2,1)S(1)}, bf16[64,1,4,128]{3,2,1,0:T(4,128)(2,1)S(1)}, u32[]{:S(2)}, u32[]{:S(2)}) collective-permute-start(bf16[64,1,4,128]{3,2,1,0:T(4,128)(2,1)S(1)} %get-tuple-element.85), channel_id=1, source_target_pairs={{0,4},{4,8},{8,12},{12,16},{16,20},{20,24},{24,28},{1,5},{5,9},{9,... | collective-permute-start | bytes 196616 | tf_op jit(solution)/shard_map/ppermute | solution.py:12
  44.3 1.3 %collective-permute-start.5 = (bf16[64,1,4,128]{3,2,1,0:T(4,128)(2,1)S(1)}, bf16[64,1,4,128]{3,2,1,0:T(4,128)(2,1)S(1)}, u32[]{:S(2)}, u32[]{:S(2)}) collective-permute-start(bf16[64,1,4,128]{3,2,1,0:T(4,128)(2,1)S(1)} %get-tuple-element.84), channel_id=1, source_target_pairs={{4,0},{8,4},{12,8},{16,12},{20,16},{24,20},{28,24},{5,1},{9,5},{13... | collective-permute-start | bytes 196616 | tf_op jit(solution)/shard_map/ppermute | solution.py:15
  45.6 0.6 collective-permute-done.4
  46.3 0.5 copy-done.7
  46.8 3.7 %collective-permute-done.5 = bf16[64,1,4,128]{3,2,1,0:T(4,128)(2,1)S(1)} collective-permute-done((bf16[64,1,4,128]{3,2,1,0:T(4,128)(2,1)S(1)}, bf16[64,1,4,128]{3,2,1,0:T(4,128)(2,1)S(1)}, u32[]{:S(2)}, u32[]{:S(2)}) %collective-permute-start.5) | collective-permute-done | bytes 65568 | tf_op jit(solution)/shard_map/ppermute | solution.py:15
  50.5 0.6 copy-done.8
  51.3 1.3 %collective-permute-start.7 = (bf16[64,4,1,128]{3,2,1,0:T(2,128)(2,1)S(1)}, bf16[64,4,1,128]{3,2,1,0:T(2,128)(2,1)S(1)}, u32[]{:S(2)}, u32[]{:S(2)}) collective-permute-start(bf16[64,4,1,128]{3,2,1,0:T(2,128)(2,1)S(1)} %get-tuple-element.77), channel_id=1, source_target_pairs={{1,0},{2,1},{3,2},{5,4},{6,5},{7,6},{9,8},{10,9},{11,10},{13,12},{... | collective-permute-start | bytes 196616 | tf_op jit(solution)/shard_map/ppermute | solution.py:15
  52.6 3.4 %collective-permute-start.6 = (bf16[64,4,1,128]{3,2,1,0:T(2,128)(2,1)S(1)}, bf16[64,4,1,128]{3,2,1,0:T(2,128)(2,1)S(1)}, u32[]{:S(2)}, u32[]{:S(2)}) collective-permute-start(bf16[64,4,1,128]{3,2,1,0:T(2,128)(2,1)S(1)} %get-tuple-element.78), channel_id=1, source_target_pairs={{0,1},{1,2},{2,3},{4,5},{5,6},{6,7},{8,9},{9,10},{10,11},{12,13},{... | collective-permute-start | bytes 196616 | tf_op jit(solution)/shard_map/ppermute | solution.py:12
  56.0 0.8 collective-permute-done.6
  56.8 1.3 %select_maximum_fusion = bf16[64,4,6,130]{3,2,1,0:T(8,128)(2,1)S(1)} fusion(bf16[64,4,1,128]{3,2,1,0:T(2,128)(2,1)S(1)} %collective-permute-done.7, bf16[64,4,4,128]{3,2,1,0:T(4,128)(2,1)S(1)} %constant_dynamic-update-slice_fusion, bf16[64,4,1,128]{3,2,1,0:T(2,128)(2,1)S(1)} %collective-permute-done.6), kind=kLoop, calls=%fused_computation.37 | loop fusion | flops 2396160 | bytes 792576 | tf_op jit(solution)/shard_map/concatenate | solution.py:16
  58.1 2.2 %fusion.86 = (bf16[64,2,4,128]{3,2,1,0:T(4,128)(2,1)S(1)}, bf16[64,2,4,128]{3,2,1,0:T(4,128)(2,1)}, bf16[64,2,4,128]{3,2,1,0:T(4,128)(2,1)}, bf16[64,2,4,128]{3,...) fusion(bf16[64,4,6,130]{3,2,1,0:T(8,128)(2,1)S(1)} %select_maxi, ...), kind=kLoop, calls=%fused_computation.178 | loop fusion | bytes 4718592 | tf_op jit(solution)/shard_map/slice | solution.py:29
  60.3 0.8 fusion.25
  61.2 0.3 reshape.133
  61.4 1.7 %fusion.29 = (bf16[192,2,4,128]{3,2,1,0:T(4,128)(2,1)S(1)}, bf16[192,2,4,128]{3,2,1,0:T(4,128)(2,1)S(1)}, bf16[192,2,4,128]{3,2,1,0:T(4,128)(2,1)S(1)}) fusion(bf16[64,4,4,128]{3,2,1,0:T(4,128)(2,1)S(1)} %constant_dynamic-update-slice_fusion, bf16[64,4,1,128]{3,2,1,0:T(2,128)(2,1)S(1)} %collective-permute-done.6, ...), kind=kLoop, calls=%fused_computation.62 | loop fusion | flops 4718592 | bytes 2293760 | tf_op jit(solution)/shard_map/concatenate | solution.py:27
  63.1 0.3 reshape.131
  63.4 0.3 reshape.125
  63.7 0.3 reshape.128
  64.2 0.3 reshape.127
  64.6 2.7 %fusion.27 = (bf16[192,2,4,128]{3,2,1,0:T(4,128)(2,1)S(1)}, bf16[192,2,4,128]{3,2,1,0:T(4,128)(2,1)S(1)}, bf16[192,2,4,128]{3,2,1,0:T(4,128)(2,1)}) fusion(bf16[64,1,4,128]{3,2,1,0:T(4,128)(2,1)} %copy-done.8, bf16[64,2,4,128]{3,2,1,0:T(4,128)(2,1)S(1)} %convert_element_type.44, bf16[64,2,4,128]{3,2,1,0:T(4,128)(2,1)S(1)} %copy-done.2, ...), kind=kLoop, calls=%fused_computation.59 | loop fusion | flops 1572864 | bytes 2228224 | tf_op jit(solution)/shard_map/concatenate | solution.py:27
  67.9 1.3 %reshape.126 = bf16[192,1024]{1,0:T(8,128)(2,1)S(1)} reshape(bf16[192,2,4,128]{3,2,1,0:T(4,128)(2,1)} %get-tuple-element.83) | data formatting | bytes 786432 | tf_op jit(solution)/shard_map/reshape | solution.py:39
  69.2 1.2 %fusion.74 = f32[1024,128]{1,0:T(8,128)S(1)} fusion(bf16[192,1024]{1,0:T(8,128)(2,1)S(1)} %reshape.125, bf16[128,1728]{0,1:T(8,128)(2,1)} %param.10), kind=kOutput, calls=%fused_computation.145 | convolution fusion | flops 50331648 | bytes 966656 | tf_op jit(solution)/shard_map/dot_general | solution.py:42
  70.4 1.2 %convolution_add_fusion.7 = f32[1024,128]{1,0:T(8,128)S(1)} fusion(f32[1024,128]{1,0:T(8,128)S(1)} %fusion.74, bf16[192,1024]{1,0:T(8,128)(2,1)S(1)} %reshape.126, bf16[128,1728]{0,1:T(8,128)(2,1)} %param.10), kind=kOutput, calls=%fused_computation.13 | convolution fusion | flops 50462720 | bytes 1490944 | tf_op jit(solution)/shard_map/dot_general | solution.py:42
  71.5 0.4 convolution_add_fusion.6
  71.9 0.4 convolution_add_fusion.5
  72.3 0.4 convolution_add_fusion.4
  72.6 0.4 convolution_add_fusion.3
  73.0 0.4 convolution_add_fusion.2
  73.3 0.4 convolution_add_fusion.1
  73.7 0.4 fusion.2
  74.1 0.4 reduce_max.11
  74.4 10.7 %all-gather = bf16[128,8,64]{0,2,1:T(8,128)(2,1)S(1)} all-gather(bf16[128,2,64]{0,2,1:T(8,128)(2,1)S(1)} %reduce_max.11), channel_id=2, replica_groups=mesh['wide'=8,'narrow'=4] {'narrow'}, dimensions={1}, use_global_device_ids=true | all-gather | bytes 163840 | tf_op jit(solution)/shard_map/all_gather | solution.py:66
  85.2 1.3 %collective-permute-start.9 = (bf16[128,1,8,64]{0,3,2,1:T(8,128)(2,1)S(1)}, bf16[128,1,8,64]{0,3,2,1:T(8,128)(2,1)S(1)}, u32[]{:S(2)}, u32[]{:S(2)}) collective-permute-start(bf16[128,1,8,64]{0,3,2,1:T(8,128)(2,1)S(1)} %bitcast.55), channel_id=1, source_target_pairs={{4,0},{8,4},{12,8},{16,12},{20,16},{24,20},{28,24},{5,1},{9,5},{13... | collective-permute-start | bytes 393224 | tf_op jit(solution)/shard_map/ppermute | solution.py:15
  86.4 4.6 %collective-permute-start.8 = (bf16[128,1,8,64]{0,3,2,1:T(8,128)(2,1)S(1)}, bf16[128,1,8,64]{0,3,2,1:T(8,128)(2,1)S(1)}, u32[]{:S(2)}, u32[]{:S(2)}) collective-permute-start(bf16[128,1,8,64]{0,3,2,1:T(8,128)(2,1)S(1)} %bitcast.56), channel_id=1, source_target_pairs={{0,4},{4,8},{8,12},{12,16},{16,20},{20,24},{24,28},{1,5},{5,9},{9,... | collective-permute-start | bytes 393224 | tf_op jit(solution)/shard_map/ppermute | solution.py:12
  91.0 1.8 %collective-permute-done.9 = bf16[128,1,8,64]{0,3,2,1:T(8,128)(2,1)S(1)} collective-permute-done((bf16[128,1,8,64]{0,3,2,1:T(8,128)(2,1)S(1)}, bf16[128,1,8,64]{0,3,2,1:T(8,128)(2,1)S(1)}, u32[]{:S(2)}, u32[]{:S(2)}) %collective-permute-start.9) | collective-permute-done | bytes 131104 | tf_op jit(solution)/shard_map/ppermute | solution.py:15
  92.8 2.7 %collective-permute-done.8 = bf16[128,1,8,64]{0,3,2,1:T(8,128)(2,1)S(1)} collective-permute-done((bf16[128,1,8,64]{0,3,2,1:T(8,128)(2,1)S(1)}, bf16[128,1,8,64]{0,3,2,1:T(8,128)(2,1)S(1)}, u32[]{:S(2)}, u32[]{:S(2)}) %collective-permute-start.8) | collective-permute-done | bytes 131104 | tf_op jit(solution)/shard_map/ppermute | solution.py:12
  95.7 0.3 pad_slice_fusion.1
  96.0 0.3 fusion.88
  96.5 0.9 copy-done.5
  99.7 0.9 fusion.8
  (50 shorter events, 5.9 us)
Async XLA Ops:
  1.2 6.8 %collective-permute-start = (bf16[64,1,4,128]{3,2,1,0:T(4,128)(2,1)S(1)}, bf16[64,1,4,128]{3,2,1,0:T(4,128)(2,1)S(1)}, u32[]{:S(2)}, u32[]{:S(2)}) collective-permute-start(bf16[64,1,4,128]{3,2,1,0:T(4,128)(2,1)S(1)} %get-tuple-element.89), channel_id=1, source_target_pairs={{0,4},{4,8},{8,12},{12,16},{16,20},{20,24},{24,28},{1,5},{5,9},{9,... | collective-permute-start | bytes 196616 | tf_op jit(solution)/shard_map/ppermute | solution.py:12
  6.1 6.2 %collective-permute-start.1 = (bf16[64,1,4,128]{3,2,1,0:T(4,128)(2,1)S(1)}, bf16[64,1,4,128]{3,2,1,0:T(4,128)(2,1)S(1)}, u32[]{:S(2)}, u32[]{:S(2)}) collective-permute-start(bf16[64,1,4,128]{3,2,1,0:T(4,128)(2,1)S(1)} %get-tuple-element.90), channel_id=1, source_target_pairs={{4,0},{8,4},{12,8},{16,12},{20,16},{24,20},{28,24},{5,1},{9,5},{13... | collective-permute-start | bytes 196616 | tf_op jit(solution)/shard_map/ppermute | solution.py:15
  12.6 4.3 %collective-permute-start.3 = (bf16[64,4,1,128]{3,2,1,0:T(2,128)(2,1)S(1)}, bf16[64,4,1,128]{3,2,1,0:T(2,128)(2,1)S(1)}, u32[]{:S(2)}, u32[]{:S(2)}) collective-permute-start(bf16[64,4,1,128]{3,2,1,0:T(2,128)(2,1)S(1)} %get-tuple-element.79), channel_id=1, source_target_pairs={{1,0},{2,1},{3,2},{5,4},{6,5},{7,6},{9,8},{10,9},{11,10},{13,12},{... | collective-permute-start | bytes 196616 | tf_op jit(solution)/shard_map/ppermute | solution.py:15
  13.9 4.0 %collective-permute-start.2 = (bf16[64,4,1,128]{3,2,1,0:T(2,128)(2,1)S(1)}, bf16[64,4,1,128]{3,2,1,0:T(2,128)(2,1)S(1)}, u32[]{:S(2)}, u32[]{:S(2)}) collective-permute-start(bf16[64,4,1,128]{3,2,1,0:T(2,128)(2,1)S(1)} %get-tuple-element.80), channel_id=1, source_target_pairs={{0,1},{1,2},{2,3},{4,5},{5,6},{6,7},{8,9},{9,10},{10,11},{12,13},{... | collective-permute-start | bytes 196616 | tf_op jit(solution)/shard_map/ppermute | solution.py:12
  32.2 3.4 %copy-start.6 = (bf16[64,1728]{1,0:T(8,128)(2,1)S(1)}, bf16[64,1728]{1,0:T(8,128)(2,1)}, u32[]{:S(2)}) copy-start(bf16[64,1728]{1,0:T(8,128)(2,1)} %param.9) | copy-start | bytes 663556
  34.5 2.2 %copy-start.1 = (bf16[192,1024]{1,0:T(8,128)(2,1)S(1)}, bf16[192,1024]{1,0:T(8,128)(2,1)}, u32[]{:S(2)}) copy-start(bf16[192,1024]{1,0:T(8,128)(2,1)} %reshape.117) | copy-start | bytes 1179652
  36.7 1.0 copy-start
  40.0 6.2 %collective-permute-start.4 = (bf16[64,1,4,128]{3,2,1,0:T(4,128)(2,1)S(1)}, bf16[64,1,4,128]{3,2,1,0:T(4,128)(2,1)S(1)}, u32[]{:S(2)}, u32[]{:S(2)}) collective-permute-start(bf16[64,1,4,128]{3,2,1,0:T(4,128)(2,1)S(1)} %get-tuple-element.85), channel_id=1, source_target_pairs={{0,4},{4,8},{8,12},{12,16},{16,20},{20,24},{24,28},{1,5},{5,9},{9,... | collective-permute-start | bytes 196616 | tf_op jit(solution)/shard_map/ppermute | solution.py:12
  44.3 6.2 %collective-permute-start.5 = (bf16[64,1,4,128]{3,2,1,0:T(4,128)(2,1)S(1)}, bf16[64,1,4,128]{3,2,1,0:T(4,128)(2,1)S(1)}, u32[]{:S(2)}, u32[]{:S(2)}) collective-permute-start(bf16[64,1,4,128]{3,2,1,0:T(4,128)(2,1)S(1)} %get-tuple-element.84), channel_id=1, source_target_pairs={{4,0},{8,4},{12,8},{16,12},{20,16},{24,20},{28,24},{5,1},{9,5},{13... | collective-permute-start | bytes 196616 | tf_op jit(solution)/shard_map/ppermute | solution.py:15
  46.2 0.6 copy-start.7
  50.5 0.6 copy-start.8
  51.3 4.7 %collective-permute-start.7 = (bf16[64,4,1,128]{3,2,1,0:T(2,128)(2,1)S(1)}, bf16[64,4,1,128]{3,2,1,0:T(2,128)(2,1)S(1)}, u32[]{:S(2)}, u32[]{:S(2)}) collective-permute-start(bf16[64,4,1,128]{3,2,1,0:T(2,128)(2,1)S(1)} %get-tuple-element.77), channel_id=1, source_target_pairs={{1,0},{2,1},{3,2},{5,4},{6,5},{7,6},{9,8},{10,9},{11,10},{13,12},{... | collective-permute-start | bytes 196616 | tf_op jit(solution)/shard_map/ppermute | solution.py:15
  52.6 4.1 %collective-permute-start.6 = (bf16[64,4,1,128]{3,2,1,0:T(2,128)(2,1)S(1)}, bf16[64,4,1,128]{3,2,1,0:T(2,128)(2,1)S(1)}, u32[]{:S(2)}, u32[]{:S(2)}) collective-permute-start(bf16[64,4,1,128]{3,2,1,0:T(2,128)(2,1)S(1)} %get-tuple-element.78), channel_id=1, source_target_pairs={{0,1},{1,2},{2,3},{4,5},{5,6},{6,7},{8,9},{9,10},{10,11},{12,13},{... | collective-permute-start | bytes 196616 | tf_op jit(solution)/shard_map/ppermute | solution.py:12
  63.6 0.9 copy-start.2
  63.7 1.0 copy-start.3
  69.1 2.4 %copy-start.4 = (bf16[128,1728]{0,1:T(8,128)(2,1)S(1)}, bf16[128,1728]{0,1:T(8,128)(2,1)}, u32[]{:S(2)}) copy-start(bf16[128,1728]{0,1:T(8,128)(2,1)} %param.10) | copy-start | bytes 1327108
  85.2 7.6 %collective-permute-start.9 = (bf16[128,1,8,64]{0,3,2,1:T(8,128)(2,1)S(1)}, bf16[128,1,8,64]{0,3,2,1:T(8,128)(2,1)S(1)}, u32[]{:S(2)}, u32[]{:S(2)}) collective-permute-start(bf16[128,1,8,64]{0,3,2,1:T(8,128)(2,1)S(1)} %bitcast.55), channel_id=1, source_target_pairs={{4,0},{8,4},{12,8},{16,12},{20,16},{24,20},{28,24},{5,1},{9,5},{13... | collective-permute-start | bytes 393224 | tf_op jit(solution)/shard_map/ppermute | solution.py:15
  86.4 9.1 %collective-permute-start.8 = (bf16[128,1,8,64]{0,3,2,1:T(8,128)(2,1)S(1)}, bf16[128,1,8,64]{0,3,2,1:T(8,128)(2,1)S(1)}, u32[]{:S(2)}, u32[]{:S(2)}) collective-permute-start(bf16[128,1,8,64]{0,3,2,1:T(8,128)(2,1)S(1)} %bitcast.56), channel_id=1, source_target_pairs={{0,4},{4,8},{8,12},{12,16},{16,20},{20,24},{24,28},{1,5},{5,9},{9,... | collective-permute-start | bytes 393224 | tf_op jit(solution)/shard_map/ppermute | solution.py:12
  96.3 1.0 %copy-start.5 = (bf16[64,3456]{1,0:T(8,128)(2,1)S(1)}, bf16[64,3456]{1,0:T(8,128)(2,1)}, u32[]{:S(2)}) copy-start(bf16[64,3456]{1,0:T(8,128)(2,1)} %param.11) | copy-start | bytes 1327108
where the time goes:
time: 102 us; the launch traced here: 101 us
  starting transfers between devices  26.6 us (26%)
  local copies, waits for them, and re-layouts  18.7 us (18%)
  other arithmetic  17.4 us (17%)
  waiting for transfers between devices  15.3 us (15%)
  matrix products  11.3 us (11%)
  blocking collectives  10.7 us (10%)
    ppermute x5, starting transfers between devices, with_halo(): lax.ppermute(lax.slice_in_dim(block, block.shape[dim] - width, None, axis...  20.2 us
    concatenate x11, other arithmetic, convolve(): jnp.concatenate([padded_width[:, depth_off:depth_off + depth_rows, height...  12.5 us
    dot_general x27, matrix products, convolve(): product = jnp.dot(weight_block, stacked, preferred_element_type=jnp.float32)  11.3 us
    all_gather x1, blocking collectives, body(): whole_height = lax.all_gather(pooled, 'narrow', axis=2, tiled=True)  10.7 us
    reshape x18, local copies, waits for them, and re-layouts, convolve(): stacked = stacked.reshape(3 * channels, -1)  10.1 us
    ppermute x5, waiting for transfers between devices, with_halo(): lax.ppermute(lax.slice_in_dim(block, 0, width, axis=dim), axis, backward)  9.71 us
    ppermute x5, starting transfers between devices, with_halo(): lax.ppermute(lax.slice_in_dim(block, 0, width, axis=dim), axis, backward)  6.45 us
    ppermute x5, waiting for transfers between devices, with_halo(): lax.ppermute(lax.slice_in_dim(block, block.shape[dim] - width, None, axis...  5.63 us
  transfers between devices with their start and end apart: 10, of which 8 were waited for; matrix products, arithmetic and copies ran while one was open for 0% of the time, Pallas kernels for 0%

commit v1 on v0

v1 whole, which is shorter than its diff:
```python
import functools

import jax
import jax.numpy as jnp
from jax import lax
from jax.experimental import pallas as pl
from jax.experimental.pallas import tpu as pltpu
from jax.sharding import PartitionSpec as P

LANES = 128
VMEM = pl.BlockSpec(memory_space=pltpu.VMEM)


def pair_swap(count, bit=1):
    return [(k, k ^ bit) for k in range(count)]


def pair_relay(count):
    steps = []
    for k in range(count):
        target = k - 2 if k % 2 == 0 else k + 2
        steps.append((k, target if 0 <= target < count else k ^ 1))
    return steps


def pair_relay_back(count):
    return [(target, source) for source, target in pair_relay(count)]


def weights_kernel(w1_ref, w2_ref, w3_ref, t1_ref, t2_ref, t3_ref):
    o1 = w1_ref.shape[0]
    c1 = w1_ref.shape[1] // 27
    o2 = w2_ref.shape[0]
    c2 = w2_ref.shape[1] // 27
    o3 = w3_ref.shape[0]
    c3 = w3_ref.shape[1] // 27
    for ref, out, o, c, rows in ((w1_ref, t1_ref, o1, c1, 4), (w2_ref, t2_ref, o2, c2, 2)):
        span = (rows + 2) * c
        for be in range(9):
            taps = [ref[:, (a * 9 + be) * c : (a * 9 + be + 1) * c] for a in range(3)]
            for row in range(rows):
                parts = []
                if row:
                    parts.append(jnp.zeros((o, row * c), jnp.bfloat16))
                parts += taps
                if row < rows - 1:
                    parts.append(jnp.zeros((o, (rows - 1 - row) * c), jnp.bfloat16))
                out[row * o : (row + 1) * o, be * span : (be + 1) * span] = jnp.concatenate(
                    parts, axis=1
                )
    for be in range(9):
        for a in range(3):
            t3_ref[be * o3 : (be + 1) * o3, a * c3 : (a + 1) * c3] = w3_ref[
                :, (a * 9 + be) * c3 : (a * 9 + be + 1) * c3
            ]


def shifted(value):
    lane = lax.broadcasted_iota(jnp.int32, value.shape, 1)
    low = jnp.where(lane == 0, 0.0, pltpu.roll(value, 1, 1))
    high = jnp.where(lane == LANES - 1, 0.0, pltpu.roll(value, LANES - 1, 1))
    return low, value, high


def fine_kernel(
    wide, narrow, channels, own_ref, pair_ref, far_ref, side_ref, scale_ref, shift_ref, w1_ref,
    w2_ref, out_ref, raw, taps, hidden,
):
    c = channels
    i, j = lax.axis_index("wide"), lax.axis_index("narrow")
    i_odd, j_odd = lax.rem(i, 2), lax.rem(j, 2)
    pair_slot, far_slot = 2 - 2 * i_odd, 2 * i_odd
    depth, height = 2, 4
    block = c * depth * height
    raw[0:block, :] = own_ref[...].astype(jnp.float32)
    raw[block : 2 * block, :] = pair_ref[...].astype(jnp.float32)
    raw[2 * block : 3 * block, :] = far_ref[...].astype(jnp.float32)
    raw[3 * block :, :] = side_ref[...].astype(jnp.float32)
    scale, shift = scale_ref[...], shift_ref[...]
    slab = 6 * c

    def put(value, slot, d, lane):
        row = pl.multiple_of(slot * (depth * c) + d * c, c)
        for e, part in enumerate(shifted(value)):
            taps[pl.ds(pl.multiple_of(e * slab + row, c), c), pl.ds(lane, LANES)] = part.astype(
                jnp.bfloat16
            )

    slots = (1, pair_slot, far_slot)
    for k in range(3):
        for d in range(depth):
            for h in range(height):
                rows = raw[pl.ds(k * block + d * height + h, c, stride=depth * height), :]
                put(rows * scale + shift, slots[k], d, (2 + h) * LANES)
    for part in range(2):
        side = (1 - j_odd) if part == 0 else j_odd
        for k in range(3):
            for d in range(depth):
                for h in range(2):
                    start = 3 * block + ((part * 3 + k) * c * depth * 2) + d * 2 + h
                    rows = raw[pl.ds(start, c, stride=depth * 2), :]
                    lane = pl.multiple_of((side * 6 + h) * LANES, LANES)
                    put(rows * scale + shift, slots[k], d, lane)

    zero = functools.partial(jnp.zeros, dtype=jnp.bfloat16)

    @pl.when(i == 0)
    def _():
        for e in range(3):
            taps[e * slab : e * slab + 2 * c, :] = zero((2 * c, 8 * LANES))

    @pl.when(i == wide - 1)
    def _():
        for e in range(3):
            taps[e * slab + 4 * c : (e + 1) * slab, :] = zero((2 * c, 8 * LANES))

    @pl.when(j == 0)
    def _():
        taps[:, 0 : 2 * LANES] = zero((3 * slab, 2 * LANES))

    @pl.when(j == narrow - 1)
    def _():
        taps[:, 6 * LANES :] = zero((3 * slab, 2 * LANES))

    h_slab = 4 * c
    w1 = w1_ref[...]
    for n in range(3):
        columns = jnp.concatenate(
            [taps[:, (2 * n + b) * LANES : (2 * n + b + 2) * LANES] for b in range(3)], axis=0
        )
        result = jnp.maximum(jnp.dot(w1, columns, preferred_element_type=jnp.float32), 0.0)
        for k in range(2):
            lane = (2 * n + k) * LANES
            for e, part in enumerate(shifted(result[:, k * LANES : (k + 1) * LANES])):
                hidden[e * h_slab : (e + 1) * h_slab, lane : lane + LANES] = part.astype(
                    jnp.bfloat16
                )

    @pl.when(i == 0)
    def _():
        for e in range(3):
            hidden[e * h_slab : e * h_slab + c, :] = zero((c, 6 * LANES))

    @pl.when(i == wide - 1)
    def _():
        for e in range(3):
            hidden[e * h_slab + 3 * c : (e + 1) * h_slab, :] = zero((c, 6 * LANES))

    @pl.when(j == 0)
    def _():
        hidden[:, 0:LANES] = zero((3 * h_slab, LANES))

    @pl.when(j == narrow - 1)
    def _():
        hidden[:, 5 * LANES :] = zero((3 * h_slab, LANES))

    w2 = w2_ref[...]
    c2 = out_ref.shape[0]
    cell = lax.broadcasted_iota(jnp.int32, (LANES, LANES), 0)
    target = lax.broadcasted_iota(jnp.int32, (LANES, LANES), 1)
    pooled = None
    for n in range(2):
        columns = jnp.concatenate(
            [hidden[:, (2 * n + b) * LANES : (2 * n + b + 2) * LANES] for b in range(3)], axis=0
        )
        result = jnp.dot(w2, columns, preferred_element_type=jnp.float32)
        best = jnp.maximum(result[0:c2], result[c2:])
        best = jnp.maximum(jnp.maximum(best[:, 0:LANES], best[:, LANES:]), 0.0)
        best = jnp.maximum(best, pltpu.roll(best, LANES - 1, 1)).astype(jnp.bfloat16)
        pick = (cell == 2 * target - n * LANES).astype(jnp.bfloat16)
        moved = jnp.dot(best, pick, preferred_element_type=jnp.float32)
        pooled = moved if pooled is None else pooled + moved
    out_ref[...] = pooled.astype(jnp.bfloat16)


def coarse_kernel(wide, narrow, mine_ref, theirs_ref, w3_ref, out_ref, slab):
    i, j = lax.axis_index("wide"), lax.axis_index("narrow")
    i_odd = lax.rem(i, 2)
    groups, _, c, lanes = mine_ref.shape
    slots = (1, 2 - 2 * i_odd, 2 * i_odd)
    for r in range(groups):
        for bit, ref in ((0, mine_ref), (1, theirs_ref)):
            lane = pl.multiple_of(jnp.bitwise_xor(j, 2 * r + bit) * lanes, lanes)
            for k in range(3):
                row = pl.multiple_of(slots[k] * c, c)
                slab[pl.ds(row, c), pl.ds(lane, lanes)] = ref[r, k]
    total = slab.shape[1]

    @pl.when(i == 0)
    def _():
        slab[0:c, :] = jnp.zeros((c, total), jnp.bfloat16)

    @pl.when(i == wide - 1)
    def _():
        slab[2 * c :, :] = jnp.zeros((c, total), jnp.bfloat16)

    o = out_ref.shape[0]
    width = lanes // 2
    z = jnp.dot(w3_ref[...], slab[...], preferred_element_type=jnp.float32)
    place = lax.broadcasted_iota(jnp.int32, (o, total), 1)
    column = lax.rem(place, width)
    result = None
    for e in range(3):
        low, mid, high = (z[(b * 3 + e) * o : (b * 3 + e + 1) * o] for b in range(3))
        low = jnp.where(place < width, 0.0, pltpu.roll(low, width, 1))
        high = jnp.where(place >= total - width, 0.0, pltpu.roll(high, total - width, 1))
        term = low + mid + high
        if e == 0:
            term = jnp.where(column == 0, 0.0, pltpu.roll(term, 1, 1))
        if e == 2:
            term = jnp.where(column == width - 1, 0.0, pltpu.roll(term, total - 1, 1))
        result = term if result is None else result + term
    out_ref[...] = jnp.maximum(result, 0.0).astype(jnp.bfloat16)


def body(
    wide, narrow, stored_features, channel_scale, channel_shift, first_weight, second_weight,
    third_weight,
):
    c1, depth, height, width = stored_features.shape
    c2 = second_weight.shape[0]
    o3 = third_weight.shape[0]
    params = pltpu.CompilerParams(vmem_limit_bytes=24 * 1024 * 1024)
    j_odd = lax.axis_index("narrow") % 2 == 1

    pair = lax.ppermute(stored_features, "wide", pair_swap(wide))
    t1, t2, t3 = pl.pallas_call(
        weights_kernel,
        out_shape=(
            jax.ShapeDtypeStruct((4 * c1, 9 * 6 * c1), jnp.bfloat16),
            jax.ShapeDtypeStruct((2 * c2, 9 * 4 * c1), jnp.bfloat16),
            jax.ShapeDtypeStruct((9 * o3, 3 * c2), jnp.bfloat16),
        ),
        in_specs=[VMEM] * 3,
        out_specs=(VMEM,) * 3,
        compiler_params=params,
        cost_estimate=pl.CostEstimate(flops=10**6, bytes_accessed=4 * 10**6, transcendentals=0),
    )(first_weight, second_weight, third_weight)
    far = lax.ppermute(pair, "wide", pair_relay_back(wide))
    half = height // 2
    blocks = jnp.stack([stored_features, pair, far])
    first_rows, last_rows = blocks[:, :, :, :half], blocks[:, :, :, half:]
    relayed = lax.ppermute(
        jnp.where(j_odd, last_rows, first_rows), "narrow", pair_relay(narrow)
    )
    side = lax.ppermute(
        jnp.stack([jnp.where(j_odd, first_rows, last_rows), relayed]), "narrow", pair_swap(narrow)
    )
    rows = c1 * depth * height
    pooled = pl.pallas_call(
        functools.partial(fine_kernel, wide, narrow, c1),
        out_shape=jax.ShapeDtypeStruct((c2, LANES), jnp.bfloat16),
        in_specs=[VMEM] * 8,
        out_specs=VMEM,
        scratch_shapes=[
            pltpu.VMEM((6 * rows, width), jnp.float32),
            pltpu.VMEM((18 * c1, 8 * width), jnp.bfloat16),
            pltpu.VMEM((12 * c1, 6 * width), jnp.bfloat16),
        ],
        compiler_params=params,
        cost_estimate=pl.CostEstimate(
            flops=2 * 10**9, bytes_accessed=4 * 10**6, transcendentals=0
        ),
    )(
        stored_features.reshape(rows, width),
        pair.reshape(rows, width),
        far.reshape(rows, width),
        side.reshape(3 * rows, width),
        channel_scale.reshape(c1, 1),
        channel_shift.reshape(c1, 1),
        t1,
        t2,
    )
    pooled_pair = lax.ppermute(pooled, "wide", pair_swap(wide))
    pooled_far = lax.ppermute(pooled_pair, "wide", pair_relay_back(wide))
    mine = jnp.stack([pooled, pooled_pair, pooled_far])[None]
    bit = narrow // 2
    while bit > 1:
        other = lax.ppermute(mine, "narrow", pair_swap(narrow, bit))
        mine = jnp.stack([mine, other], axis=1).reshape((-1,) + mine.shape[1:])
        bit //= 2
    theirs = lax.ppermute(mine, "narrow", pair_swap(narrow))
    total = narrow * LANES
    coarse = pl.pallas_call(
        functools.partial(coarse_kernel, wide, narrow),
        out_shape=jax.ShapeDtypeStruct((o3, total), jnp.bfloat16),
        in_specs=[VMEM] * 3,
        out_specs=VMEM,
        scratch_shapes=[pltpu.VMEM((3 * c2, total), jnp.bfloat16)],
        compiler_params=params,
        cost_estimate=pl.CostEstimate(flops=10**9, bytes_accessed=10**6, transcendentals=0),
    )(mine, theirs, t3)
    return coarse[:, None, :]


def solution(mesh):
    in_specs = (P(None, "wide", "narrow", None), P(), P(), P(), P(), P("narrow", None))
    out_specs = P("narrow", "wide", None)
    return jax.shard_map(
        functools.partial(body, mesh.shape["wide"], mesh.shape["narrow"]),
        mesh=mesh,
        in_specs=in_specs,
        out_specs=out_specs,
        check_vma=False,
    )
```

time: 102 us -> 42 us (0.41); the launches traced: 101 us -> 41.8 us
  local copies, waits for them, and re-layouts: 18.7 us -> 0.43 us
  starting transfers between devices: 26.6 us -> 8.55 us
  other arithmetic: 17.4 us -> 2.28 us
  matrix products: 11.3 us -> 0 us
  blocking collectives: 10.7 us -> 0 us
  waiting for transfers between devices: 15.3 us -> 23.8 us
  Pallas kernels: 0 us -> 6.67 us
    ppermute x10 -> x8, starting transfers between devices: 26.6 us -> 8.55 us  [the longest x1 3.05 us: body(): pair = lax.ppermute(stored_features, 'wide', pair_swap(wide))]
    concatenate x15 -> x0, other arithmetic: 15.9 us -> none  [the longest x11 12.5 us: convolve(): jnp.concatenate([padded_width[:, depth_off:depth_off + depth_rows, height...]
    dot_general x27 -> x0, matrix products: 11.3 us -> none  [convolve(): product = jnp.dot(weight_block, stacked, preferred_element_type=jnp.float32)]
    all_gather x1 -> x0, blocking collectives: 10.7 us -> none  [body(): whole_height = lax.all_gather(pooled, 'narrow', axis=2, tiled=True)]
    reshape x18 -> x2, local copies, waits for them, and re-layouts: 10.1 us -> 0.19 us  [the longest x1 0.1 us: body(): channel_scale.reshape(c1, 1)]
    ppermute x10 -> x8, waiting for transfers between devices: 15.3 us -> 23.8 us  [the longest x1 5.66 us: body(): lax.ppermute(jnp.where(j_odd, last_rows, first_rows), 'narrow', pair_rela...]
    pallas_call x0 -> x3, Pallas kernels: none -> 6.67 us  [the longest x1 4.84 us: body(): pl.pallas_call(functools.partial(fine_kernel, wide, narrow, c1), out_shap...]
    slice x9 -> x0, local copies, waits for them, and re-layouts: 5.61 us -> none  [the longest x5 5.14 us: convolve(): padded_width[:, depth_off:depth_off + depth_rows, height_off:height_off +...]
  transfers between devices with their start and end apart: 10 -> 8, of which waited for: 8 -> 8; matrix products, arithmetic and copies ran while one was open for 0% -> 1% of each run, Pallas kernels for 0% -> 1%
where the time goes in v1:
time: 42 us; the launch traced here: 41.8 us
  waiting for transfers between devices  23.8 us (57%)
  starting transfers between devices  8.55 us (20%)
  Pallas kernels  6.67 us (16%)
  other arithmetic  2.28 us (5%)
  local copies, waits for them, and re-layouts  0.43 us (1%)
    ppermute x1, waiting for transfers between devices, body(): lax.ppermute(jnp.where(j_odd, last_rows, first_rows), 'narrow', pair_rela...  5.66 us
    pallas_call x1, Pallas kernels, body(): pl.pallas_call(functools.partial(fine_kernel, wide, narrow, c1), out_shap...  4.84 us
    ppermute x1, waiting for transfers between devices, body(): other = lax.ppermute(mine, 'narrow', pair_swap(narrow, bit))  4.6 us
    ppermute x1, waiting for transfers between devices, body(): pair = lax.ppermute(stored_features, 'wide', pair_swap(wide))  3.71 us
    ppermute x1, waiting for transfers between devices, body(): far = lax.ppermute(pair, 'wide', pair_relay_back(wide))  3.17 us
    ppermute x1, starting transfers between devices, body(): pair = lax.ppermute(stored_features, 'wide', pair_swap(wide))  3.05 us
    ppermute x1, waiting for transfers between devices, body(): pooled_pair = lax.ppermute(pooled, 'wide', pair_swap(wide))  2.24 us
    ppermute x1, waiting for transfers between devices, body(): pooled_far = lax.ppermute(pooled_pair, 'wide', pair_relay_back(wide))  2.18 us
  transfers between devices with their start and end apart: 8, of which 8 were waited for; matrix products, arithmetic and copies ran while one was open for 1% of the time, Pallas kernels for 1%

profile of v1, /device:TPU:0, one launch (start us, length us, event | category | flops | bytes accessed | tf_op | source)
XLA Modules:
  0.0 41.8 jit_solution(4686744184795652159)
XLA Ops:
  0.0 0.0 copy-start.3
  0.0 0.0 copy-start.4
  0.0 0.0 copy-start.5
  0.0 0.0 copy-start
  0.0 0.0 copy-start.1
  0.0 3.0 %collective-permute-start = (bf16[64,2,4,128]{3,2,1,0:T(4,128)(2,1)}, bf16[64,2,4,128]{3,2,1,0:T(4,128)(2,1)S(1)}, u32[]{:S(2)}, u32[]{:S(2)}) collective-permute-start(bf16[64,2,4,128]{3,2,1,0:T(4,128)(2,1)} %param.6), channel_id=1, source_target_pairs={{0,4},{4,0},{8,12},{12,8},{16,20},{20,16},{24,28},{28,24},{1,5},{5... | collective-permute-start | bytes 393224 | tf_op jit(solution)/shard_map/ppermute | solution.py:226
  3.1 3.7 %collective-permute-done = bf16[64,2,4,128]{3,2,1,0:T(4,128)(2,1)S(1)} collective-permute-done((bf16[64,2,4,128]{3,2,1,0:T(4,128)(2,1)}, bf16[64,2,4,128]{3,2,1,0:T(4,128)(2,1)S(1)}, u32[]{:S(2)}, u32[]{:S(2)}) %collective-permute-start) | collective-permute-done | bytes 131104 | tf_op jit(solution)/shard_map/ppermute | solution.py:226
  6.8 1.8 %collective-permute-start.1 = (bf16[64,2,4,128]{3,2,1,0:T(4,128)(2,1)S(1)}, bf16[64,2,4,128]{3,2,1,0:T(4,128)(2,1)S(1)}, u32[]{:S(2)}, u32[]{:S(2)}) collective-permute-start(bf16[64,2,4,128]{3,2,1,0:T(4,128)(2,1)S(1)} %collective-permute-done), channel_id=1, source_target_pairs={{4,0},{12,4},{0,8},{20,12},{8,16},{28,20},{16,24},{24,28},{5,1},{1... | collective-permute-start | bytes 393224 | tf_op jit(solution)/shard_map/ppermute | solution.py:239
  8.6 3.2 %collective-permute-done.1 = bf16[64,2,4,128]{3,2,1,0:T(4,128)(2,1)S(1)} collective-permute-done((bf16[64,2,4,128]{3,2,1,0:T(4,128)(2,1)S(1)}, bf16[64,2,4,128]{3,2,1,0:T(4,128)(2,1)S(1)}, u32[]{:S(2)}, u32[]{:S(2)}) %collective-permute-start.1) | collective-permute-done | bytes 131104 | tf_op jit(solution)/shard_map/ppermute | solution.py:239
  11.7 1.2 %pad_maximum_fusion = bf16[3,64,2,4,128]{4,3,2,1,0:T(4,128)(2,1)S(1)} fusion(bf16[1,64,2,4,128]{4,3,2,1,0:T(4,128)(2,1)S(1)} %bitcast.27, bf16[1,64,2,4,128]{4,3,2,1,0:T(4,128)(2,1)S(1)} %bitcast.25, bf16[1,64,2,4,128]{4,3,2,1,0:T(4,128)(2,1)} %bitcast.23), kind=kLoop, calls=%fused_computation | loop fusion | flops 393216 | bytes 786432 | tf_op jit(solution)/shard_map/stack | solution.py:241
  13.0 0.0 copy-start.2
  13.0 0.5 %fusion = (bf16[1,3,64,2,2,128]{5,4,3,2,1,0:T(2,128)(2,1)S(1)}, bf16[3,64,2,2,128]{4,3,2,1,0:T(2,128)(2,1)S(1)}) fusion(pred[]{:T(512)S(6)} %eq.5, bf16[3,64,2,4,128]{4,3,2,1,0:T(4,128)(2,1)S(1)} %pad_maximum_fusion), kind=kLoop, calls=%fused_computation.4 | loop fusion | flops 196608 | bytes 786433 | tf_op jit(solution)/shard_map/stack | solution.py:247
  13.4 0.0 collective-permute-start.2
  13.5 5.7 %collective-permute-done.2 = bf16[3,64,2,2,128]{4,3,2,1,0:T(2,128)(2,1)S(1)} collective-permute-done((bf16[3,64,2,2,128]{4,3,2,1,0:T(2,128)(2,1)S(1)}, bf16[3,64,2,2,128]{4,3,2,1,0:T(2,128)(2,1)S(1)}, u32[]{:S(2)}, u32[]{:S(2)}) %collective-permute-start.2) | collective-permute-done | bytes 196640 | tf_op jit(solution)/shard_map/ppermute | solution.py:243
  19.1 0.6 %pad_maximum_fusion.1 = bf16[2,3,64,2,2,128]{5,4,3,2,1,0:T(2,128)(2,1)S(1)} fusion(bf16[1,3,64,2,2,128]{5,4,3,2,1,0:T(2,128)(2,1)S(1)} %bitcast.31, bf16[1,3,64,2,2,128]{5,4,3,2,1,0:T(2,128)(2,1)S(1)} %get-tuple-element.11), kind=kLoop, calls=%fused_computation.1 | loop fusion | flops 196608 | bytes 786432 | tf_op jit(solution)/shard_map/stack | solution.py:247
  19.7 0.1 collective-permute-start.3
  19.8 0.0 copy-done.3
  19.8 0.2 copy.7.w2_ref
  20.0 0.0 copy-done.4
  20.0 0.1 copy.8.scale_ref
  20.1 0.0 copy-done.5
  20.1 0.1 copy.9.shift_ref
  20.2 0.0 copy-done
  20.2 0.0 copy-done.1
  20.2 0.5 %shard_map.64 = (bf16[256,3456]{1,0:T(8,128)(2,1)S(1)}, bf16[256,2304]{1,0:T(8,128)(2,1)S(1)}, bf16[576,384]{1,0:T(8,128)(2,1)S(1)}) custom-call(bf16[64,1728]{1,0:T(8,128)(2,1)S(1)} %copy-done.1, bf16[128,1728]{1,0:T(8,128)(2,1)S(1)} %copy.7.w2_ref, bf16[64,3456]{1,0:T(8,128)(2,1)S(1)} %copy-done), custom_call_target="tpu_custom_call" | custom-call | flops 1000000 | bytes 4000000 | tf_op jit(solution)/shard_map/pallas_call | solution.py:227
  20.7 0.8 %collective-permute-done.3 = bf16[2,3,64,2,2,128]{5,4,3,2,1,0:T(2,128)(2,1)S(1)} collective-permute-done((bf16[2,3,64,2,2,128]{5,4,3,2,1,0:T(2,128)(2,1)S(1)}, bf16[2,3,64,2,2,128]{5,4,3,2,1,0:T(2,128)(2,1)S(1)}, u32[]{:S(2)}, u32[]{:S(2)}) %collective-permute-start.3) | collective-permute-done | bytes 393248 | tf_op jit(solution)/shard_map/ppermute | solution.py:246
  21.5 0.0 copy-done.2
  21.5 4.8 %shard_map.65 = bf16[128,128]{1,0:T(8,128)(2,1)S(1)} custom-call(bf16[512,128]{1,0:T(8,128)(2,1)S(1)} %bitcast.24, bf16[512,128]{1,0:T(8,128)(2,1)S(1)} %bitcast.26, bf16[512,128]{1,0:T(8,128)(2,1)S(1)} %bitcast.28, bf16[1536,128]{1,0:T(8,128)(2,1)S(1)} %bitcast.30, f32[64,1]{1,0:T(8,128)S(1)} %copy.8.scale_ref, f32[64,1]{1,0:T(8,128)S(1)} %copy.9.shift_ref, ...), custom_call_target="tpu_custom_call" | custom-call | flops 2000000000 | bytes 4000000 | tf_op jit(solution)/shard_map/pallas_call | solution.py:250
  26.3 1.7 %collective-permute-start.4 = (bf16[128,128]{1,0:T(8,128)(2,1)S(1)}, bf16[128,128]{1,0:T(8,128)(2,1)S(1)}, u32[]{:S(2)}, u32[]{:S(2)}) collective-permute-start(bf16[128,128]{1,0:T(8,128)(2,1)S(1)} %shard_map.65), channel_id=1, source_target_pairs={{0,4},{4,0},{8,12},{12,8},{16,20},{20,16},{24,28},{28,24},{1,5},{5... | collective-permute-start | bytes 98312 | tf_op jit(solution)/shard_map/ppermute | solution.py:274
  28.1 2.2 %collective-permute-done.4 = bf16[128,128]{1,0:T(8,128)(2,1)S(1)} collective-permute-done((bf16[128,128]{1,0:T(8,128)(2,1)S(1)}, bf16[128,128]{1,0:T(8,128)(2,1)S(1)}, u32[]{:S(2)}, u32[]{:S(2)}) %collective-permute-start.4) | collective-permute-done | bytes 32800 | tf_op jit(solution)/shard_map/ppermute | solution.py:274
  30.3 1.7 %collective-permute-start.5 = (bf16[128,128]{1,0:T(8,128)(2,1)S(1)}, bf16[128,128]{1,0:T(8,128)(2,1)S(1)}, u32[]{:S(2)}, u32[]{:S(2)}) collective-permute-start(bf16[128,128]{1,0:T(8,128)(2,1)S(1)} %collective-permute-done.4), channel_id=1, source_target_pairs={{4,0},{12,4},{0,8},{20,12},{8,16},{28,20},{16,24},{24,28},{5,1},{1... | collective-permute-start | bytes 98312 | tf_op jit(solution)/shard_map/ppermute | solution.py:275
  32.0 2.2 %collective-permute-done.5 = bf16[128,128]{1,0:T(8,128)(2,1)S(1)} collective-permute-done((bf16[128,128]{1,0:T(8,128)(2,1)S(1)}, bf16[128,128]{1,0:T(8,128)(2,1)S(1)}, u32[]{:S(2)}, u32[]{:S(2)}) %collective-permute-start.5) | collective-permute-done | bytes 32800 | tf_op jit(solution)/shard_map/ppermute | solution.py:275
  34.2 0.1 collective-permute-start.6
  34.3 4.6 %collective-permute-done.6 = bf16[1,3,128,128]{3,2,1,0:T(8,128)(2,1)S(1)} collective-permute-done((bf16[1,3,128,128]{3,2,1,0:T(8,128)(2,1)S(1)}, bf16[1,3,128,128]{3,2,1,0:T(8,128)(2,1)S(1)}, u32[]{:S(2)}, u32[]{:S(2)}) %collective-permute-start.6) | collective-permute-done | bytes 98336 | tf_op jit(solution)/shard_map/ppermute | solution.py:279
  38.9 0.1 collective-permute-start.7
  39.0 1.4 %collective-permute-done.7.theirs_ref = bf16[2,3,128,128]{3,2,1,0:T(8,128)(2,1)S(1)} collective-permute-done((bf16[2,3,128,128]{3,2,1,0:T(8,128)(2,1)S(1)}, bf16[2,3,128,128]{3,2,1,0:T(8,128)(2,1)S(1)}, u32[]{:S(2)}, u32[]{:S(2)}) %collective-permute-start.7) | collective-permute-done | bytes 196640 | tf_op jit(solution)/shard_map/ppermute | solution.py:282
  40.5 1.4 %shard_map.66 = bf16[64,512]{1,0:T(8,128)(2,1)} custom-call(bf16[2,3,128,128]{3,2,1,0:T(8,128)(2,1)S(1)} %maximum_bitcast_fusion.mine_ref, bf16[2,3,128,128]{3,2,1,0:T(8,128)(2,1)S(1)} %collective-permute-done.7.theirs_ref, bf16[576,384]{1,0:T(8,128)(2,1)S(1)} %get-tuple-element.10.w3_ref), custom_call_target="tpu_custom_call" | custom-call | flops 1000000000 | bytes 1000000 | tf_op jit(solution)/shard_map/pallas_call | solution.py:284
  (2 shorter events, 0.0 us)
Async XLA Ops:
  0.0 19.8 %copy-start.3 = (bf16[128,1728]{0,1:T(8,128)(2,1)S(1)}, bf16[128,1728]{0,1:T(8,128)(2,1)}, u32[]{:S(2)}) copy-start(bf16[128,1728]{0,1:T(8,128)(2,1)} %param.10) | copy-start | bytes 1327108
  0.0 20.0 %copy-start.4 = (f32[64]{0:T(128)S(1)}, f32[64]{0:T(128)}, u32[]{:S(2)}) copy-start(f32[64]{0:T(128)} %param.7) | copy-start | bytes 772
  0.0 20.1 %copy-start.5 = (f32[64]{0:T(128)S(1)}, f32[64]{0:T(128)}, u32[]{:S(2)}) copy-start(f32[64]{0:T(128)} %param.8) | copy-start | bytes 772
  0.0 20.2 %copy-start = (bf16[64,3456]{1,0:T(8,128)(2,1)S(1)}, bf16[64,3456]{1,0:T(8,128)(2,1)}, u32[]{:S(2)}) copy-start(bf16[64,3456]{1,0:T(8,128)(2,1)} %w3_ref.1) | copy-start | bytes 1327108
  0.0 20.2 %copy-start.1 = (bf16[64,1728]{1,0:T(8,128)(2,1)S(1)}, bf16[64,1728]{1,0:T(8,128)(2,1)}, u32[]{:S(2)}) copy-start(bf16[64,1728]{1,0:T(8,128)(2,1)} %w1_ref.1) | copy-start | bytes 663556
  0.0 6.8 %collective-permute-start = (bf16[64,2,4,128]{3,2,1,0:T(4,128)(2,1)}, bf16[64,2,4,128]{3,2,1,0:T(4,128)(2,1)S(1)}, u32[]{:S(2)}, u32[]{:S(2)}) collective-permute-start(bf16[64,2,4,128]{3,2,1,0:T(4,128)(2,1)} %param.6), channel_id=1, source_target_pairs={{0,4},{4,0},{8,12},{12,8},{16,20},{20,16},{24,28},{28,24},{1,5},{5... | collective-permute-start | bytes 393224 | tf_op jit(solution)/shard_map/ppermute | solution.py:226
  6.8 5.0 %collective-permute-start.1 = (bf16[64,2,4,128]{3,2,1,0:T(4,128)(2,1)S(1)}, bf16[64,2,4,128]{3,2,1,0:T(4,128)(2,1)S(1)}, u32[]{:S(2)}, u32[]{:S(2)}) collective-permute-start(bf16[64,2,4,128]{3,2,1,0:T(4,128)(2,1)S(1)} %collective-permute-done), channel_id=1, source_target_pairs={{4,0},{12,4},{0,8},{20,12},{8,16},{28,20},{16,24},{24,28},{5,1},{1... | collective-permute-start | bytes 393224 | tf_op jit(solution)/shard_map/ppermute | solution.py:239
  13.0 8.5 %copy-start.2 = (bf16[64,2,4,128]{3,2,1,0:T(4,128)(2,1)S(1)}, bf16[64,2,4,128]{3,2,1,0:T(4,128)(2,1)}, u32[]{:S(2)}) copy-start(bf16[64,2,4,128]{3,2,1,0:T(4,128)(2,1)} %param.6) | copy-start | bytes 393220
  13.4 5.7 %collective-permute-start.2 = (bf16[3,64,2,2,128]{4,3,2,1,0:T(2,128)(2,1)S(1)}, bf16[3,64,2,2,128]{4,3,2,1,0:T(2,128)(2,1)S(1)}, u32[]{:S(2)}, u32[]{:S(2)}) collective-permute-start(bf16[3,64,2,2,128]{4,3,2,1,0:T(2,128)(2,1)S(1)} %get-tuple-element.12), channel_id=1, source_target_pairs={{0,1},{1,3},{2,0},{3,2},{4,5},{5,7},{6,4},{7,6},{8,9},{9,11},{10,8... | collective-permute-start | bytes 589832 | tf_op jit(solution)/shard_map/ppermute | solution.py:243
  19.7 1.8 %collective-permute-start.3 = (bf16[2,3,64,2,2,128]{5,4,3,2,1,0:T(2,128)(2,1)S(1)}, bf16[2,3,64,2,2,128]{5,4,3,2,1,0:T(2,128)(2,1)S(1)}, u32[]{:S(2)}, u32[]{:S(2)}) collective-permute-start(bf16[2,3,64,2,2,128]{5,4,3,2,1,0:T(2,128)(2,1)S(1)} %pad_maximum_fusion.1), channel_id=1, source_target_pairs={{0,1},{1,0},{2,3},{3,2},{4,5},{5,4},{6,7},{7,6},{8,9},{9,8},{10,11... | collective-permute-start | bytes 1179656 | tf_op jit(solution)/shard_map/ppermute | solution.py:246
  26.3 4.0 %collective-permute-start.4 = (bf16[128,128]{1,0:T(8,128)(2,1)S(1)}, bf16[128,128]{1,0:T(8,128)(2,1)S(1)}, u32[]{:S(2)}, u32[]{:S(2)}) collective-permute-start(bf16[128,128]{1,0:T(8,128)(2,1)S(1)} %shard_map.65), channel_id=1, source_target_pairs={{0,4},{4,0},{8,12},{12,8},{16,20},{20,16},{24,28},{28,24},{1,5},{5... | collective-permute-start | bytes 98312 | tf_op jit(solution)/shard_map/ppermute | solution.py:274
  30.3 3.9 %collective-permute-start.5 = (bf16[128,128]{1,0:T(8,128)(2,1)S(1)}, bf16[128,128]{1,0:T(8,128)(2,1)S(1)}, u32[]{:S(2)}, u32[]{:S(2)}) collective-permute-start(bf16[128,128]{1,0:T(8,128)(2,1)S(1)} %collective-permute-done.4), channel_id=1, source_target_pairs={{4,0},{12,4},{0,8},{20,12},{8,16},{28,20},{16,24},{24,28},{5,1},{1... | collective-permute-start | bytes 98312 | tf_op jit(solution)/shard_map/ppermute | solution.py:275
  34.2 4.7 %collective-permute-start.6 = (bf16[1,3,128,128]{3,2,1,0:T(8,128)(2,1)S(1)}, bf16[1,3,128,128]{3,2,1,0:T(8,128)(2,1)S(1)}, u32[]{:S(2)}, u32[]{:S(2)}) collective-permute-start(bf16[1,3,128,128]{3,2,1,0:T(8,128)(2,1)S(1)} %get-tuple-element.14), channel_id=1, source_target_pairs={{0,2},{1,3},{2,0},{3,1},{4,6},{5,7},{6,4},{7,5},{8,10},{9,11},{10,... | collective-permute-start | bytes 294920 | tf_op jit(solution)/shard_map/ppermute | solution.py:279
  38.9 1.5 %collective-permute-start.7 = (bf16[2,3,128,128]{3,2,1,0:T(8,128)(2,1)S(1)}, bf16[2,3,128,128]{3,2,1,0:T(8,128)(2,1)S(1)}, u32[]{:S(2)}, u32[]{:S(2)}) collective-permute-start(bf16[2,3,128,128]{3,2,1,0:T(8,128)(2,1)S(1)} %maximum_bitcast_fusion.mine_ref), channel_id=1, source_target_pairs={{0,1},{1,0},{2,3},{3,2},{4,5},{5,4},{6,7},{7,6},{8,9},{9,8},{10,11... | collective-permute-start | bytes 589832 | tf_op jit(solution)/shard_map/ppermute | solution.py:282

commit v2 on v1

v2 whole, which is shorter than its diff:
```python
import functools

import jax
import jax.numpy as jnp
from jax import lax
from jax.experimental import pallas as pl
from jax.experimental.pallas import tpu as pltpu
from jax.sharding import PartitionSpec as P

LANES = 128
VMEM = pl.BlockSpec(memory_space=pltpu.VMEM)


def pair_swap(count, bit=1):
    return [(k, k ^ bit) for k in range(count)]


def pair_relay(count):
    steps = []
    for k in range(count):
        target = k - 2 if k % 2 == 0 else k + 2
        steps.append((k, target if 0 <= target < count else k ^ 1))
    return steps


def pair_relay_back(count):
    return [(target, source) for source, target in pair_relay(count)]


def weights_kernel(w1_ref, w2_ref, w3_ref, t1_ref, t2_ref, t3_ref):
    o1 = w1_ref.shape[0]
    c1 = w1_ref.shape[1] // 27
    o2 = w2_ref.shape[0]
    c2 = w2_ref.shape[1] // 27
    o3 = w3_ref.shape[0]
    c3 = w3_ref.shape[1] // 27
    for ref, out, o, c, rows in ((w1_ref, t1_ref, o1, c1, 4), (w2_ref, t2_ref, o2, c2, 2)):
        span = (rows + 2) * c
        for be in range(9):
            taps = [ref[:, (a * 9 + be) * c : (a * 9 + be + 1) * c] for a in range(3)]
            for row in range(rows):
                parts = []
                if row:
                    parts.append(jnp.zeros((o, row * c), jnp.bfloat16))
                parts += taps
                if row < rows - 1:
                    parts.append(jnp.zeros((o, (rows - 1 - row) * c), jnp.bfloat16))
                out[row * o : (row + 1) * o, be * span : (be + 1) * span] = jnp.concatenate(
                    parts, axis=1
                )
    for be in range(9):
        for a in range(3):
            t3_ref[be * o3 : (be + 1) * o3, a * c3 : (a + 1) * c3] = w3_ref[
                :, (a * 9 + be) * c3 : (a * 9 + be + 1) * c3
            ]


def shifted(value):
    lane = lax.broadcasted_iota(jnp.int32, value.shape, 1)
    low = jnp.where(lane == 0, 0.0, pltpu.roll(value, 1, 1))
    high = jnp.where(lane == LANES - 1, 0.0, pltpu.roll(value, LANES - 1, 1))
    return low, value, high


def unpack_kernel(raw_ref, scale_ref, shift_ref, out_ref, staged):
    c = scale_ref.shape[0]
    depth, height = out_ref.shape[0] // c, out_ref.shape[1] // LANES
    staged[...] = raw_ref[...].astype(jnp.float32)
    scale, shift = scale_ref[...], shift_ref[...]
    for d in range(depth):
        for h in range(height):
            rows = staged[pl.ds(d * height + h, c, stride=depth * height), :]
            out_ref[d * c : (d + 1) * c, h * LANES : (h + 1) * LANES] = (
                rows * scale + shift
            ).astype(jnp.bfloat16)


def slab_kernel(
    wide, raw_ref, scale_ref, shift_ref, own_ref, pair_ref, out_ref, relay_ref, side_ref, staged
):
    i, j = lax.axis_index("wide"), lax.axis_index("narrow")
    i_odd, j_odd = lax.rem(i, 2), lax.rem(j, 2)
    block, columns = own_ref.shape
    c = scale_ref.shape[0]
    depth, height = block // c, columns // LANES
    far_row = pl.multiple_of(2 * i_odd * block, block)
    pair_row = pl.multiple_of((2 - 2 * i_odd) * block, block)
    staged[...] = raw_ref[...].astype(jnp.float32)
    scale, shift = scale_ref[...], shift_ref[...]
    for d in range(depth):
        for h in range(height):
            rows = staged[pl.ds(d * height + h, c, stride=depth * height), :]
            out_ref[
                pl.ds(pl.multiple_of(far_row + d * c, c), c), h * LANES : (h + 1) * LANES
            ] = (rows * scale + shift).astype(jnp.bfloat16)

    @pl.when(jnp.where(i_odd == 0, i == 0, i == wide - 1))
    def _():
        out_ref[pl.ds(far_row, block), :] = jnp.zeros((block, columns), jnp.bfloat16)

    out_ref[block : 2 * block, :] = own_ref[...]
    out_ref[pl.ds(pair_row, block), :] = pair_ref[...]
    half = columns // 2
    relay_ref[...] = out_ref[:, pl.ds(pl.multiple_of(j_odd * half, half), half)]
    side_ref[...] = out_ref[:, pl.ds(pl.multiple_of((1 - j_odd) * half, half), half)]


def dot(a, b):
    return jnp.dot(a, b, preferred_element_type=jnp.float32)


def tile(ref, *picks):
    return jnp.concatenate([ref[:, k * LANES : (k + 1) * LANES] for k in picks], axis=1)


def spread(value, ref, at):
    rows, columns = value.shape
    for k in range(columns // LANES):
        parts = shifted(value[:, k * LANES : (k + 1) * LANES].astype(jnp.float32))
        for e, part in enumerate(parts):
            ref[e * rows : (e + 1) * rows, pl.ds(at + k * LANES, LANES)] = part.astype(jnp.bfloat16)


def clear_depth(wide, ref):
    i = lax.axis_index("wide")
    span = ref.shape[0] // 3
    c = span // 4

    @pl.when(i == 0)
    def _():
        for e in range(3):
            ref[e * span : e * span + c, :] = jnp.zeros((c, ref.shape[1]), jnp.bfloat16)

    @pl.when(i == wide - 1)
    def _():
        for e in range(3):
            ref[e * span + 3 * c : (e + 1) * span, :] = jnp.zeros((c, ref.shape[1]), jnp.bfloat16)


def thirds(ref):
    span = ref.shape[1] // 3
    return [ref[:, b * span : (b + 1) * span] for b in range(3)]


def centre_kernel(wide, x_ref, w1_ref, w2_ref, p1_ref, p2_ref, taps, hidden):
    spread(x_ref[...], taps, 0)
    first = thirds(w1_ref)
    columns = jnp.concatenate(
        [taps[:, b * LANES : (b + 2) * LANES] for b in range(3)], axis=0
    )
    spread(jnp.maximum(dot(w1_ref[...], columns), 0.0), hidden, 0)
    clear_depth(wide, hidden)
    r0 = dot(first[0], tile(taps, 2, 3))
    r1 = dot(first[1], tile(taps, 0, 3))
    r2 = dot(first[2], tile(taps, 0, 1))
    p1_ref[:, 0:LANES] = r2[:, :LANES]
    p1_ref[:, LANES : 2 * LANES] = r2[:, LANES:] + r1[:, :LANES]
    p1_ref[:, 2 * LANES : 3 * LANES] = r1[:, LANES:] + r0[:, :LANES]
    p1_ref[:, 3 * LANES :] = r0[:, LANES:]
    both = hidden[...]
    q0, q1, q2 = (dot(w, both) for w in thirds(w2_ref))
    p2_ref[:, 0:LANES] = q2[:, :LANES]
    p2_ref[:, LANES : 2 * LANES] = q2[:, LANES:] + q1[:, :LANES]
    p2_ref[:, 2 * LANES : 3 * LANES] = q1[:, LANES:] + q0[:, :LANES]
    p2_ref[:, 3 * LANES :] = q0[:, LANES:]


def edge_kernel(
    wide, narrow, partner_ref, relayed_ref, p1_ref, p2_ref, w1_ref, w2_ref, out_ref, taps, hidden
):
    j = lax.axis_index("narrow")
    j_odd = lax.rem(j, 2)
    half = partner_ref.shape[1]
    spread(partner_ref[...], taps, pl.multiple_of((1 - j_odd) * half, half))
    spread(relayed_ref[...], taps, pl.multiple_of(j_odd * half, half))

    @pl.when(j == 0)
    def _():
        taps[:, :half] = jnp.zeros((taps.shape[0], half), jnp.bfloat16)

    @pl.when(j == narrow - 1)
    def _():
        taps[:, half:] = jnp.zeros((taps.shape[0], half), jnp.bfloat16)

    first = thirds(w1_ref)
    r0 = dot(first[0], tile(taps, 0, 1))
    r1 = dot(first[1], tile(taps, 1, 2))
    r2 = dot(first[2], tile(taps, 2, 3))
    rows = (
        r0[:, :LANES] + r1[:, :LANES],
        r0[:, LANES:],
        r2[:, :LANES],
        r1[:, LANES:] + r2[:, LANES:],
    )
    for k, value in enumerate(rows):
        spread(
            jnp.maximum(value + p1_ref[:, k * LANES : (k + 1) * LANES], 0.0), hidden, k * LANES
        )
    clear_depth(wide, hidden)

    @pl.when(j == 0)
    def _():
        hidden[:, :LANES] = jnp.zeros((hidden.shape[0], LANES), jnp.bfloat16)

    @pl.when(j == narrow - 1)
    def _():
        hidden[:, 3 * LANES :] = jnp.zeros((hidden.shape[0], LANES), jnp.bfloat16)

    second = thirds(w2_ref)
    q0 = dot(second[0], tile(hidden, 0, 1))
    q1 = dot(second[1], tile(hidden, 1, 2))
    q2 = dot(second[2], tile(hidden, 2, 3))
    outs = (
        q0[:, :LANES] + q1[:, :LANES],
        q0[:, LANES:],
        q2[:, :LANES],
        q1[:, LANES:] + q2[:, LANES:],
    )
    outs = [value + p2_ref[:, k * LANES : (k + 1) * LANES] for k, value in enumerate(outs)]
    c2 = out_ref.shape[0]
    best = []
    for n in range(2):
        value = jnp.maximum(outs[2 * n], outs[2 * n + 1])
        value = jnp.maximum(jnp.maximum(value[:c2], value[c2:]), 0.0)
        best.append(jnp.maximum(value, pltpu.roll(value, LANES - 1, 1)).astype(jnp.bfloat16))
    cell = lax.broadcasted_iota(jnp.int32, (2 * LANES, LANES), 0)
    target = lax.broadcasted_iota(jnp.int32, (2 * LANES, LANES), 1)
    pick = (cell == 2 * target).astype(jnp.bfloat16)
    out_ref[...] = dot(jnp.concatenate(best, axis=1), pick).astype(jnp.bfloat16)


def coarse_kernel(wide, narrow, mine_ref, theirs_ref, w3_ref, out_ref, slab):
    i, j = lax.axis_index("wide"), lax.axis_index("narrow")
    i_odd = lax.rem(i, 2)
    groups, _, c, lanes = mine_ref.shape
    slots = (1, 2 - 2 * i_odd, 2 * i_odd)
    for r in range(groups):
        for bit, ref in ((0, mine_ref), (1, theirs_ref)):
            lane = pl.multiple_of(jnp.bitwise_xor(j, 2 * r + bit) * lanes, lanes)
            for k in range(3):
                row = pl.multiple_of(slots[k] * c, c)
                slab[pl.ds(row, c), pl.ds(lane, lanes)] = ref[r, k]
    total = slab.shape[1]

    @pl.when(i == 0)
    def _():
        slab[0:c, :] = jnp.zeros((c, total), jnp.bfloat16)

    @pl.when(i == wide - 1)
    def _():
        slab[2 * c :, :] = jnp.zeros((c, total), jnp.bfloat16)

    o = out_ref.shape[0]
    width = lanes // 2
    z = jnp.dot(w3_ref[...], slab[...], preferred_element_type=jnp.float32)
    place = lax.broadcasted_iota(jnp.int32, (o, total), 1)
    column = lax.rem(place, width)
    result = None
    for e in range(3):
        low, mid, high = (z[(b * 3 + e) * o : (b * 3 + e + 1) * o] for b in range(3))
        low = jnp.where(place < width, 0.0, pltpu.roll(low, width, 1))
        high = jnp.where(place >= total - width, 0.0, pltpu.roll(high, total - width, 1))
        term = low + mid + high
        if e == 0:
            term = jnp.where(column == 0, 0.0, pltpu.roll(term, 1, 1))
        if e == 2:
            term = jnp.where(column == width - 1, 0.0, pltpu.roll(term, total - 1, 1))
        result = term if result is None else result + term
    out_ref[...] = jnp.maximum(result, 0.0).astype(jnp.bfloat16)


def body(
    wide, narrow, stored_features, channel_scale, channel_shift, first_weight, second_weight,
    third_weight,
):
    c1, depth, height, width = stored_features.shape
    c2 = second_weight.shape[0]
    o3 = third_weight.shape[0]
    params = pltpu.CompilerParams(vmem_limit_bytes=24 * 1024 * 1024)
    rows = c1 * depth * height
    columns = height * width
    scale, shift = channel_scale.reshape(c1, 1), channel_shift.reshape(c1, 1)

    def cost(flops, size):
        return pl.CostEstimate(flops=flops, bytes_accessed=size, transcendentals=0)

    def unpack(block):
        return pl.pallas_call(
            unpack_kernel,
            out_shape=jax.ShapeDtypeStruct((depth * c1, columns), jnp.bfloat16),
            in_specs=[VMEM] * 3,
            out_specs=VMEM,
            scratch_shapes=[pltpu.VMEM((rows, width), jnp.float32)],
            compiler_params=params,
            cost_estimate=cost(10**6, 10**6),
        )(block.reshape(rows, width), scale, shift)

    pair = lax.ppermute(stored_features, "wide", pair_swap(wide))
    t1, t2, t3 = pl.pallas_call(
        weights_kernel,
        out_shape=(
            jax.ShapeDtypeStruct((4 * c1, 9 * 6 * c1), jnp.bfloat16),
            jax.ShapeDtypeStruct((2 * c2, 9 * 4 * c1), jnp.bfloat16),
            jax.ShapeDtypeStruct((9 * o3, 3 * c2), jnp.bfloat16),
        ),
        in_specs=[VMEM] * 3,
        out_specs=(VMEM,) * 3,
        compiler_params=params,
        cost_estimate=cost(10**6, 4 * 10**6),
    )(first_weight, second_weight, third_weight)
    own_slab = unpack(stored_features)
    far = lax.ppermute(pair, "wide", pair_relay_back(wide))
    pair_slab = unpack(pair)
    slab, relay, side = pl.pallas_call(
        functools.partial(slab_kernel, wide),
        out_shape=(
            jax.ShapeDtypeStruct((6 * c1, columns), jnp.bfloat16),
            jax.ShapeDtypeStruct((6 * c1, columns // 2), jnp.bfloat16),
            jax.ShapeDtypeStruct((6 * c1, columns // 2), jnp.bfloat16),
        ),
        in_specs=[VMEM] * 5,
        out_specs=(VMEM,) * 3,
        scratch_shapes=[pltpu.VMEM((rows, width), jnp.float32)],
        compiler_params=params,
        cost_estimate=cost(10**6, 2 * 10**6),
    )(far.reshape(rows, width), scale, shift, own_slab, pair_slab)
    passed = lax.ppermute(relay, "narrow", pair_relay(narrow))
    partner_rows = lax.ppermute(side, "narrow", pair_swap(narrow))
    p1, p2 = pl.pallas_call(
        functools.partial(centre_kernel, wide),
        out_shape=(
            jax.ShapeDtypeStruct((4 * c1, 4 * width), jnp.float32),
            jax.ShapeDtypeStruct((2 * c2, 4 * width), jnp.float32),
        ),
        in_specs=[VMEM] * 3,
        out_specs=(VMEM,) * 2,
        scratch_shapes=[
            pltpu.VMEM((18 * c1, 4 * width), jnp.bfloat16),
            pltpu.VMEM((12 * c1, 2 * width), jnp.bfloat16),
        ],
        compiler_params=params,
        cost_estimate=cost(2 * 10**9, 4 * 10**6),
    )(slab, t1, t2)
    relayed_rows = lax.ppermute(passed, "narrow", pair_swap(narrow))
    pooled = pl.pallas_call(
        functools.partial(edge_kernel, wide, narrow),
        out_shape=jax.ShapeDtypeStruct((c2, LANES), jnp.bfloat16),
        in_specs=[VMEM] * 6,
        out_specs=VMEM,
        scratch_shapes=[
            pltpu.VMEM((18 * c1, 4 * width), jnp.bfloat16),
            pltpu.VMEM((12 * c1, 4 * width), jnp.bfloat16),
        ],
        compiler_params=params,
        cost_estimate=cost(10**9, 4 * 10**6),
    )(partner_rows, relayed_rows, p1, p2, t1, t2)
    pooled_pair = lax.ppermute(pooled, "wide", pair_swap(wide))
    pooled_far = lax.ppermute(pooled_pair, "wide", pair_relay_back(wide))
    mine = jnp.stack([pooled, pooled_pair, pooled_far])[None]
    bit = narrow // 2
    while bit > 1:
        other = lax.ppermute(mine, "narrow", pair_swap(narrow, bit))
        mine = jnp.stack([mine, other], axis=1).reshape((-1,) + mine.shape[1:])
        bit //= 2
    theirs = lax.ppermute(mine, "narrow", pair_swap(narrow))
    total = narrow * LANES
    coarse = pl.pallas_call(
        functools.partial(coarse_kernel, wide, narrow),
        out_shape=jax.ShapeDtypeStruct((o3, total), jnp.bfloat16),
        in_specs=[VMEM] * 3,
        out_specs=VMEM,
        scratch_shapes=[pltpu.VMEM((3 * c2, total), jnp.bfloat16)],
        compiler_params=params,
        cost_estimate=pl.CostEstimate(flops=10**9, bytes_accessed=10**6, transcendentals=0),
    )(mine, theirs, t3)
    return coarse[:, None, :]


def solution(mesh):
    in_specs = (P(None, "wide", "narrow", None), P(), P(), P(), P(), P("narrow", None))
    out_specs = P("narrow", "wide", None)
    return jax.shard_map(
        functools.partial(body, mesh.shape["wide"], mesh.shape["narrow"]),
        mesh=mesh,
        in_specs=in_specs,
        out_specs=out_specs,
        check_vma=False,
    )
```

time: 42 us -> 39.6 us (0.943)
  waiting for transfers between devices: 23.8 us -> 20.2 us
  local copies, waits for them, and re-layouts: 0.43 us -> 3.61 us
  other arithmetic: 2.28 us -> 0.04 us
    ppermute x1, waiting for transfers between devices: 3.17 us -> 0.56 us  [body(): far = lax.ppermute(pair, 'wide', pair_relay_back(wide))]
    another operation x3 -> x0, other arithmetic: 2.24 us -> none  [the longest x1 1.22 us: body(): blocks = jnp.stack([stored_features, pair, far])]
    unnamed x13 -> x7, local copies, waits for them, and re-layouts: 0.24 us -> 2.13 us
    reshape x2, local copies, waits for them, and re-layouts: 0.19 us -> 1.49 us  [body(): scale, shift = (channel_scale.reshape(c1, 1), channel_shift.reshape(c1, 1))]
    ppermute x2 -> x3, waiting for transfers between devices: 6.46 us -> 5.58 us  [the longest x1 5.58 us: body(): passed = lax.ppermute(relay, 'narrow', pair_relay(narrow))]
    pallas_call x1 -> x5, Pallas kernels: 4.84 us -> 5.05 us  [the longest x1 2.61 us: body(): pl.pallas_call(functools.partial(centre_kernel, wide), out_shape=(jax.Sha...]
  transfers between devices with their start and end apart: 8 -> 9, of which waited for: 8 -> 7; matrix products, arithmetic and copies ran while one was open for 1% -> 7% of each run, Pallas kernels for 1% -> 8%
where the time goes in v2:
time: 39.6 us; the launch traced here: 39.4 us
  waiting for transfers between devices  20.2 us (51%)
  starting transfers between devices  8.58 us (22%)
  Pallas kernels  6.88 us (17%)
  local copies, waits for them, and re-layouts  3.61 us (9%)
    ppermute x1, waiting for transfers between devices, body(): passed = lax.ppermute(relay, 'narrow', pair_relay(narrow))  5.58 us
    ppermute x1, waiting for transfers between devices, body(): other = lax.ppermute(mine, 'narrow', pair_swap(narrow, bit))  4.6 us
    ppermute x1, waiting for transfers between devices, body(): pair = lax.ppermute(stored_features, 'wide', pair_swap(wide))  3.7 us
    ppermute x1, starting transfers between devices, body(): pair = lax.ppermute(stored_features, 'wide', pair_swap(wide))  2.97 us
    pallas_call x1, Pallas kernels, body(): pl.pallas_call(functools.partial(centre_kernel, wide), out_shape=(jax.Sha...  2.61 us
    ppermute x1, waiting for transfers between devices, body(): pooled_pair = lax.ppermute(pooled, 'wide', pair_swap(wide))  2.18 us
    ppermute x1, waiting for transfers between devices, body(): pooled_far = lax.ppermute(pooled_pair, 'wide', pair_relay_back(wide))  2.13 us
    unnamed x7, local copies, waits for them, and re-layouts  2.13 us
  transfers between devices with their start and end apart: 9, of which 7 were waited for; matrix products, arithmetic and copies ran while one was open for 7% of the time, Pallas kernels for 8%

profile of v2, /device:TPU:0, one launch (start us, length us, event | category | flops | bytes accessed | tf_op | source)
XLA Modules:
  0.0 39.4 jit_solution(16728272004577244842)
XLA Ops:
  0.0 0.0 copy-start
  0.0 0.0 copy-start.1
  0.0 3.0 %collective-permute-start = (bf16[64,2,4,128]{3,2,1,0:T(4,128)(2,1)}, bf16[64,2,4,128]{3,2,1,0:T(4,128)(2,1)S(1)}, u32[]{:S(2)}, u32[]{:S(2)}) collective-permute-start(bf16[64,2,4,128]{3,2,1,0:T(4,128)(2,1)} %param.6), channel_id=1, source_target_pairs={{0,4},{4,0},{8,12},{12,8},{16,20},{20,16},{24,28},{28,24},{1,5},{5... | collective-permute-start | bytes 393224 | tf_op jit(solution)/shard_map/ppermute | solution.py:298
  3.0 3.7 %collective-permute-done = bf16[64,2,4,128]{3,2,1,0:T(4,128)(2,1)S(1)} collective-permute-done((bf16[64,2,4,128]{3,2,1,0:T(4,128)(2,1)}, bf16[64,2,4,128]{3,2,1,0:T(4,128)(2,1)S(1)}, u32[]{:S(2)}, u32[]{:S(2)}) %collective-permute-start) | collective-permute-done | bytes 131104 | tf_op jit(solution)/shard_map/ppermute | solution.py:298
  6.7 1.8 %collective-permute-start.1 = (bf16[64,2,4,128]{3,2,1,0:T(4,128)(2,1)S(1)}, bf16[64,2,4,128]{3,2,1,0:T(4,128)(2,1)S(1)}, u32[]{:S(2)}, u32[]{:S(2)}) collective-permute-start(bf16[64,2,4,128]{3,2,1,0:T(4,128)(2,1)S(1)} %collective-permute-done), channel_id=1, source_target_pairs={{4,0},{12,4},{0,8},{20,12},{8,16},{28,20},{16,24},{24,28},{5,1},{1... | collective-permute-start | bytes 393224 | tf_op jit(solution)/shard_map/ppermute | solution.py:312
  8.5 0.7 %copy.11.scale_ref = f32[64,1]{1,0:T(8,128)S(1)} copy(f32[64,1]{0,1:T(1,128)} %bitcast.23) | data formatting | bytes 512 | tf_op jit(solution)/shard_map/reshape | solution.py:282
  9.2 0.7 %copy.12.shift_ref = f32[64,1]{1,0:T(8,128)S(1)} copy(f32[64,1]{0,1:T(1,128)} %bitcast.24) | data formatting | bytes 512 | tf_op jit(solution)/shard_map/reshape | solution.py:282
  10.0 0.0 copy-start.2
  10.0 0.9 %copy-done.2 = bf16[64,2,4,128]{3,2,1,0:T(4,128)(2,1)S(1)} copy-done((bf16[64,2,4,128]{3,2,1,0:T(4,128)(2,1)S(1)}, bf16[64,2,4,128]{3,2,1,0:T(4,128)(2,1)}, u32[]{:S(2)}) %copy-start.2) | copy-done | bytes 131096
  10.9 0.1 shard_map.64.own_ref
  11.0 0.1 shard_map.65.pair_ref
  11.1 0.6 %collective-permute-done.1 = bf16[64,2,4,128]{3,2,1,0:T(4,128)(2,1)S(1)} collective-permute-done((bf16[64,2,4,128]{3,2,1,0:T(4,128)(2,1)S(1)}, bf16[64,2,4,128]{3,2,1,0:T(4,128)(2,1)S(1)}, u32[]{:S(2)}, u32[]{:S(2)}) %collective-permute-start.1) | collective-permute-done | bytes 131104 | tf_op jit(solution)/shard_map/ppermute | solution.py:312
  11.6 0.2 shard_map.66
  11.8 0.0 collective-permute-start.3
  11.8 0.1 collective-permute-start.2
  11.9 5.6 %collective-permute-done.3 = bf16[384,256]{1,0:T(8,128)(2,1)S(1)} collective-permute-done((bf16[384,256]{1,0:T(8,128)(2,1)S(1)}, bf16[384,256]{1,0:T(8,128)(2,1)S(1)}, u32[]{:S(2)}, u32[]{:S(2)}) %collective-permute-start.3) | collective-permute-done | bytes 196640 | tf_op jit(solution)/shard_map/ppermute | solution.py:327
  17.5 0.0 collective-permute-start.4
  17.5 1.2 %copy.13.w2_ref = bf16[128,1728]{1,0:T(8,128)(2,1)S(1)} copy(bf16[128,1728]{0,1:T(8,128)(2,1)} %param.10) | data formatting | bytes 884736 | tf_op args[4]
  18.7 0.0 copy-done
  18.7 0.0 copy-done.1
  18.7 0.5 %shard_map.67 = (bf16[256,3456]{1,0:T(8,128)(2,1)S(1)}, bf16[256,2304]{1,0:T(8,128)(2,1)S(1)}, bf16[576,384]{1,0:T(8,128)(2,1)S(1)}) custom-call(bf16[64,1728]{1,0:T(8,128)(2,1)S(1)} %copy-done.1, bf16[128,1728]{1,0:T(8,128)(2,1)S(1)} %copy.13.w2_ref, bf16[64,3456]{1,0:T(8,128)(2,1)S(1)} %copy-done), custom_call_target="tpu_custom_call" | custom-call | flops 1000000 | bytes 4000000 | tf_op jit(solution)/shard_map/pallas_call | solution.py:299
  19.2 2.6 %shard_map.68 = (f32[256,512]{1,0:T(8,128)S(1)}, f32[256,512]{1,0:T(8,128)S(1)}) custom-call(bf16[384,512]{1,0:T(8,128)(2,1)S(1)} %get-tuple-element.15.x_ref, bf16[256,3456]{1,0:T(8,128)(2,1)S(1)} %get-tuple-element.16.w1_ref, bf16[256,2304]{1,0:T(8,128)(2,1)S(1)} %get-tuple-element.17.w2_ref), custom_call_target="tpu_custom_call" | custom-call | flops 2000000000 | bytes 4000000 | tf_op jit(solution)/shard_map/pallas_call | solution.py:329
  21.8 0.0 collective-permute-done.2.partner_ref
  21.8 0.0 collective-permute-done.4.relayed_ref
  21.8 2.1 %shard_map.69 = bf16[128,128]{1,0:T(8,128)(2,1)S(1)} custom-call(bf16[384,256]{1,0:T(8,128)(2,1)S(1)} %collective-permute-done.2.partner_ref, bf16[384,256]{1,0:T(8,128)(2,1)S(1)} %collective-permute-done.4.relayed_ref, f32[256,512]{1,0:T(8,128)S(1)} %get-tuple-element.18.p1_ref, f32[256,512]{1,0:T(8,128)S(1)} %get-tuple-element.19.p2_ref, ...), custom_call_target="tpu_custom_call" | custom-call | flops 1000000000 | bytes 4000000 | tf_op jit(solution)/shard_map/pallas_call | solution.py:345
  23.9 1.8 %collective-permute-start.5 = (bf16[128,128]{1,0:T(8,128)(2,1)S(1)}, bf16[128,128]{1,0:T(8,128)(2,1)S(1)}, u32[]{:S(2)}, u32[]{:S(2)}) collective-permute-start(bf16[128,128]{1,0:T(8,128)(2,1)S(1)} %shard_map.69), channel_id=1, source_target_pairs={{0,4},{4,0},{8,12},{12,8},{16,20},{20,16},{24,28},{28,24},{1,5},{5... | collective-permute-start | bytes 98312 | tf_op jit(solution)/shard_map/ppermute | solution.py:357
  25.7 2.2 %collective-permute-done.5 = bf16[128,128]{1,0:T(8,128)(2,1)S(1)} collective-permute-done((bf16[128,128]{1,0:T(8,128)(2,1)S(1)}, bf16[128,128]{1,0:T(8,128)(2,1)S(1)}, u32[]{:S(2)}, u32[]{:S(2)}) %collective-permute-start.5) | collective-permute-done | bytes 32800 | tf_op jit(solution)/shard_map/ppermute | solution.py:357
  27.9 1.8 %collective-permute-start.6 = (bf16[128,128]{1,0:T(8,128)(2,1)S(1)}, bf16[128,128]{1,0:T(8,128)(2,1)S(1)}, u32[]{:S(2)}, u32[]{:S(2)}) collective-permute-start(bf16[128,128]{1,0:T(8,128)(2,1)S(1)} %collective-permute-done.5), channel_id=1, source_target_pairs={{4,0},{12,4},{0,8},{20,12},{8,16},{28,20},{16,24},{24,28},{5,1},{1... | collective-permute-start | bytes 98312 | tf_op jit(solution)/shard_map/ppermute | solution.py:358
  29.7 2.1 %collective-permute-done.6 = bf16[128,128]{1,0:T(8,128)(2,1)S(1)} collective-permute-done((bf16[128,128]{1,0:T(8,128)(2,1)S(1)}, bf16[128,128]{1,0:T(8,128)(2,1)S(1)}, u32[]{:S(2)}, u32[]{:S(2)}) %collective-permute-start.6) | collective-permute-done | bytes 32800 | tf_op jit(solution)/shard_map/ppermute | solution.py:358
  31.8 0.1 collective-permute-start.7
  31.9 4.6 %collective-permute-done.7 = bf16[1,3,128,128]{3,2,1,0:T(8,128)(2,1)S(1)} collective-permute-done((bf16[1,3,128,128]{3,2,1,0:T(8,128)(2,1)S(1)}, bf16[1,3,128,128]{3,2,1,0:T(8,128)(2,1)S(1)}, u32[]{:S(2)}, u32[]{:S(2)}) %collective-permute-start.7) | collective-permute-done | bytes 98336 | tf_op jit(solution)/shard_map/ppermute | solution.py:362
  36.5 0.1 collective-permute-start.8
  36.6 1.4 %collective-permute-done.8.theirs_ref = bf16[2,3,128,128]{3,2,1,0:T(8,128)(2,1)S(1)} collective-permute-done((bf16[2,3,128,128]{3,2,1,0:T(8,128)(2,1)S(1)}, bf16[2,3,128,128]{3,2,1,0:T(8,128)(2,1)S(1)}, u32[]{:S(2)}, u32[]{:S(2)}) %collective-permute-start.8) | collective-permute-done | bytes 196640 | tf_op jit(solution)/shard_map/ppermute | solution.py:365
  38.0 1.4 %shard_map.70 = bf16[64,512]{1,0:T(8,128)(2,1)} custom-call(bf16[2,3,128,128]{3,2,1,0:T(8,128)(2,1)S(1)} %maximum_bitcast_fusion.mine_ref, bf16[2,3,128,128]{3,2,1,0:T(8,128)(2,1)S(1)} %collective-permute-done.8.theirs_ref, bf16[576,384]{1,0:T(8,128)(2,1)S(1)} %get-tuple-element.20.w3_ref), custom_call_target="tpu_custom_call" | custom-call | flops 1000000000 | bytes 1000000 | tf_op jit(solution)/shard_map/pallas_call | solution.py:367
  (2 shorter events, 0.0 us)
Async XLA Ops:
  0.0 18.7 %copy-start = (bf16[64,3456]{1,0:T(8,128)(2,1)S(1)}, bf16[64,3456]{1,0:T(8,128)(2,1)}, u32[]{:S(2)}) copy-start(bf16[64,3456]{1,0:T(8,128)(2,1)} %w3_ref.1) | copy-start | bytes 1327108
  0.0 18.7 %copy-start.1 = (bf16[64,1728]{1,0:T(8,128)(2,1)S(1)}, bf16[64,1728]{1,0:T(8,128)(2,1)}, u32[]{:S(2)}) copy-start(bf16[64,1728]{1,0:T(8,128)(2,1)} %w1_ref.1) | copy-start | bytes 663556
  0.0 6.7 %collective-permute-start = (bf16[64,2,4,128]{3,2,1,0:T(4,128)(2,1)}, bf16[64,2,4,128]{3,2,1,0:T(4,128)(2,1)S(1)}, u32[]{:S(2)}, u32[]{:S(2)}) collective-permute-start(bf16[64,2,4,128]{3,2,1,0:T(4,128)(2,1)} %param.6), channel_id=1, source_target_pairs={{0,4},{4,0},{8,12},{12,8},{16,20},{20,16},{24,28},{28,24},{1,5},{5... | collective-permute-start | bytes 393224 | tf_op jit(solution)/shard_map/ppermute | solution.py:298
  6.7 5.0 %collective-permute-start.1 = (bf16[64,2,4,128]{3,2,1,0:T(4,128)(2,1)S(1)}, bf16[64,2,4,128]{3,2,1,0:T(4,128)(2,1)S(1)}, u32[]{:S(2)}, u32[]{:S(2)}) collective-permute-start(bf16[64,2,4,128]{3,2,1,0:T(4,128)(2,1)S(1)} %collective-permute-done), channel_id=1, source_target_pairs={{4,0},{12,4},{0,8},{20,12},{8,16},{28,20},{16,24},{24,28},{5,1},{1... | collective-permute-start | bytes 393224 | tf_op jit(solution)/shard_map/ppermute | solution.py:312
  10.0 0.9 %copy-start.2 = (bf16[64,2,4,128]{3,2,1,0:T(4,128)(2,1)S(1)}, bf16[64,2,4,128]{3,2,1,0:T(4,128)(2,1)}, u32[]{:S(2)}) copy-start(bf16[64,2,4,128]{3,2,1,0:T(4,128)(2,1)} %param.6) | copy-start | bytes 393220
  11.8 5.7 %collective-permute-start.3 = (bf16[384,256]{1,0:T(8,128)(2,1)S(1)}, bf16[384,256]{1,0:T(8,128)(2,1)S(1)}, u32[]{:S(2)}, u32[]{:S(2)}) collective-permute-start(bf16[384,256]{1,0:T(8,128)(2,1)S(1)} %get-tuple-element.14), channel_id=1, source_target_pairs={{0,1},{1,3},{2,0},{3,2},{4,5},{5,7},{6,4},{7,6},{8,9},{9,11},{10,8... | collective-permute-start | bytes 589832 | tf_op jit(solution)/shard_map/ppermute | solution.py:327
  11.8 10.0 %collective-permute-start.2 = (bf16[384,256]{1,0:T(8,128)(2,1)S(1)}, bf16[384,256]{1,0:T(8,128)(2,1)S(1)}, u32[]{:S(2)}, u32[]{:S(2)}) collective-permute-start(bf16[384,256]{1,0:T(8,128)(2,1)S(1)} %get-tuple-element.13), channel_id=1, source_target_pairs={{0,1},{1,0},{2,3},{3,2},{4,5},{5,4},{6,7},{7,6},{8,9},{9,8},{10,11... | collective-permute-start | bytes 589832 | tf_op jit(solution)/shard_map/ppermute | solution.py:328
  17.5 4.3 %collective-permute-start.4 = (bf16[384,256]{1,0:T(8,128)(2,1)S(1)}, bf16[384,256]{1,0:T(8,128)(2,1)S(1)}, u32[]{:S(2)}, u32[]{:S(2)}) collective-permute-start(bf16[384,256]{1,0:T(8,128)(2,1)S(1)} %collective-permute-done.3), channel_id=1, source_target_pairs={{0,1},{1,0},{2,3},{3,2},{4,5},{5,4},{6,7},{7,6},{8,9},{9,8},{10,11... | collective-permute-start | bytes 589832 | tf_op jit(solution)/shard_map/ppermute | solution.py:344
  23.9 4.0 %collective-permute-start.5 = (bf16[128,128]{1,0:T(8,128)(2,1)S(1)}, bf16[128,128]{1,0:T(8,128)(2,1)S(1)}, u32[]{:S(2)}, u32[]{:S(2)}) collective-permute-start(bf16[128,128]{1,0:T(8,128)(2,1)S(1)} %shard_map.69), channel_id=1, source_target_pairs={{0,4},{4,0},{8,12},{12,8},{16,20},{20,16},{24,28},{28,24},{1,5},{5... | collective-permute-start | bytes 98312 | tf_op jit(solution)/shard_map/ppermute | solution.py:357
  27.9 3.9 %collective-permute-start.6 = (bf16[128,128]{1,0:T(8,128)(2,1)S(1)}, bf16[128,128]{1,0:T(8,128)(2,1)S(1)}, u32[]{:S(2)}, u32[]{:S(2)}) collective-permute-start(bf16[128,128]{1,0:T(8,128)(2,1)S(1)} %collective-permute-done.5), channel_id=1, source_target_pairs={{4,0},{12,4},{0,8},{20,12},{8,16},{28,20},{16,24},{24,28},{5,1},{1... | collective-permute-start | bytes 98312 | tf_op jit(solution)/shard_map/ppermute | solution.py:358
  31.8 4.7 %collective-permute-start.7 = (bf16[1,3,128,128]{3,2,1,0:T(8,128)(2,1)S(1)}, bf16[1,3,128,128]{3,2,1,0:T(8,128)(2,1)S(1)}, u32[]{:S(2)}, u32[]{:S(2)}) collective-permute-start(bf16[1,3,128,128]{3,2,1,0:T(8,128)(2,1)S(1)} %get-tuple-element.22), channel_id=1, source_target_pairs={{0,2},{1,3},{2,0},{3,1},{4,6},{5,7},{6,4},{7,5},{8,10},{9,11},{10,... | collective-permute-start | bytes 294920 | tf_op jit(solution)/shard_map/ppermute | solution.py:362
  36.5 1.5 %collective-permute-start.8 = (bf16[2,3,128,128]{3,2,1,0:T(8,128)(2,1)S(1)}, bf16[2,3,128,128]{3,2,1,0:T(8,128)(2,1)S(1)}, u32[]{:S(2)}, u32[]{:S(2)}) collective-permute-start(bf16[2,3,128,128]{3,2,1,0:T(8,128)(2,1)S(1)} %maximum_bitcast_fusion.mine_ref), channel_id=1, source_target_pairs={{0,1},{1,0},{2,3},{3,2},{4,5},{5,4},{6,7},{7,6},{8,9},{9,8},{10,11... | collective-permute-start | bytes 589832 | tf_op jit(solution)/shard_map/ppermute | solution.py:365

commit v3 on v2

--- a/solution.py
+++ b/solution.py
@@ -62,11 +62,18 @@
     return low, value, high
 
 
+def column(row_ref):
+    row = row_ref[...]
+    square = (row.shape[1], row.shape[1])
+    here = lax.broadcasted_iota(jnp.int32, square, 0) == lax.broadcasted_iota(jnp.int32, square, 1)
+    return jnp.sum(jnp.where(here, jnp.broadcast_to(row, square), 0.0), axis=1, keepdims=True)
+
+
 def unpack_kernel(raw_ref, scale_ref, shift_ref, out_ref, staged):
-    c = scale_ref.shape[0]
+    c = scale_ref.shape[1]
     depth, height = out_ref.shape[0] // c, out_ref.shape[1] // LANES
     staged[...] = raw_ref[...].astype(jnp.float32)
-    scale, shift = scale_ref[...], shift_ref[...]
+    scale, shift = column(scale_ref), column(shift_ref)
     for d in range(depth):
         for h in range(height):
             rows = staged[pl.ds(d * height + h, c, stride=depth * height), :]
@@ -81,12 +88,12 @@
     i, j = lax.axis_index("wide"), lax.axis_index("narrow")
     i_odd, j_odd = lax.rem(i, 2), lax.rem(j, 2)
     block, columns = own_ref.shape
-    c = scale_ref.shape[0]
+    c = scale_ref.shape[1]
     depth, height = block // c, columns // LANES
     far_row = pl.multiple_of(2 * i_odd * block, block)
     pair_row = pl.multiple_of((2 - 2 * i_odd) * block, block)
     staged[...] = raw_ref[...].astype(jnp.float32)
-    scale, shift = scale_ref[...], shift_ref[...]
+    scale, shift = column(scale_ref), column(shift_ref)
     for d in range(depth):
         for h in range(height):
             rows = staged[pl.ds(d * height + h, c, stride=depth * height), :]
@@ -155,118 +162,139 @@
     r2 = dot(first[2], tile(taps, 0, 1))
     p1_ref[:, 0:LANES] = r2[:, :LANES]
     p1_ref[:, LANES : 2 * LANES] = r2[:, LANES:] + r1[:, :LANES]
-    p1_ref[:, 2 * LANES : 3 * LANES] = r1[:, LANES:] + r0[:, :LANES]
-    p1_ref[:, 3 * LANES :] = r0[:, LANES:]
+    p1_ref[:, 2 * LANES : 3 * LANES] = r0[:, LANES:]
+    p1_ref[:, 3 * LANES :] = r1[:, LANES:] + r0[:, :LANES]
     both = hidden[...]
     q0, q1, q2 = (dot(w, both) for w in thirds(w2_ref))
     p2_ref[:, 0:LANES] = q2[:, :LANES]
     p2_ref[:, LANES : 2 * LANES] = q2[:, LANES:] + q1[:, :LANES]
-    p2_ref[:, 2 * LANES : 3 * LANES] = q1[:, LANES:] + q0[:, :LANES]
-    p2_ref[:, 3 * LANES :] = q0[:, LANES:]
+    p2_ref[:, 2 * LANES : 3 * LANES] = q0[:, LANES:]
+    p2_ref[:, 3 * LANES :] = q1[:, LANES:] + q0[:, :LANES]
+
+
+def side_terms(wide, narrow, high, last, rows_ref, p1_ref, w1_ref, w2_ref, taps, hidden):
+    span1, span2 = w1_ref.shape[1] // 3, w2_ref.shape[1] // 3
+    outer1, outer2 = pl.multiple_of(2 * high * span1, LANES), pl.multiple_of(2 * high * span2, LANES)
+    for k in range(2):
+        at = pl.multiple_of((k + high * (1 - 2 * k)) * LANES, LANES)
+        spread(rows_ref[:, k * LANES : (k + 1) * LANES], taps, at)
+
+    @pl.when(last)
+    def _():
+        taps[...] = jnp.zeros_like(taps)
+
+    r = dot(w1_ref[:, pl.ds(outer1, span1)], taps[...])
+    r1 = dot(w1_ref[:, span1 : 2 * span1], taps[:, LANES:])
+    before = p1_ref[:, pl.ds(pl.multiple_of(high * 2 * LANES, LANES), 2 * LANES)]
+    spread(jnp.maximum(r[:, :LANES] + r1 + before[:, :LANES], 0.0), hidden, 0)
+    spread(jnp.maximum(r[:, LANES:] + before[:, LANES:], 0.0), hidden, LANES)
+    clear_depth(wide, hidden)
+
+    @pl.when(last)
+    def _():
+        hidden[:, :LANES] = jnp.zeros((hidden.shape[0], LANES), jnp.bfloat16)
+
+    q = dot(w2_ref[:, pl.ds(outer2, span2)], hidden[...])
+    q1 = dot(w2_ref[:, span2 : 2 * span2], hidden[:, LANES:])
+    return q[:, :LANES] + q1, q[:, LANES:]
+
+
+def partner_kernel(
+    wide, narrow, rows_ref, p1_ref, p2_ref, w1_ref, w2_ref, out_ref, taps, hidden
+):
+    high = 1 - lax.rem(lax.axis_index("narrow"), 2)
+    end, near = side_terms(
+        wide, narrow, high, False, rows_ref, p1_ref, w1_ref, w2_ref, taps, hidden
+    )
+    at = pl.multiple_of(high * 2 * LANES, LANES)
+    out_ref[...] = p2_ref[...]
+    out_ref[:, pl.ds(at, LANES)] += end
+    out_ref[:, pl.ds(at + LANES, LANES)] += near
 
 
 def edge_kernel(
-    wide, narrow, partner_ref, relayed_ref, p1_ref, p2_ref, w1_ref, w2_ref, out_ref, taps, hidden
+    wide, narrow, rows_ref, p1_ref, p2_ref, w1_ref, w2_ref, out_ref, taps, hidden
 ):
     j = lax.axis_index("narrow")
-    j_odd = lax.rem(j, 2)
-    half = partner_ref.shape[1]
-    spread(partner_ref[...], taps, pl.multiple_of((1 - j_odd) * half, half))
-    spread(relayed_ref[...], taps, pl.multiple_of(j_odd * half, half))
-
-    @pl.when(j == 0)
-    def _():
-        taps[:, :half] = jnp.zeros((taps.shape[0], half), jnp.bfloat16)
-
-    @pl.when(j == narrow - 1)
-    def _():
-        taps[:, half:] = jnp.zeros((taps.shape[0], half), jnp.bfloat16)
-
-    first = thirds(w1_ref)
-    r0 = dot(first[0], tile(taps, 0, 1))
-    r1 = dot(first[1], tile(taps, 1, 2))
-    r2 = dot(first[2], tile(taps, 2, 3))
-    rows = (
-        r0[:, :LANES] + r1[:, :LANES],
-        r0[:, LANES:],
-        r2[:, :LANES],
-        r1[:, LANES:] + r2[:, LANES:],
+    high = lax.rem(j, 2)
+    last = jnp.where(high == 0, j == 0, j == narrow - 1)
+    end, near = side_terms(
+        wide, narrow, high, last, rows_ref, p1_ref, w1_ref, w2_ref, taps, hidden
     )
-    for k, value in enumerate(rows):
-        spread(
-            jnp.maximum(value + p1_ref[:, k * LANES : (k + 1) * LANES], 0.0), hidden, k * LANES
-        )
-    clear_depth(wide, hidden)
-
-    @pl.when(j == 0)
-    def _():
-        hidden[:, :LANES] = jnp.zeros((hidden.shape[0], LANES), jnp.bfloat16)
-
-    @pl.when(j == narrow - 1)
-    def _():
-        hidden[:, 3 * LANES :] = jnp.zeros((hidden.shape[0], LANES), jnp.bfloat16)
-
-    second = thirds(w2_ref)
-    q0 = dot(second[0], tile(hidden, 0, 1))
-    q1 = dot(second[1], tile(hidden, 1, 2))
-    q2 = dot(second[2], tile(hidden, 2, 3))
-    outs = (
-        q0[:, :LANES] + q1[:, :LANES],
-        q0[:, LANES:],
-        q2[:, :LANES],
-        q1[:, LANES:] + q2[:, LANES:],
-    )
-    outs = [value + p2_ref[:, k * LANES : (k + 1) * LANES] for k, value in enumerate(outs)]
     c2 = out_ref.shape[0]
-    best = []
-    for n in range(2):
-        value = jnp.maximum(outs[2 * n], outs[2 * n + 1])
+    at = pl.multiple_of(high * 2 * LANES, LANES)
+    other = pl.multiple_of((1 - high) * 2 * LANES, LANES)
+
+    def best(one, two):
+        value = jnp.maximum(one, two)
         value = jnp.maximum(jnp.maximum(value[:c2], value[c2:]), 0.0)
-        best.append(jnp.maximum(value, pltpu.roll(value, LANES - 1, 1)).astype(jnp.bfloat16))
+        return jnp.maximum(value, pltpu.roll(value, LANES - 1, 1)).astype(jnp.bfloat16)
+
+    mine = best(end + p2_ref[:, pl.ds(at, LANES)], near + p2_ref[:, pl.ds(at + LANES, LANES)])
+    rest = best(p2_ref[:, pl.ds(other, LANES)], p2_ref[:, pl.ds(other + LANES, LANES)])
     cell = lax.broadcasted_iota(jnp.int32, (2 * LANES, LANES), 0)
     target = lax.broadcasted_iota(jnp.int32, (2 * LANES, LANES), 1)
-    pick = (cell == 2 * target).astype(jnp.bfloat16)
-    out_ref[...] = dot(jnp.concatenate(best, axis=1), pick).astype(jnp.bfloat16)
-
-
-def coarse_kernel(wide, narrow, mine_ref, theirs_ref, w3_ref, out_ref, slab):
+    wanted = jnp.bitwise_xor(2 * target, high * LANES)
+    pick = (cell == wanted).astype(jnp.bfloat16)
+    out_ref[...] = dot(jnp.concatenate([mine, rest], axis=1), pick).astype(jnp.bfloat16)
+
+
+def coarse_products(wide, bit, blocks_ref, w3_ref, z_ref, slab):
     i, j = lax.axis_index("wide"), lax.axis_index("narrow")
     i_odd = lax.rem(i, 2)
-    groups, _, c, lanes = mine_ref.shape
+    groups, _, c, lanes = blocks_ref.shape
     slots = (1, 2 - 2 * i_odd, 2 * i_odd)
     for r in range(groups):
-        for bit, ref in ((0, mine_ref), (1, theirs_ref)):
-            lane = pl.multiple_of(jnp.bitwise_xor(j, 2 * r + bit) * lanes, lanes)
-            for k in range(3):
-                row = pl.multiple_of(slots[k] * c, c)
-                slab[pl.ds(row, c), pl.ds(lane, lanes)] = ref[r, k]
-    total = slab.shape[1]
+        for k in range(3):
+            slab[pl.ds(pl.multiple_of(slots[k] * c, c), c), r * lanes : (r + 1) * lanes] = blocks_ref[
+                r, k
+            ]
 
     @pl.when(i == 0)
     def _():
-        slab[0:c, :] = jnp.zeros((c, total), jnp.bfloat16)
+        slab[0:c, :] = jnp.zeros((c, slab.shape[1]), jnp.bfloat16)
 
     @pl.when(i == wide - 1)
     def _():
-        slab[2 * c :, :] = jnp.zeros((c, total), jnp.bfloat16)
-
-    o = out_ref.shape[0]
-    width = lanes // 2
-    z = jnp.dot(w3_ref[...], slab[...], preferred_element_type=jnp.float32)
-    place = lax.broadcasted_iota(jnp.int32, (o, total), 1)
-    column = lax.rem(place, width)
-    result = None
-    for e in range(3):
-        low, mid, high = (z[(b * 3 + e) * o : (b * 3 + e + 1) * o] for b in range(3))
-        low = jnp.where(place < width, 0.0, pltpu.roll(low, width, 1))
-        high = jnp.where(place >= total - width, 0.0, pltpu.roll(high, total - width, 1))
-        term = low + mid + high
-        if e == 0:
-            term = jnp.where(column == 0, 0.0, pltpu.roll(term, 1, 1))
-        if e == 2:
-            term = jnp.where(column == width - 1, 0.0, pltpu.roll(term, total - 1, 1))
-        result = term if result is None else result + term
-    out_ref[...] = jnp.maximum(result, 0.0).astype(jnp.bfloat16)
+        slab[2 * c :, :] = jnp.zeros((c, slab.shape[1]), jnp.bfloat16)
+
+    z = dot(w3_ref[...], slab[...])
+    for r in range(groups):
+        at = pl.multiple_of(jnp.bitwise_xor(j, 2 * r + bit) * lanes, lanes)
+        z_ref[:, pl.ds(at, lanes)] = z[:, r * lanes : (r + 1) * lanes]
+
+
+def coarse_first_kernel(wide, blocks_ref, w3_ref, z_ref, slab):
+    coarse_products(wide, 0, blocks_ref, w3_ref, z_ref, slab)
+
+
+def coarse_kernel(wide, blocks_ref, w3_ref, first_ref, out_ref, z_ref, slab):
+    del first_ref
+    coarse_products(wide, 1, blocks_ref, w3_ref, z_ref, slab)
+    o, total = out_ref.shape
+    width = LANES // 2
+    count = total // LANES
+    lane = lax.broadcasted_iota(jnp.int32, (o, LANES), 1)
+    column_of = lax.rem(lane, width)
+
+    def z(b, e, q):
+        if q < 0 or q >= count:
+            return jnp.zeros((o, LANES), jnp.float32)
+        at = (b * 3 + e) * o
+        return z_ref[at : at + o, q * LANES : (q + 1) * LANES]
+
+    for q in range(count):
+        terms = []
+        for e in range(3):
+            crossed = jnp.where(
+                lane < width, z(0, e, q) + z(2, e, q + 1), z(0, e, q - 1) + z(2, e, q)
+            )
+            terms.append(z(1, e, q) + pltpu.roll(crossed, width, 1))
+        low = jnp.where(column_of == 0, 0.0, pltpu.roll(terms[0], 1, 1))
+        high = jnp.where(column_of == width - 1, 0.0, pltpu.roll(terms[2], LANES - 1, 1))
+        out_ref[:, q * LANES : (q + 1) * LANES] = jnp.maximum(low + terms[1] + high, 0.0).astype(
+            jnp.bfloat16
+        )
 
 
 def body(
@@ -279,7 +307,7 @@
     params = pltpu.CompilerParams(vmem_limit_bytes=24 * 1024 * 1024)
     rows = c1 * depth * height
     columns = height * width
-    scale, shift = channel_scale.reshape(c1, 1), channel_shift.reshape(c1, 1)
+    scale, shift = channel_scale.reshape(1, c1), channel_shift.reshape(1, c1)
 
     def cost(flops, size):
         return pl.CostEstimate(flops=flops, bytes_accessed=size, transcendentals=0)
@@ -309,6 +337,7 @@
         cost_estimate=cost(10**6, 4 * 10**6),
     )(first_weight, second_weight, third_weight)
     own_slab = unpack(stored_features)
+    pair, own_slab, t1, t2, t3 = lax.optimization_barrier((pair, own_slab, t1, t2, t3))
     far = lax.ppermute(pair, "wide", pair_relay_back(wide))
     pair_slab = unpack(pair)
     slab, relay, side = pl.pallas_call(
@@ -341,19 +370,25 @@
         compiler_params=params,
         cost_estimate=cost(2 * 10**9, 4 * 10**6),
     )(slab, t1, t2)
+    passed, p1, p2 = lax.optimization_barrier((passed, p1, p2))
     relayed_rows = lax.ppermute(passed, "narrow", pair_swap(narrow))
-    pooled = pl.pallas_call(
-        functools.partial(edge_kernel, wide, narrow),
-        out_shape=jax.ShapeDtypeStruct((c2, LANES), jnp.bfloat16),
-        in_specs=[VMEM] * 6,
-        out_specs=VMEM,
-        scratch_shapes=[
-            pltpu.VMEM((18 * c1, 4 * width), jnp.bfloat16),
-            pltpu.VMEM((12 * c1, 4 * width), jnp.bfloat16),
-        ],
-        compiler_params=params,
-        cost_estimate=cost(10**9, 4 * 10**6),
-    )(partner_rows, relayed_rows, p1, p2, t1, t2)
+
+    def side(kernel, out, rows, before):
+        return pl.pallas_call(
+            functools.partial(kernel, wide, narrow),
+            out_shape=out,
+            in_specs=[VMEM] * 5,
+            out_specs=VMEM,
+            scratch_shapes=[
+                pltpu.VMEM((18 * c1, 2 * width), jnp.bfloat16),
+                pltpu.VMEM((12 * c1, 2 * width), jnp.bfloat16),
+            ],
+            compiler_params=params,
+            cost_estimate=cost(10**9, 4 * 10**6),
+        )(rows, p1, before, t1, t2)
+
+    p2 = side(partner_kernel, jax.ShapeDtypeStruct(p2.shape, p2.dtype), partner_rows, p2)
+    pooled = side(edge_kernel, jax.ShapeDtypeStruct((c2, LANES), jnp.bfloat16), relayed_rows, p2)
     pooled_pair = lax.ppermute(pooled, "wide", pair_swap(wide))
     pooled_far = lax.ppermute(pooled_pair, "wide", pair_relay_back(wide))
     mine = jnp.stack([pooled, pooled_pair, pooled_far])[None]
@@ -364,15 +399,27 @@
         bit //= 2
     theirs = lax.ppermute(mine, "narrow", pair_swap(narrow))
     total = narrow * LANES
-    coarse = pl.pallas_call(
-        functools.partial(coarse_kernel, wide, narrow),
-        out_shape=jax.ShapeDtypeStruct((o3, total), jnp.bfloat16),
+    products = jax.ShapeDtypeStruct((9 * o3, total), jnp.float32)
+    scratch = [pltpu.VMEM((3 * c2, total // 2), jnp.bfloat16)]
+    first = pl.pallas_call(
+        functools.partial(coarse_first_kernel, wide),
+        out_shape=products,
+        in_specs=[VMEM] * 2,
+        out_specs=VMEM,
+        scratch_shapes=scratch,
+        compiler_params=params,
+        cost_estimate=cost(10**9, 10**6),
+    )(mine, t3)
+    coarse, _ = pl.pallas_call(
+        functools.partial(coarse_kernel, wide),
+        out_shape=(jax.ShapeDtypeStruct((o3, total), jnp.bfloat16), products),
         in_specs=[VMEM] * 3,
-        out_specs=VMEM,
-        scratch_shapes=[pltpu.VMEM((3 * c2, total), jnp.bfloat16)],
+        out_specs=(VMEM,) * 2,
+        scratch_shapes=scratch,
+        input_output_aliases={2: 1},
         compiler_params=params,
-        cost_estimate=pl.CostEstimate(flops=10**9, bytes_accessed=10**6, transcendentals=0),
-    )(mine, theirs, t3)
+        cost_estimate=cost(10**9, 10**6),
+    )(theirs, t3, first)
     return coarse[:, None, :]
 
 

time: 39.6 us -> 36.3 us (0.917)
  waiting for transfers between devices: 20.2 us -> 16.9 us
  Pallas kernels: 6.88 us -> 7.8 us
  starting transfers between devices: 8.58 us -> 7.81 us
    ppermute x1, waiting for transfers between devices: 3.7 us -> 0.01 us  [body(): pair = lax.ppermute(stored_features, 'wide', pair_swap(wide))]
    ppermute x1, waiting for transfers between devices: 0.56 us -> 3.28 us  [body(): far = lax.ppermute(pair, 'wide', pair_relay_back(wide))]
    ppermute x1, waiting for transfers between devices: 5.58 us -> 2.96 us  [body(): passed = lax.ppermute(relay, 'narrow', pair_relay(narrow))]
    reshape x2 -> x0, local copies, waits for them, and re-layouts: 1.49 us -> none  [body(): scale, shift = (channel_scale.reshape(c1, 1), channel_shift.reshape(c1, 1))]
    unnamed x7 -> x11, local copies, waits for them, and re-layouts: 2.13 us -> 3.43 us
    pallas_call x2 -> x4, Pallas kernels: 3.46 us -> 4.35 us  [the longest x2 2.71 us: side(): pl.pallas_call(functools.partial(kernel, wide, narrow), out_shape=out, in...]
  transfers between devices with their start and end apart: 9 -> 9, of which waited for: 7 -> 7; matrix products, arithmetic and copies ran while one was open for 7% -> 3% of each run, Pallas kernels for 8% -> 14%
where the time goes in v3:
time: 36.3 us; the launch traced here: 36.1 us
  waiting for transfers between devices  16.9 us (47%)
  starting transfers between devices  7.81 us (22%)
  Pallas kernels  7.8 us (21%)
  local copies, waits for them, and re-layouts  3.43 us (9%)
    ppermute x1, waiting for transfers between devices, body(): other = lax.ppermute(mine, 'narrow', pair_swap(narrow, bit))  4.6 us
    unnamed x11, local copies, waits for them, and re-layouts  3.43 us
    ppermute x1, waiting for transfers between devices, body(): far = lax.ppermute(pair, 'wide', pair_relay_back(wide))  3.28 us
    ppermute x1, starting transfers between devices, body(): pair = lax.ppermute(stored_features, 'wide', pair_swap(wide))  2.97 us
    ppermute x1, waiting for transfers between devices, body(): passed = lax.ppermute(relay, 'narrow', pair_relay(narrow))  2.96 us
    pallas_call x2, Pallas kernels, side(): pl.pallas_call(functools.partial(kernel, wide, narrow), out_shape=out, in...  2.71 us
    pallas_call x1, Pallas kernels, body(): pl.pallas_call(functools.partial(centre_kernel, wide), out_shape=(jax.Sha...  2.61 us
    ppermute x1, waiting for transfers between devices, body(): pooled_pair = lax.ppermute(pooled, 'wide', pair_swap(wide))  2.57 us
  transfers between devices with their start and end apart: 9, of which 7 were waited for; matrix products, arithmetic and copies ran while one was open for 3% of the time, Pallas kernels for 14%

profile of v3, /device:TPU:0, one launch (start us, length us, event | category | flops | bytes accessed | tf_op | source)
XLA Modules:
  0.0 36.1 jit_solution(8867919143147134424)
XLA Ops:
  0.0 0.0 copy-start
  0.0 0.0 copy-start.1
  0.0 3.0 %collective-permute-start = (bf16[64,2,4,128]{3,2,1,0:T(4,128)(2,1)}, bf16[64,2,4,128]{3,2,1,0:T(4,128)(2,1)S(1)}, u32[]{:S(2)}, u32[]{:S(2)}) collective-permute-start(bf16[64,2,4,128]{3,2,1,0:T(4,128)(2,1)} %param.6), channel_id=1, source_target_pairs={{0,4},{4,0},{8,12},{12,8},{16,20},{20,16},{24,28},{28,24},{1,5},{5... | collective-permute-start | bytes 393224 | tf_op jit(solution)/shard_map/ppermute | solution.py:326
  3.0 1.2 %copy.8.w2_ref = bf16[128,1728]{1,0:T(8,128)(2,1)S(1)} copy(bf16[128,1728]{0,1:T(8,128)(2,1)} %param.10) | data formatting | bytes 884736 | tf_op args[4]
  4.2 0.0 copy-start.2
  4.2 0.9 %copy-done.2 = bf16[64,2,4,128]{3,2,1,0:T(4,128)(2,1)S(1)} copy-done((bf16[64,2,4,128]{3,2,1,0:T(4,128)(2,1)S(1)}, bf16[64,2,4,128]{3,2,1,0:T(4,128)(2,1)}, u32[]{:S(2)}) %copy-start.2) | copy-done | bytes 131096
  5.1 0.0 copy-start.3
  5.1 0.7 %copy-done.3 = f32[64]{0:T(128)S(1)} copy-done((f32[64]{0:T(128)S(1)}, f32[64]{0:T(128)}, u32[]{:S(2)}) %copy-start.3) | copy-done | bytes 280
  5.8 0.0 copy-start.4
  5.8 0.7 %copy-done.4 = f32[64]{0:T(128)S(1)} copy-done((f32[64]{0:T(128)S(1)}, f32[64]{0:T(128)}, u32[]{:S(2)}) %copy-start.4) | copy-done | bytes 280
  6.4 0.1 shard_map.64.own_ref
  6.5 0.0 copy-done
  6.5 0.0 copy-done.1
  6.5 0.5 %shard_map.65 = (bf16[256,3456]{1,0:T(8,128)(2,1)S(1)}, bf16[256,2304]{1,0:T(8,128)(2,1)S(1)}, bf16[576,384]{1,0:T(8,128)(2,1)S(1)}) custom-call(bf16[64,1728]{1,0:T(8,128)(2,1)S(1)} %copy-done.1, bf16[128,1728]{1,0:T(8,128)(2,1)S(1)} %copy.8.w2_ref, bf16[64,3456]{1,0:T(8,128)(2,1)S(1)} %copy-done), custom_call_target="tpu_custom_call" | custom-call | flops 1000000 | bytes 4000000 | tf_op jit(solution)/shard_map/pallas_call | solution.py:327
  7.0 0.0 collective-permute-done
  7.0 1.6 %collective-permute-start.1 = (bf16[64,2,4,128]{3,2,1,0:T(4,128)(2,1)S(1)}, bf16[64,2,4,128]{3,2,1,0:T(4,128)(2,1)S(1)}, u32[]{:S(2)}, u32[]{:S(2)}) collective-permute-start(bf16[64,2,4,128]{3,2,1,0:T(4,128)(2,1)S(1)} %collective-permute-done), channel_id=1, source_target_pairs={{4,0},{12,4},{0,8},{20,12},{8,16},{28,20},{16,24},{24,28},{5,1},{1... | collective-permute-start | bytes 393224 | tf_op jit(solution)/shard_map/ppermute | solution.py:341
  8.6 0.1 shard_map.66.pair_ref
  8.8 3.3 %collective-permute-done.1 = bf16[64,2,4,128]{3,2,1,0:T(4,128)(2,1)S(1)} collective-permute-done((bf16[64,2,4,128]{3,2,1,0:T(4,128)(2,1)S(1)}, bf16[64,2,4,128]{3,2,1,0:T(4,128)(2,1)S(1)}, u32[]{:S(2)}, u32[]{:S(2)}) %collective-permute-start.1) | collective-permute-done | bytes 131104 | tf_op jit(solution)/shard_map/ppermute | solution.py:341
  12.0 0.2 shard_map.67
  12.2 0.0 collective-permute-start.2
  12.2 0.1 collective-permute-start.4
  12.3 2.6 %shard_map.68 = (f32[256,512]{1,0:T(8,128)S(1)}, f32[256,512]{1,0:T(8,128)S(1)}) custom-call(bf16[384,512]{1,0:T(8,128)(2,1)S(1)} %get-tuple-element.28.x_ref, bf16[256,3456]{1,0:T(8,128)(2,1)S(1)} %get-tuple-element.29.w1_ref, bf16[256,2304]{1,0:T(8,128)(2,1)S(1)} %get-tuple-element.30.w2_ref), custom_call_target="tpu_custom_call" | custom-call | flops 2000000000 | bytes 4000000 | tf_op jit(solution)/shard_map/pallas_call | solution.py:358
  14.9 3.0 %collective-permute-done.2 = bf16[384,256]{1,0:T(8,128)(2,1)S(1)} collective-permute-done((bf16[384,256]{1,0:T(8,128)(2,1)S(1)}, bf16[384,256]{1,0:T(8,128)(2,1)S(1)}, u32[]{:S(2)}, u32[]{:S(2)}) %collective-permute-start.2) | collective-permute-done | bytes 196640 | tf_op jit(solution)/shard_map/ppermute | solution.py:356
  17.9 0.0 collective-permute-start.3
  17.9 0.0 collective-permute-done.4.rows_ref
  17.9 1.3 %shard_map.69.p2_ref = f32[256,512]{1,0:T(8,128)S(1)} custom-call(bf16[384,256]{1,0:T(8,128)(2,1)S(1)} %collective-permute-done.4.rows_ref, f32[256,512]{1,0:T(8,128)S(1)} %get-tuple-element.34.p1_ref, f32[256,512]{1,0:T(8,128)S(1)} %get-tuple-element.36.p2_ref, bf16[256,3456]{1,0:T(8,128)(2,1)S(1)} %get-tuple-element.29.w1_ref, ...), custom_call_target="tpu_custom_call" | custom-call | flops 1000000000 | bytes 4000000 | tf_op jit(solution)/shard_map/pallas_call | solution.py:377
  19.2 0.1 collective-permute-done.3.rows_ref
  19.3 1.4 %shard_map.70 = bf16[128,128]{1,0:T(8,128)(2,1)S(1)} custom-call(bf16[384,256]{1,0:T(8,128)(2,1)S(1)} %collective-permute-done.3.rows_ref, f32[256,512]{1,0:T(8,128)S(1)} %get-tuple-element.34.p1_ref, f32[256,512]{1,0:T(8,128)S(1)} %shard_map.69.p2_ref, bf16[256,3456]{1,0:T(8,128)(2,1)S(1)} %get-tuple-element.29.w1_ref, ...), custom_call_target="tpu_custom_call" | custom-call | flops 1000000000 | bytes 4000000 | tf_op jit(solution)/shard_map/pallas_call | solution.py:377
  20.8 1.4 %collective-permute-start.5 = (bf16[128,128]{1,0:T(8,128)(2,1)S(1)}, bf16[128,128]{1,0:T(8,128)(2,1)S(1)}, u32[]{:S(2)}, u32[]{:S(2)}) collective-permute-start(bf16[128,128]{1,0:T(8,128)(2,1)S(1)} %shard_map.70), channel_id=1, source_target_pairs={{0,4},{4,0},{8,12},{12,8},{16,20},{20,16},{24,28},{28,24},{1,5},{5... | collective-permute-start | bytes 98312 | tf_op jit(solution)/shard_map/ppermute | solution.py:392
  22.2 2.6 %collective-permute-done.5 = bf16[128,128]{1,0:T(8,128)(2,1)S(1)} collective-permute-done((bf16[128,128]{1,0:T(8,128)(2,1)S(1)}, bf16[128,128]{1,0:T(8,128)(2,1)S(1)}, u32[]{:S(2)}, u32[]{:S(2)}) %collective-permute-start.5) | collective-permute-done | bytes 32800 | tf_op jit(solution)/shard_map/ppermute | solution.py:392
  24.7 1.6 %collective-permute-start.6 = (bf16[128,128]{1,0:T(8,128)(2,1)S(1)}, bf16[128,128]{1,0:T(8,128)(2,1)S(1)}, u32[]{:S(2)}, u32[]{:S(2)}) collective-permute-start(bf16[128,128]{1,0:T(8,128)(2,1)S(1)} %collective-permute-done.5), channel_id=1, source_target_pairs={{4,0},{12,4},{0,8},{20,12},{8,16},{28,20},{16,24},{24,28},{5,1},{1... | collective-permute-start | bytes 98312 | tf_op jit(solution)/shard_map/ppermute | solution.py:393
  26.3 2.3 %collective-permute-done.6 = bf16[128,128]{1,0:T(8,128)(2,1)S(1)} collective-permute-done((bf16[128,128]{1,0:T(8,128)(2,1)S(1)}, bf16[128,128]{1,0:T(8,128)(2,1)S(1)}, u32[]{:S(2)}, u32[]{:S(2)}) %collective-permute-start.6) | collective-permute-done | bytes 32800 | tf_op jit(solution)/shard_map/ppermute | solution.py:393
  28.7 0.1 collective-permute-start.7
  28.7 4.6 %collective-permute-done.7 = bf16[1,3,128,128]{3,2,1,0:T(8,128)(2,1)S(1)} collective-permute-done((bf16[1,3,128,128]{3,2,1,0:T(8,128)(2,1)S(1)}, bf16[1,3,128,128]{3,2,1,0:T(8,128)(2,1)S(1)}, u32[]{:S(2)}, u32[]{:S(2)}) %collective-permute-start.7) | collective-permute-done | bytes 98336 | tf_op jit(solution)/shard_map/ppermute | solution.py:397
  33.4 0.1 collective-permute-start.8
  33.5 0.4 %shard_map.71.first_ref = f32[576,512]{1,0:T(8,128)S(1)} custom-call(bf16[2,3,128,128]{3,2,1,0:T(8,128)(2,1)S(1)} %maximum_bitcast_fusion.blocks_ref, bf16[576,384]{1,0:T(8,128)(2,1)S(1)} %get-tuple-element.37.w3_ref), custom_call_target="tpu_custom_call" | custom-call | flops 1000000000 | bytes 1000000 | tf_op jit(solution)/shard_map/pallas_call | solution.py:404
  33.8 1.0 %collective-permute-done.8.blocks_ref = bf16[2,3,128,128]{3,2,1,0:T(8,128)(2,1)S(1)} collective-permute-done((bf16[2,3,128,128]{3,2,1,0:T(8,128)(2,1)S(1)}, bf16[2,3,128,128]{3,2,1,0:T(8,128)(2,1)S(1)}, u32[]{:S(2)}, u32[]{:S(2)}) %collective-permute-start.8) | collective-permute-done | bytes 196640 | tf_op jit(solution)/shard_map/ppermute | solution.py:400
  34.9 1.3 %shard_map.72 = (bf16[64,512]{1,0:T(8,128)(2,1)}, f32[576,512]{1,0:T(8,128)S(1)}) custom-call(bf16[2,3,128,128]{3,2,1,0:T(8,128)(2,1)S(1)} %collective-permute-done.8.blocks_ref, bf16[576,384]{1,0:T(8,128)(2,1)S(1)} %get-tuple-element.37.w3_ref, f32[576,512]{1,0:T(8,128)S(1)} %shard_map.71.first_ref), custom_call_target="tpu_custom_call", output_to_operand_aliasing={{1}: (2, {})} | custom-call | flops 1000000000 | bytes 1000000 | tf_op jit(solution)/shard_map/pallas_call | solution.py:413
  (2 shorter events, 0.0 us)
Async XLA Ops:
  0.0 6.5 %copy-start = (bf16[64,3456]{1,0:T(8,128)(2,1)S(1)}, bf16[64,3456]{1,0:T(8,128)(2,1)}, u32[]{:S(2)}) copy-start(bf16[64,3456]{1,0:T(8,128)(2,1)} %w3_ref.1) | copy-start | bytes 1327108
  0.0 6.5 %copy-start.1 = (bf16[64,1728]{1,0:T(8,128)(2,1)S(1)}, bf16[64,1728]{1,0:T(8,128)(2,1)}, u32[]{:S(2)}) copy-start(bf16[64,1728]{1,0:T(8,128)(2,1)} %w1_ref.1) | copy-start | bytes 663556
  0.0 7.0 %collective-permute-start = (bf16[64,2,4,128]{3,2,1,0:T(4,128)(2,1)}, bf16[64,2,4,128]{3,2,1,0:T(4,128)(2,1)S(1)}, u32[]{:S(2)}, u32[]{:S(2)}) collective-permute-start(bf16[64,2,4,128]{3,2,1,0:T(4,128)(2,1)} %param.6), channel_id=1, source_target_pairs={{0,4},{4,0},{8,12},{12,8},{16,20},{20,16},{24,28},{28,24},{1,5},{5... | collective-permute-start | bytes 393224 | tf_op jit(solution)/shard_map/ppermute | solution.py:326
  4.2 0.9 %copy-start.2 = (bf16[64,2,4,128]{3,2,1,0:T(4,128)(2,1)S(1)}, bf16[64,2,4,128]{3,2,1,0:T(4,128)(2,1)}, u32[]{:S(2)}) copy-start(bf16[64,2,4,128]{3,2,1,0:T(4,128)(2,1)} %param.6) | copy-start | bytes 393220
  5.1 0.7 %copy-start.3 = (f32[64]{0:T(128)S(1)}, f32[64]{0:T(128)}, u32[]{:S(2)}) copy-start(f32[64]{0:T(128)} %param.7) | copy-start | bytes 772
  5.8 0.7 %copy-start.4 = (f32[64]{0:T(128)S(1)}, f32[64]{0:T(128)}, u32[]{:S(2)}) copy-start(f32[64]{0:T(128)} %param.8) | copy-start | bytes 772
  7.0 5.0 %collective-permute-start.1 = (bf16[64,2,4,128]{3,2,1,0:T(4,128)(2,1)S(1)}, bf16[64,2,4,128]{3,2,1,0:T(4,128)(2,1)S(1)}, u32[]{:S(2)}, u32[]{:S(2)}) collective-permute-start(bf16[64,2,4,128]{3,2,1,0:T(4,128)(2,1)S(1)} %collective-permute-done), channel_id=1, source_target_pairs={{4,0},{12,4},{0,8},{20,12},{8,16},{28,20},{16,24},{24,28},{5,1},{1... | collective-permute-start | bytes 393224 | tf_op jit(solution)/shard_map/ppermute | solution.py:341
  12.2 5.7 %collective-permute-start.2 = (bf16[384,256]{1,0:T(8,128)(2,1)S(1)}, bf16[384,256]{1,0:T(8,128)(2,1)S(1)}, u32[]{:S(2)}, u32[]{:S(2)}) collective-permute-start(bf16[384,256]{1,0:T(8,128)(2,1)S(1)} %get-tuple-element.27), channel_id=1, source_target_pairs={{0,1},{1,3},{2,0},{3,2},{4,5},{5,7},{6,4},{7,6},{8,9},{9,11},{10,8... | collective-permute-start | bytes 589832 | tf_op jit(solution)/shard_map/ppermute | solution.py:356
  12.2 5.7 %collective-permute-start.4 = (bf16[384,256]{1,0:T(8,128)(2,1)S(1)}, bf16[384,256]{1,0:T(8,128)(2,1)S(1)}, u32[]{:S(2)}, u32[]{:S(2)}) collective-permute-start(bf16[384,256]{1,0:T(8,128)(2,1)S(1)} %get-tuple-element.35), channel_id=1, source_target_pairs={{0,1},{1,0},{2,3},{3,2},{4,5},{5,4},{6,7},{7,6},{8,9},{9,8},{10,11... | collective-permute-start | bytes 589832 | tf_op jit(solution)/shard_map/ppermute | solution.py:357
  17.9 1.4 %collective-permute-start.3 = (bf16[384,256]{1,0:T(8,128)(2,1)S(1)}, bf16[384,256]{1,0:T(8,128)(2,1)S(1)}, u32[]{:S(2)}, u32[]{:S(2)}) collective-permute-start(bf16[384,256]{1,0:T(8,128)(2,1)S(1)} %collective-permute-done.2), channel_id=1, source_target_pairs={{0,1},{1,0},{2,3},{3,2},{4,5},{5,4},{6,7},{7,6},{8,9},{9,8},{10,11... | collective-permute-start | bytes 589832 | tf_op jit(solution)/shard_map/ppermute | solution.py:374
  20.8 4.0 %collective-permute-start.5 = (bf16[128,128]{1,0:T(8,128)(2,1)S(1)}, bf16[128,128]{1,0:T(8,128)(2,1)S(1)}, u32[]{:S(2)}, u32[]{:S(2)}) collective-permute-start(bf16[128,128]{1,0:T(8,128)(2,1)S(1)} %shard_map.70), channel_id=1, source_target_pairs={{0,4},{4,0},{8,12},{12,8},{16,20},{20,16},{24,28},{28,24},{1,5},{5... | collective-permute-start | bytes 98312 | tf_op jit(solution)/shard_map/ppermute | solution.py:392
  24.7 3.9 %collective-permute-start.6 = (bf16[128,128]{1,0:T(8,128)(2,1)S(1)}, bf16[128,128]{1,0:T(8,128)(2,1)S(1)}, u32[]{:S(2)}, u32[]{:S(2)}) collective-permute-start(bf16[128,128]{1,0:T(8,128)(2,1)S(1)} %collective-permute-done.5), channel_id=1, source_target_pairs={{4,0},{12,4},{0,8},{20,12},{8,16},{28,20},{16,24},{24,28},{5,1},{1... | collective-permute-start | bytes 98312 | tf_op jit(solution)/shard_map/ppermute | solution.py:393
  28.7 4.7 %collective-permute-start.7 = (bf16[1,3,128,128]{3,2,1,0:T(8,128)(2,1)S(1)}, bf16[1,3,128,128]{3,2,1,0:T(8,128)(2,1)S(1)}, u32[]{:S(2)}, u32[]{:S(2)}) collective-permute-start(bf16[1,3,128,128]{3,2,1,0:T(8,128)(2,1)S(1)} %get-tuple-element.40), channel_id=1, source_target_pairs={{0,2},{1,3},{2,0},{3,1},{4,6},{5,7},{6,4},{7,5},{8,10},{9,11},{10,... | collective-permute-start | bytes 294920 | tf_op jit(solution)/shard_map/ppermute | solution.py:397
  33.4 1.5 %collective-permute-start.8 = (bf16[2,3,128,128]{3,2,1,0:T(8,128)(2,1)S(1)}, bf16[2,3,128,128]{3,2,1,0:T(8,128)(2,1)S(1)}, u32[]{:S(2)}, u32[]{:S(2)}) collective-permute-start(bf16[2,3,128,128]{3,2,1,0:T(8,128)(2,1)S(1)} %maximum_bitcast_fusion.blocks_ref), channel_id=1, source_target_pairs={{0,1},{1,0},{2,3},{3,2},{4,5},{5,4},{6,7},{7,6},{8,9},{9,8},{10,11... | collective-permute-start | bytes 589832 | tf_op jit(solution)/shard_map/ppermute | solution.py:400

commit v4 on v3

--- a/solution.py
+++ b/solution.py
@@ -27,7 +27,14 @@
     return [(target, source) for source, target in pair_relay(count)]
 
 
-def weights_kernel(w1_ref, w2_ref, w3_ref, t1_ref, t2_ref, t3_ref):
+def weights_kernel(wide, w1_ref, w2_ref, w3_ref, t1_ref, t2_ref, t3_ref):
+    i = lax.axis_index("wide")
+    keep_low = jnp.where(i == 0, 0.0, 1.0)
+    keep_high = jnp.where(i == wide - 1, 0.0, 1.0)
+
+    def kept(value, keep):
+        return (value.astype(jnp.float32) * keep).astype(jnp.bfloat16)
+
     o1 = w1_ref.shape[0]
     c1 = w1_ref.shape[1] // 27
     o2 = w2_ref.shape[0]
@@ -45,14 +52,16 @@
                 parts += taps
                 if row < rows - 1:
                     parts.append(jnp.zeros((o, (rows - 1 - row) * c), jnp.bfloat16))
-                out[row * o : (row + 1) * o, be * span : (be + 1) * span] = jnp.concatenate(
-                    parts, axis=1
-                )
+                value = jnp.concatenate(parts, axis=1)
+                if rows == 4 and row in (0, 3):
+                    value = kept(value, keep_low if row == 0 else keep_high)
+                out[row * o : (row + 1) * o, be * span : (be + 1) * span] = value
     for be in range(9):
         for a in range(3):
-            t3_ref[be * o3 : (be + 1) * o3, a * c3 : (a + 1) * c3] = w3_ref[
-                :, (a * 9 + be) * c3 : (a * 9 + be + 1) * c3
-            ]
+            value = w3_ref[:, (a * 9 + be) * c3 : (a * 9 + be + 1) * c3]
+            if a != 1:
+                value = kept(value, keep_low if a == 0 else keep_high)
+            t3_ref[be * o3 : (be + 1) * o3, a * c3 : (a + 1) * c3] = value
 
 
 def shifted(value):
@@ -92,19 +101,15 @@
     depth, height = block // c, columns // LANES
     far_row = pl.multiple_of(2 * i_odd * block, block)
     pair_row = pl.multiple_of((2 - 2 * i_odd) * block, block)
+    keep = jnp.where(i == i_odd * (wide - 1), 0.0, 1.0)
     staged[...] = raw_ref[...].astype(jnp.float32)
-    scale, shift = column(scale_ref), column(shift_ref)
+    scale, shift = column(scale_ref) * keep, column(shift_ref) * keep
     for d in range(depth):
         for h in range(height):
             rows = staged[pl.ds(d * height + h, c, stride=depth * height), :]
             out_ref[
                 pl.ds(pl.multiple_of(far_row + d * c, c), c), h * LANES : (h + 1) * LANES
             ] = (rows * scale + shift).astype(jnp.bfloat16)
-
-    @pl.when(jnp.where(i_odd == 0, i == 0, i == wide - 1))
-    def _():
-        out_ref[pl.ds(far_row, block), :] = jnp.zeros((block, columns), jnp.bfloat16)
-
     out_ref[block : 2 * block, :] = own_ref[...]
     out_ref[pl.ds(pair_row, block), :] = pair_ref[...]
     half = columns // 2
@@ -128,35 +133,18 @@
             ref[e * rows : (e + 1) * rows, pl.ds(at + k * LANES, LANES)] = part.astype(jnp.bfloat16)
 
 
-def clear_depth(wide, ref):
-    i = lax.axis_index("wide")
-    span = ref.shape[0] // 3
-    c = span // 4
-
-    @pl.when(i == 0)
-    def _():
-        for e in range(3):
-            ref[e * span : e * span + c, :] = jnp.zeros((c, ref.shape[1]), jnp.bfloat16)
-
-    @pl.when(i == wide - 1)
-    def _():
-        for e in range(3):
-            ref[e * span + 3 * c : (e + 1) * span, :] = jnp.zeros((c, ref.shape[1]), jnp.bfloat16)
-
-
 def thirds(ref):
     span = ref.shape[1] // 3
     return [ref[:, b * span : (b + 1) * span] for b in range(3)]
 
 
-def centre_kernel(wide, x_ref, w1_ref, w2_ref, p1_ref, p2_ref, taps, hidden):
+def centre_kernel(x_ref, w1_ref, p1_ref, hidden_ref, taps):
     spread(x_ref[...], taps, 0)
     first = thirds(w1_ref)
     columns = jnp.concatenate(
         [taps[:, b * LANES : (b + 2) * LANES] for b in range(3)], axis=0
     )
-    spread(jnp.maximum(dot(w1_ref[...], columns), 0.0), hidden, 0)
-    clear_depth(wide, hidden)
+    spread(jnp.maximum(dot(w1_ref[...], columns), 0.0), hidden_ref, 0)
     r0 = dot(first[0], tile(taps, 2, 3))
     r1 = dot(first[1], tile(taps, 0, 3))
     r2 = dot(first[2], tile(taps, 0, 1))
@@ -164,7 +152,10 @@
     p1_ref[:, LANES : 2 * LANES] = r2[:, LANES:] + r1[:, :LANES]
     p1_ref[:, 2 * LANES : 3 * LANES] = r0[:, LANES:]
     p1_ref[:, 3 * LANES :] = r1[:, LANES:] + r0[:, :LANES]
-    both = hidden[...]
+
+
+def second_kernel(hidden_ref, w2_ref, p2_ref):
+    both = hidden_ref[...]
     q0, q1, q2 = (dot(w, both) for w in thirds(w2_ref))
     p2_ref[:, 0:LANES] = q2[:, :LANES]
     p2_ref[:, LANES : 2 * LANES] = q2[:, LANES:] + q1[:, :LANES]
@@ -172,55 +163,38 @@
     p2_ref[:, 3 * LANES :] = q1[:, LANES:] + q0[:, :LANES]
 
 
-def side_terms(wide, narrow, high, last, rows_ref, p1_ref, w1_ref, w2_ref, taps, hidden):
+def side_terms(high, keep, rows_ref, p1_ref, w1_ref, w2_ref, taps, hidden):
     span1, span2 = w1_ref.shape[1] // 3, w2_ref.shape[1] // 3
     outer1, outer2 = pl.multiple_of(2 * high * span1, LANES), pl.multiple_of(2 * high * span2, LANES)
     for k in range(2):
         at = pl.multiple_of((k + high * (1 - 2 * k)) * LANES, LANES)
-        spread(rows_ref[:, k * LANES : (k + 1) * LANES], taps, at)
-
-    @pl.when(last)
-    def _():
-        taps[...] = jnp.zeros_like(taps)
-
+        value = rows_ref[:, k * LANES : (k + 1) * LANES].astype(jnp.float32)
+        spread(value if keep is None else value * keep, taps, at)
     r = dot(w1_ref[:, pl.ds(outer1, span1)], taps[...])
     r1 = dot(w1_ref[:, span1 : 2 * span1], taps[:, LANES:])
     before = p1_ref[:, pl.ds(pl.multiple_of(high * 2 * LANES, LANES), 2 * LANES)]
-    spread(jnp.maximum(r[:, :LANES] + r1 + before[:, :LANES], 0.0), hidden, 0)
+    end = jnp.maximum(r[:, :LANES] + r1 + before[:, :LANES], 0.0)
+    spread(end if keep is None else end * keep, hidden, 0)
     spread(jnp.maximum(r[:, LANES:] + before[:, LANES:], 0.0), hidden, LANES)
-    clear_depth(wide, hidden)
-
-    @pl.when(last)
-    def _():
-        hidden[:, :LANES] = jnp.zeros((hidden.shape[0], LANES), jnp.bfloat16)
-
     q = dot(w2_ref[:, pl.ds(outer2, span2)], hidden[...])
     q1 = dot(w2_ref[:, span2 : 2 * span2], hidden[:, LANES:])
     return q[:, :LANES] + q1, q[:, LANES:]
 
 
-def partner_kernel(
-    wide, narrow, rows_ref, p1_ref, p2_ref, w1_ref, w2_ref, out_ref, taps, hidden
-):
+def partner_kernel(narrow, rows_ref, p1_ref, p2_ref, w1_ref, w2_ref, out_ref, taps, hidden):
     high = 1 - lax.rem(lax.axis_index("narrow"), 2)
-    end, near = side_terms(
-        wide, narrow, high, False, rows_ref, p1_ref, w1_ref, w2_ref, taps, hidden
-    )
+    end, near = side_terms(high, None, rows_ref, p1_ref, w1_ref, w2_ref, taps, hidden)
     at = pl.multiple_of(high * 2 * LANES, LANES)
     out_ref[...] = p2_ref[...]
     out_ref[:, pl.ds(at, LANES)] += end
     out_ref[:, pl.ds(at + LANES, LANES)] += near
 
 
-def edge_kernel(
-    wide, narrow, rows_ref, p1_ref, p2_ref, w1_ref, w2_ref, out_ref, taps, hidden
-):
+def edge_kernel(narrow, rows_ref, p1_ref, p2_ref, w1_ref, w2_ref, out_ref, taps, hidden):
     j = lax.axis_index("narrow")
     high = lax.rem(j, 2)
-    last = jnp.where(high == 0, j == 0, j == narrow - 1)
-    end, near = side_terms(
-        wide, narrow, high, last, rows_ref, p1_ref, w1_ref, w2_ref, taps, hidden
-    )
+    keep = jnp.where(j == high * (narrow - 1), 0.0, 1.0)
+    end, near = side_terms(high, keep, rows_ref, p1_ref, w1_ref, w2_ref, taps, hidden)
     c2 = out_ref.shape[0]
     at = pl.multiple_of(high * 2 * LANES, LANES)
     other = pl.multiple_of((1 - high) * 2 * LANES, LANES)
@@ -239,7 +213,7 @@
     out_ref[...] = dot(jnp.concatenate([mine, rest], axis=1), pick).astype(jnp.bfloat16)
 
 
-def coarse_products(wide, bit, blocks_ref, w3_ref, z_ref, slab):
+def coarse_products(bit, blocks_ref, w3_ref, z_ref, slab):
     i, j = lax.axis_index("wide"), lax.axis_index("narrow")
     i_odd = lax.rem(i, 2)
     groups, _, c, lanes = blocks_ref.shape
@@ -250,27 +224,19 @@
                 r, k
             ]
 
-    @pl.when(i == 0)
-    def _():
-        slab[0:c, :] = jnp.zeros((c, slab.shape[1]), jnp.bfloat16)
-
-    @pl.when(i == wide - 1)
-    def _():
-        slab[2 * c :, :] = jnp.zeros((c, slab.shape[1]), jnp.bfloat16)
-
     z = dot(w3_ref[...], slab[...])
     for r in range(groups):
         at = pl.multiple_of(jnp.bitwise_xor(j, 2 * r + bit) * lanes, lanes)
         z_ref[:, pl.ds(at, lanes)] = z[:, r * lanes : (r + 1) * lanes]
 
 
-def coarse_first_kernel(wide, blocks_ref, w3_ref, z_ref, slab):
-    coarse_products(wide, 0, blocks_ref, w3_ref, z_ref, slab)
-
-
-def coarse_kernel(wide, blocks_ref, w3_ref, first_ref, out_ref, z_ref, slab):
+def coarse_first_kernel(blocks_ref, w3_ref, z_ref, slab):
+    coarse_products(0, blocks_ref, w3_ref, z_ref, slab)
+
+
+def coarse_kernel(blocks_ref, w3_ref, first_ref, out_ref, z_ref, slab):
     del first_ref
-    coarse_products(wide, 1, blocks_ref, w3_ref, z_ref, slab)
+    coarse_products(1, blocks_ref, w3_ref, z_ref, slab)
     o, total = out_ref.shape
     width = LANES // 2
     count = total // LANES
@@ -325,7 +291,7 @@
 
     pair = lax.ppermute(stored_features, "wide", pair_swap(wide))
     t1, t2, t3 = pl.pallas_call(
-        weights_kernel,
+        functools.partial(weights_kernel, wide),
         out_shape=(
             jax.ShapeDtypeStruct((4 * c1, 9 * 6 * c1), jnp.bfloat16),
             jax.ShapeDtypeStruct((2 * c2, 9 * 4 * c1), jnp.bfloat16),
@@ -336,8 +302,8 @@
         compiler_params=params,
         cost_estimate=cost(10**6, 4 * 10**6),
     )(first_weight, second_weight, third_weight)
+    pair, t1, t2, t3 = lax.optimization_barrier((pair, t1, t2, t3))
     own_slab = unpack(stored_features)
-    pair, own_slab, t1, t2, t3 = lax.optimization_barrier((pair, own_slab, t1, t2, t3))
     far = lax.ppermute(pair, "wide", pair_relay_back(wide))
     pair_slab = unpack(pair)
     slab, relay, side = pl.pallas_call(
@@ -354,28 +320,34 @@
         cost_estimate=cost(10**6, 2 * 10**6),
     )(far.reshape(rows, width), scale, shift, own_slab, pair_slab)
     passed = lax.ppermute(relay, "narrow", pair_relay(narrow))
-    partner_rows = lax.ppermute(side, "narrow", pair_swap(narrow))
-    p1, p2 = pl.pallas_call(
-        functools.partial(centre_kernel, wide),
+    p1, hidden = pl.pallas_call(
+        centre_kernel,
         out_shape=(
             jax.ShapeDtypeStruct((4 * c1, 4 * width), jnp.float32),
-            jax.ShapeDtypeStruct((2 * c2, 4 * width), jnp.float32),
+            jax.ShapeDtypeStruct((12 * c1, 2 * width), jnp.bfloat16),
         ),
-        in_specs=[VMEM] * 3,
+        in_specs=[VMEM] * 2,
         out_specs=(VMEM,) * 2,
-        scratch_shapes=[
-            pltpu.VMEM((18 * c1, 4 * width), jnp.bfloat16),
-            pltpu.VMEM((12 * c1, 2 * width), jnp.bfloat16),
-        ],
+        scratch_shapes=[pltpu.VMEM((18 * c1, 4 * width), jnp.bfloat16)],
         compiler_params=params,
         cost_estimate=cost(2 * 10**9, 4 * 10**6),
-    )(slab, t1, t2)
+    )(slab, t1)
+    side, p1, hidden = lax.optimization_barrier((side, p1, hidden))
+    partner_rows = lax.ppermute(side, "narrow", pair_swap(narrow))
+    p2 = pl.pallas_call(
+        second_kernel,
+        out_shape=jax.ShapeDtypeStruct((2 * c2, 4 * width), jnp.float32),
+        in_specs=[VMEM] * 2,
+        out_specs=VMEM,
+        compiler_params=params,
+        cost_estimate=cost(10**9, 2 * 10**6),
+    )(hidden, t2)
     passed, p1, p2 = lax.optimization_barrier((passed, p1, p2))
     relayed_rows = lax.ppermute(passed, "narrow", pair_swap(narrow))
 
-    def side(kernel, out, rows, before):
+    def add_side(kernel, out, rows, before):
         return pl.pallas_call(
-            functools.partial(kernel, wide, narrow),
+            functools.partial(kernel, narrow),
             out_shape=out,
             in_specs=[VMEM] * 5,
             out_specs=VMEM,
@@ -387,8 +359,8 @@
             cost_estimate=cost(10**9, 4 * 10**6),
         )(rows, p1, before, t1, t2)
 
-    p2 = side(partner_kernel, jax.ShapeDtypeStruct(p2.shape, p2.dtype), partner_rows, p2)
-    pooled = side(edge_kernel, jax.ShapeDtypeStruct((c2, LANES), jnp.bfloat16), relayed_rows, p2)
+    p2 = add_side(partner_kernel, jax.ShapeDtypeStruct(p2.shape, p2.dtype), partner_rows, p2)
+    pooled = add_side(edge_kernel, jax.ShapeDtypeStruct((c2, LANES), jnp.bfloat16), relayed_rows, p2)
     pooled_pair = lax.ppermute(pooled, "wide", pair_swap(wide))
     pooled_far = lax.ppermute(pooled_pair, "wide", pair_relay_back(wide))
     mine = jnp.stack([pooled, pooled_pair, pooled_far])[None]
@@ -402,7 +374,7 @@
     products = jax.ShapeDtypeStruct((9 * o3, total), jnp.float32)
     scratch = [pltpu.VMEM((3 * c2, total // 2), jnp.bfloat16)]
     first = pl.pallas_call(
-        functools.partial(coarse_first_kernel, wide),
+        coarse_first_kernel,
         out_shape=products,
         in_specs=[VMEM] * 2,
         out_specs=VMEM,
@@ -411,7 +383,7 @@
         cost_estimate=cost(10**9, 10**6),
     )(mine, t3)
     coarse, _ = pl.pallas_call(
-        functools.partial(coarse_kernel, wide),
+        coarse_kernel,
         out_shape=(jax.ShapeDtypeStruct((o3, total), jnp.bfloat16), products),
         in_specs=[VMEM] * 3,
         out_specs=(VMEM,) * 2,

time: 36.3 us -> 36 us (level)
  local copies, waits for them, and re-layouts: 3.43 us -> 2.16 us
  waiting for transfers between devices: 16.9 us -> 17.9 us
  Pallas kernels: 7.8 us -> 6.9 us
  starting transfers between devices: 7.81 us -> 8.7 us
    unnamed x11, local copies, waits for them, and re-layouts: 3.43 us -> 2.16 us
    ppermute x1, waiting for transfers between devices: 0.01 us -> 1.09 us  [body(): pair = lax.ppermute(stored_features, 'wide', pair_swap(wide))]
    pallas_call x6 -> x7, Pallas kernels: 7.41 us -> 6.51 us  [the longest x2 2.65 us: add_side(): pl.pallas_call(functools.partial(kernel, narrow), out_shape=out, in_specs...]
    ppermute x1, waiting for transfers between devices: 2.96 us -> 3.76 us  [body(): passed = lax.ppermute(relay, 'narrow', pair_relay(narrow))]
    ppermute x1, starting transfers between devices: 1.41 us -> 1.83 us  [body(): pooled_pair = lax.ppermute(pooled, 'wide', pair_swap(wide))]
    ppermute x1, waiting for transfers between devices: 2.57 us -> 2.18 us  [body(): pooled_pair = lax.ppermute(pooled, 'wide', pair_swap(wide))]
  transfers between devices with their start and end apart: 9 -> 9, of which waited for: 7 -> 8; matrix products, arithmetic and copies ran while one was open for 3% -> 3% of each run, Pallas kernels for 14% -> 12%
where the time goes in v4:
time: 36 us; the launch traced here: 35.8 us
  waiting for transfers between devices  17.9 us (50%)
  starting transfers between devices  8.7 us (24%)
  Pallas kernels  6.9 us (19%)
  local copies, waits for them, and re-layouts  2.16 us (6%)
    ppermute x1, waiting for transfers between devices, body(): other = lax.ppermute(mine, 'narrow', pair_swap(narrow, bit))  4.6 us
    ppermute x1, waiting for transfers between devices, body(): passed = lax.ppermute(relay, 'narrow', pair_relay(narrow))  3.76 us
    ppermute x1, starting transfers between devices, body(): pair = lax.ppermute(stored_features, 'wide', pair_swap(wide))  3.04 us
    ppermute x1, waiting for transfers between devices, body(): far = lax.ppermute(pair, 'wide', pair_relay_back(wide))  2.93 us
    pallas_call x2, Pallas kernels, add_side(): pl.pallas_call(functools.partial(kernel, narrow), out_shape=out, in_specs...  2.65 us
    ppermute x1, waiting for transfers between devices, body(): pooled_pair = lax.ppermute(pooled, 'wide', pair_swap(wide))  2.18 us
    unnamed x11, local copies, waits for them, and re-layouts  2.16 us
    ppermute x1, waiting for transfers between devices, body(): pooled_far = lax.ppermute(pooled_pair, 'wide', pair_relay_back(wide))  2.12 us
  transfers between devices with their start and end apart: 9, of which 8 were waited for; matrix products, arithmetic and copies ran while one was open for 3% of the time, Pallas kernels for 12%

profile of v4, /device:TPU:0, one launch (start us, length us, event | category | flops | bytes accessed | tf_op | source)
XLA Modules:
  0.0 35.8 jit_solution(15645823293176720974)
XLA Ops:
  0.0 0.0 copy-start.2
  0.0 0.0 copy-start
  0.0 0.0 copy-start.4
  0.0 0.0 copy-start.3
  0.0 3.0 %collective-permute-start = (bf16[64,2,4,128]{3,2,1,0:T(4,128)(2,1)}, bf16[64,2,4,128]{3,2,1,0:T(4,128)(2,1)S(1)}, u32[]{:S(2)}, u32[]{:S(2)}) collective-permute-start(bf16[64,2,4,128]{3,2,1,0:T(4,128)(2,1)} %param.6), channel_id=1, source_target_pairs={{0,4},{4,0},{8,12},{12,8},{16,20},{20,16},{24,28},{28,24},{1,5},{5... | collective-permute-start | bytes 393224 | tf_op jit(solution)/shard_map/ppermute | solution.py:292
  3.1 1.2 %copy.8.w2_ref = bf16[128,1728]{1,0:T(8,128)(2,1)S(1)} copy(bf16[128,1728]{0,1:T(8,128)(2,1)} %param.10) | data formatting | bytes 884736 | tf_op args[4]
  4.3 0.0 copy-done
  4.3 0.0 copy-start.1
  4.3 0.9 %copy-done.1 = bf16[64,1728]{1,0:T(8,128)(2,1)S(1)} copy-done((bf16[64,1728]{1,0:T(8,128)(2,1)S(1)}, bf16[64,1728]{1,0:T(8,128)(2,1)}, u32[]{:S(2)}) %copy-start.1) | copy-done | bytes 221208
  5.2 0.4 %shard_map.64 = (bf16[256,3456]{1,0:T(8,128)(2,1)S(1)}, bf16[256,2304]{1,0:T(8,128)(2,1)S(1)}, bf16[576,384]{1,0:T(8,128)(2,1)S(1)}) custom-call(bf16[64,1728]{1,0:T(8,128)(2,1)S(1)} %copy-done.1, bf16[128,1728]{1,0:T(8,128)(2,1)S(1)} %copy.8.w2_ref, bf16[64,3456]{1,0:T(8,128)(2,1)S(1)} %copy-done), custom_call_target="tpu_custom_call" | custom-call | flops 1000000 | bytes 4000000 | tf_op jit(solution)/shard_map/pallas_call | solution.py:293
  5.7 1.1 %collective-permute-done = bf16[64,2,4,128]{3,2,1,0:T(4,128)(2,1)S(1)} collective-permute-done((bf16[64,2,4,128]{3,2,1,0:T(4,128)(2,1)}, bf16[64,2,4,128]{3,2,1,0:T(4,128)(2,1)S(1)}, u32[]{:S(2)}, u32[]{:S(2)}) %collective-permute-start) | collective-permute-done | bytes 131104 | tf_op jit(solution)/shard_map/ppermute | solution.py:292
  6.8 1.8 %collective-permute-start.1 = (bf16[64,2,4,128]{3,2,1,0:T(4,128)(2,1)S(1)}, bf16[64,2,4,128]{3,2,1,0:T(4,128)(2,1)S(1)}, u32[]{:S(2)}, u32[]{:S(2)}) collective-permute-start(bf16[64,2,4,128]{3,2,1,0:T(4,128)(2,1)S(1)} %collective-permute-done), channel_id=1, source_target_pairs={{4,0},{12,4},{0,8},{20,12},{8,16},{28,20},{16,24},{24,28},{5,1},{1... | collective-permute-start | bytes 393224 | tf_op jit(solution)/shard_map/ppermute | solution.py:307
  8.6 0.0 copy-done.2
  8.6 0.0 copy-done.4
  8.6 0.0 copy-done.3
  8.6 0.1 shard_map.65.own_ref
  8.7 0.1 shard_map.66.pair_ref
  8.8 2.9 %collective-permute-done.1 = bf16[64,2,4,128]{3,2,1,0:T(4,128)(2,1)S(1)} collective-permute-done((bf16[64,2,4,128]{3,2,1,0:T(4,128)(2,1)S(1)}, bf16[64,2,4,128]{3,2,1,0:T(4,128)(2,1)S(1)}, u32[]{:S(2)}, u32[]{:S(2)}) %collective-permute-start.1) | collective-permute-done | bytes 131104 | tf_op jit(solution)/shard_map/ppermute | solution.py:307
  11.7 0.2 shard_map.67
  11.9 0.0 collective-permute-start.2
  11.9 1.3 %shard_map.68 = (f32[256,512]{1,0:T(8,128)S(1)}, bf16[768,256]{1,0:T(8,128)(2,1)S(1)}) custom-call(bf16[384,512]{1,0:T(8,128)(2,1)S(1)} %get-tuple-element.30.x_ref, bf16[256,3456]{1,0:T(8,128)(2,1)S(1)} %get-tuple-element.31.w1_ref), custom_call_target="tpu_custom_call" | custom-call | flops 2000000000 | bytes 4000000 | tf_op jit(solution)/shard_map/pallas_call | solution.py:323
  13.2 0.1 collective-permute-start.4
  13.3 0.5 %shard_map.69.p2_ref = f32[256,512]{1,0:T(8,128)S(1)} custom-call(bf16[768,256]{1,0:T(8,128)(2,1)S(1)} %get-tuple-element.35.hidden_ref, bf16[256,2304]{1,0:T(8,128)(2,1)S(1)} %get-tuple-element.36.w2_ref), custom_call_target="tpu_custom_call" | custom-call | flops 1000000000 | bytes 2000000 | tf_op jit(solution)/shard_map/pallas_call | solution.py:337
  13.8 3.8 %collective-permute-done.2 = bf16[384,256]{1,0:T(8,128)(2,1)S(1)} collective-permute-done((bf16[384,256]{1,0:T(8,128)(2,1)S(1)}, bf16[384,256]{1,0:T(8,128)(2,1)S(1)}, u32[]{:S(2)}, u32[]{:S(2)}) %collective-permute-start.2) | collective-permute-done | bytes 196640 | tf_op jit(solution)/shard_map/ppermute | solution.py:322
  17.6 0.0 collective-permute-start.3
  17.6 0.0 collective-permute-done.4.rows_ref
  17.6 1.3 %shard_map.70.p2_ref = f32[256,512]{1,0:T(8,128)S(1)} custom-call(bf16[384,256]{1,0:T(8,128)(2,1)S(1)} %collective-permute-done.4.rows_ref, f32[256,512]{1,0:T(8,128)S(1)} %get-tuple-element.38.p1_ref, f32[256,512]{1,0:T(8,128)S(1)} %shard_map.69.p2_ref, bf16[256,3456]{1,0:T(8,128)(2,1)S(1)} %get-tuple-element.31.w1_ref, ...), custom_call_target="tpu_custom_call" | custom-call | flops 1000000000 | bytes 4000000 | tf_op jit(solution)/shard_map/pallas_call | solution.py:349
  18.9 0.1 collective-permute-done.3.rows_ref
  19.0 1.4 %shard_map.71 = bf16[128,128]{1,0:T(8,128)(2,1)S(1)} custom-call(bf16[384,256]{1,0:T(8,128)(2,1)S(1)} %collective-permute-done.3.rows_ref, f32[256,512]{1,0:T(8,128)S(1)} %get-tuple-element.38.p1_ref, f32[256,512]{1,0:T(8,128)S(1)} %shard_map.70.p2_ref, bf16[256,3456]{1,0:T(8,128)(2,1)S(1)} %get-tuple-element.31.w1_ref, ...), custom_call_target="tpu_custom_call" | custom-call | flops 1000000000 | bytes 4000000 | tf_op jit(solution)/shard_map/pallas_call | solution.py:349
  20.4 1.8 %collective-permute-start.5 = (bf16[128,128]{1,0:T(8,128)(2,1)S(1)}, bf16[128,128]{1,0:T(8,128)(2,1)S(1)}, u32[]{:S(2)}, u32[]{:S(2)}) collective-permute-start(bf16[128,128]{1,0:T(8,128)(2,1)S(1)} %shard_map.71), channel_id=1, source_target_pairs={{0,4},{4,0},{8,12},{12,8},{16,20},{20,16},{24,28},{28,24},{1,5},{5... | collective-permute-start | bytes 98312 | tf_op jit(solution)/shard_map/ppermute | solution.py:364
  22.2 2.2 %collective-permute-done.5 = bf16[128,128]{1,0:T(8,128)(2,1)S(1)} collective-permute-done((bf16[128,128]{1,0:T(8,128)(2,1)S(1)}, bf16[128,128]{1,0:T(8,128)(2,1)S(1)}, u32[]{:S(2)}, u32[]{:S(2)}) %collective-permute-start.5) | collective-permute-done | bytes 32800 | tf_op jit(solution)/shard_map/ppermute | solution.py:364
  24.4 1.8 %collective-permute-start.6 = (bf16[128,128]{1,0:T(8,128)(2,1)S(1)}, bf16[128,128]{1,0:T(8,128)(2,1)S(1)}, u32[]{:S(2)}, u32[]{:S(2)}) collective-permute-start(bf16[128,128]{1,0:T(8,128)(2,1)S(1)} %collective-permute-done.5), channel_id=1, source_target_pairs={{4,0},{12,4},{0,8},{20,12},{8,16},{28,20},{16,24},{24,28},{5,1},{1... | collective-permute-start | bytes 98312 | tf_op jit(solution)/shard_map/ppermute | solution.py:365
  26.2 2.1 %collective-permute-done.6 = bf16[128,128]{1,0:T(8,128)(2,1)S(1)} collective-permute-done((bf16[128,128]{1,0:T(8,128)(2,1)S(1)}, bf16[128,128]{1,0:T(8,128)(2,1)S(1)}, u32[]{:S(2)}, u32[]{:S(2)}) %collective-permute-start.6) | collective-permute-done | bytes 32800 | tf_op jit(solution)/shard_map/ppermute | solution.py:365
  28.3 0.1 collective-permute-start.7
  28.4 4.6 %collective-permute-done.7 = bf16[1,3,128,128]{3,2,1,0:T(8,128)(2,1)S(1)} collective-permute-done((bf16[1,3,128,128]{3,2,1,0:T(8,128)(2,1)S(1)}, bf16[1,3,128,128]{3,2,1,0:T(8,128)(2,1)S(1)}, u32[]{:S(2)}, u32[]{:S(2)}) %collective-permute-start.7) | collective-permute-done | bytes 98336 | tf_op jit(solution)/shard_map/ppermute | solution.py:369
  33.0 0.1 collective-permute-start.8
  33.1 0.4 %shard_map.72.first_ref = f32[576,512]{1,0:T(8,128)S(1)} custom-call(bf16[2,3,128,128]{3,2,1,0:T(8,128)(2,1)S(1)} %maximum_bitcast_fusion.blocks_ref, bf16[576,384]{1,0:T(8,128)(2,1)S(1)} %get-tuple-element.41.w3_ref), custom_call_target="tpu_custom_call" | custom-call | flops 1000000000 | bytes 1000000 | tf_op jit(solution)/shard_map/pallas_call | solution.py:376
  33.5 1.0 %collective-permute-done.8.blocks_ref = bf16[2,3,128,128]{3,2,1,0:T(8,128)(2,1)S(1)} collective-permute-done((bf16[2,3,128,128]{3,2,1,0:T(8,128)(2,1)S(1)}, bf16[2,3,128,128]{3,2,1,0:T(8,128)(2,1)S(1)}, u32[]{:S(2)}, u32[]{:S(2)}) %collective-permute-start.8) | collective-permute-done | bytes 196640 | tf_op jit(solution)/shard_map/ppermute | solution.py:372
  34.5 1.3 %shard_map.73 = (bf16[64,512]{1,0:T(8,128)(2,1)}, f32[576,512]{1,0:T(8,128)S(1)}) custom-call(bf16[2,3,128,128]{3,2,1,0:T(8,128)(2,1)S(1)} %collective-permute-done.8.blocks_ref, bf16[576,384]{1,0:T(8,128)(2,1)S(1)} %get-tuple-element.41.w3_ref, f32[576,512]{1,0:T(8,128)S(1)} %shard_map.72.first_ref), custom_call_target="tpu_custom_call", output_to_operand_aliasing={{1}: (2, {})} | custom-call | flops 1000000000 | bytes 1000000 | tf_op jit(solution)/shard_map/pallas_call | solution.py:385
  (2 shorter events, 0.0 us)
Async XLA Ops:
  0.0 8.6 %copy-start.2 = (bf16[64,2,4,128]{3,2,1,0:T(4,128)(2,1)S(1)}, bf16[64,2,4,128]{3,2,1,0:T(4,128)(2,1)}, u32[]{:S(2)}) copy-start(bf16[64,2,4,128]{3,2,1,0:T(4,128)(2,1)} %param.6) | copy-start | bytes 393220
  0.0 4.3 %copy-start = (bf16[64,3456]{1,0:T(8,128)(2,1)S(1)}, bf16[64,3456]{1,0:T(8,128)(2,1)}, u32[]{:S(2)}) copy-start(bf16[64,3456]{1,0:T(8,128)(2,1)} %w3_ref.1) | copy-start | bytes 1327108
  0.0 8.6 %copy-start.4 = (f32[64]{0:T(128)S(1)}, f32[64]{0:T(128)}, u32[]{:S(2)}) copy-start(f32[64]{0:T(128)} %param.8) | copy-start | bytes 772
  0.0 8.6 %copy-start.3 = (f32[64]{0:T(128)S(1)}, f32[64]{0:T(128)}, u32[]{:S(2)}) copy-start(f32[64]{0:T(128)} %param.7) | copy-start | bytes 772
  0.0 6.7 %collective-permute-start = (bf16[64,2,4,128]{3,2,1,0:T(4,128)(2,1)}, bf16[64,2,4,128]{3,2,1,0:T(4,128)(2,1)S(1)}, u32[]{:S(2)}, u32[]{:S(2)}) collective-permute-start(bf16[64,2,4,128]{3,2,1,0:T(4,128)(2,1)} %param.6), channel_id=1, source_target_pairs={{0,4},{4,0},{8,12},{12,8},{16,20},{20,16},{24,28},{28,24},{1,5},{5... | collective-permute-start | bytes 393224 | tf_op jit(solution)/shard_map/ppermute | solution.py:292
  4.3 0.9 %copy-start.1 = (bf16[64,1728]{1,0:T(8,128)(2,1)S(1)}, bf16[64,1728]{1,0:T(8,128)(2,1)}, u32[]{:S(2)}) copy-start(bf16[64,1728]{1,0:T(8,128)(2,1)} %w1_ref.1) | copy-start | bytes 663556
  6.8 5.0 %collective-permute-start.1 = (bf16[64,2,4,128]{3,2,1,0:T(4,128)(2,1)S(1)}, bf16[64,2,4,128]{3,2,1,0:T(4,128)(2,1)S(1)}, u32[]{:S(2)}, u32[]{:S(2)}) collective-permute-start(bf16[64,2,4,128]{3,2,1,0:T(4,128)(2,1)S(1)} %collective-permute-done), channel_id=1, source_target_pairs={{4,0},{12,4},{0,8},{20,12},{8,16},{28,20},{16,24},{24,28},{5,1},{1... | collective-permute-start | bytes 393224 | tf_op jit(solution)/shard_map/ppermute | solution.py:307
  11.9 5.7 %collective-permute-start.2 = (bf16[384,256]{1,0:T(8,128)(2,1)S(1)}, bf16[384,256]{1,0:T(8,128)(2,1)S(1)}, u32[]{:S(2)}, u32[]{:S(2)}) collective-permute-start(bf16[384,256]{1,0:T(8,128)(2,1)S(1)} %get-tuple-element.28), channel_id=1, source_target_pairs={{0,1},{1,3},{2,0},{3,2},{4,5},{5,7},{6,4},{7,6},{8,9},{9,11},{10,8... | collective-permute-start | bytes 589832 | tf_op jit(solution)/shard_map/ppermute | solution.py:322
  13.2 4.3 %collective-permute-start.4 = (bf16[384,256]{1,0:T(8,128)(2,1)S(1)}, bf16[384,256]{1,0:T(8,128)(2,1)S(1)}, u32[]{:S(2)}, u32[]{:S(2)}) collective-permute-start(bf16[384,256]{1,0:T(8,128)(2,1)S(1)} %get-tuple-element.39), channel_id=1, source_target_pairs={{0,1},{1,0},{2,3},{3,2},{4,5},{5,4},{6,7},{7,6},{8,9},{9,8},{10,11... | collective-permute-start | bytes 589832 | tf_op jit(solution)/shard_map/ppermute | solution.py:336
  17.6 1.4 %collective-permute-start.3 = (bf16[384,256]{1,0:T(8,128)(2,1)S(1)}, bf16[384,256]{1,0:T(8,128)(2,1)S(1)}, u32[]{:S(2)}, u32[]{:S(2)}) collective-permute-start(bf16[384,256]{1,0:T(8,128)(2,1)S(1)} %collective-permute-done.2), channel_id=1, source_target_pairs={{0,1},{1,0},{2,3},{3,2},{4,5},{5,4},{6,7},{7,6},{8,9},{9,8},{10,11... | collective-permute-start | bytes 589832 | tf_op jit(solution)/shard_map/ppermute | solution.py:346
  20.4 4.0 %collective-permute-start.5 = (bf16[128,128]{1,0:T(8,128)(2,1)S(1)}, bf16[128,128]{1,0:T(8,128)(2,1)S(1)}, u32[]{:S(2)}, u32[]{:S(2)}) collective-permute-start(bf16[128,128]{1,0:T(8,128)(2,1)S(1)} %shard_map.71), channel_id=1, source_target_pairs={{0,4},{4,0},{8,12},{12,8},{16,20},{20,16},{24,28},{28,24},{1,5},{5... | collective-permute-start | bytes 98312 | tf_op jit(solution)/shard_map/ppermute | solution.py:364
  24.4 3.9 %collective-permute-start.6 = (bf16[128,128]{1,0:T(8,128)(2,1)S(1)}, bf16[128,128]{1,0:T(8,128)(2,1)S(1)}, u32[]{:S(2)}, u32[]{:S(2)}) collective-permute-start(bf16[128,128]{1,0:T(8,128)(2,1)S(1)} %collective-permute-done.5), channel_id=1, source_target_pairs={{4,0},{12,4},{0,8},{20,12},{8,16},{28,20},{16,24},{24,28},{5,1},{1... | collective-permute-start | bytes 98312 | tf_op jit(solution)/shard_map/ppermute | solution.py:365
  28.3 4.7 %collective-permute-start.7 = (bf16[1,3,128,128]{3,2,1,0:T(8,128)(2,1)S(1)}, bf16[1,3,128,128]{3,2,1,0:T(8,128)(2,1)S(1)}, u32[]{:S(2)}, u32[]{:S(2)}) collective-permute-start(bf16[1,3,128,128]{3,2,1,0:T(8,128)(2,1)S(1)} %get-tuple-element.44), channel_id=1, source_target_pairs={{0,2},{1,3},{2,0},{3,1},{4,6},{5,7},{6,4},{7,5},{8,10},{9,11},{10,... | collective-permute-start | bytes 294920 | tf_op jit(solution)/shard_map/ppermute | solution.py:369
  33.0 1.5 %collective-permute-start.8 = (bf16[2,3,128,128]{3,2,1,0:T(8,128)(2,1)S(1)}, bf16[2,3,128,128]{3,2,1,0:T(8,128)(2,1)S(1)}, u32[]{:S(2)}, u32[]{:S(2)}) collective-permute-start(bf16[2,3,128,128]{3,2,1,0:T(8,128)(2,1)S(1)} %maximum_bitcast_fusion.blocks_ref), channel_id=1, source_target_pairs={{0,1},{1,0},{2,3},{3,2},{4,5},{5,4},{6,7},{7,6},{8,9},{9,8},{10,11... | collective-permute-start | bytes 589832 | tf_op jit(solution)/shard_map/ppermute | solution.py:372

commit v5 on v4

--- a/solution.py
+++ b/solution.py
@@ -15,16 +15,33 @@
     return [(k, k ^ bit) for k in range(count)]
 
 
-def pair_relay(count):
+BOTH = ("wide", "narrow")
+
+
+def crossing(position, count):
+    target = position + 1 if position % 2 else position - 1
+    return target if 0 <= target < count else None
+
+
+def cross_wide(wide, narrow):
+    bit = 2 if narrow % 4 == 0 else 1
     steps = []
-    for k in range(count):
-        target = k - 2 if k % 2 == 0 else k + 2
-        steps.append((k, target if 0 <= target < count else k ^ 1))
+    for i in range(wide):
+        for j in range(narrow):
+            target = crossing(i, wide)
+            end = i * narrow + (j ^ bit) if target is None else target * narrow + j
+            steps.append((i * narrow + j, end))
     return steps
 
 
-def pair_relay_back(count):
-    return [(target, source) for source, target in pair_relay(count)]
+def cross_narrow(wide, narrow):
+    steps = []
+    for i in range(wide):
+        for j in range(narrow):
+            target = crossing(j, narrow)
+            end = (i ^ 1) * narrow + j if target is None else i * narrow + target
+            steps.append((i * narrow + j, end))
+    return steps
 
 
 def weights_kernel(wide, w1_ref, w2_ref, w3_ref, t1_ref, t2_ref, t3_ref):
@@ -213,30 +230,36 @@
     out_ref[...] = dot(jnp.concatenate([mine, rest], axis=1), pick).astype(jnp.bfloat16)
 
 
-def coarse_products(bit, blocks_ref, w3_ref, z_ref, slab):
+def coarse_products(places, blocks, w3_ref, z_ref, slab):
     i, j = lax.axis_index("wide"), lax.axis_index("narrow")
     i_odd = lax.rem(i, 2)
-    groups, _, c, lanes = blocks_ref.shape
     slots = (1, 2 - 2 * i_odd, 2 * i_odd)
-    for r in range(groups):
-        for k in range(3):
-            slab[pl.ds(pl.multiple_of(slots[k] * c, c), c), r * lanes : (r + 1) * lanes] = blocks_ref[
-                r, k
-            ]
-
+    at = 0
+    for ref in blocks:
+        for r in range(ref.shape[0]):
+            for k in range(3):
+                row = pl.multiple_of(slots[k] * ref.shape[2], ref.shape[2])
+                slab[pl.ds(row, ref.shape[2]), at : at + LANES] = ref[r, k]
+            at += LANES
     z = dot(w3_ref[...], slab[...])
-    for r in range(groups):
-        at = pl.multiple_of(jnp.bitwise_xor(j, 2 * r + bit) * lanes, lanes)
-        z_ref[:, pl.ds(at, lanes)] = z[:, r * lanes : (r + 1) * lanes]
-
-
-def coarse_first_kernel(blocks_ref, w3_ref, z_ref, slab):
-    coarse_products(0, blocks_ref, w3_ref, z_ref, slab)
-
-
-def coarse_kernel(blocks_ref, w3_ref, first_ref, out_ref, z_ref, slab):
-    del first_ref
-    coarse_products(1, blocks_ref, w3_ref, z_ref, slab)
+    for k, place in enumerate(places):
+        lane = pl.multiple_of(jnp.bitwise_xor(j, place) * LANES, LANES)
+        z_ref[:, pl.ds(lane, LANES)] = z[:, k * LANES : (k + 1) * LANES]
+
+
+def first_products_kernel(places, *refs):
+    *blocks, w3_ref, z_ref, slab = refs
+    coarse_products(places, blocks, w3_ref, z_ref, slab)
+
+
+def more_products_kernel(places, *refs):
+    *blocks, w3_ref, _, z_ref, slab = refs
+    coarse_products(places, blocks, w3_ref, z_ref, slab)
+
+
+def coarse_kernel(places, blocks_ref, w3_ref, before_ref, out_ref, z_ref, slab):
+    del before_ref
+    coarse_products(places, [blocks_ref], w3_ref, z_ref, slab)
     o, total = out_ref.shape
     width = LANES // 2
     count = total // LANES
@@ -289,6 +312,7 @@
             cost_estimate=cost(10**6, 10**6),
         )(block.reshape(rows, width), scale, shift)
 
+    far = lax.ppermute(stored_features, BOTH, cross_wide(wide, narrow))
     pair = lax.ppermute(stored_features, "wide", pair_swap(wide))
     t1, t2, t3 = pl.pallas_call(
         functools.partial(weights_kernel, wide),
@@ -302,10 +326,9 @@
         compiler_params=params,
         cost_estimate=cost(10**6, 4 * 10**6),
     )(first_weight, second_weight, third_weight)
-    pair, t1, t2, t3 = lax.optimization_barrier((pair, t1, t2, t3))
     own_slab = unpack(stored_features)
-    far = lax.ppermute(pair, "wide", pair_relay_back(wide))
     pair_slab = unpack(pair)
+    far, t1, t2, t3 = lax.optimization_barrier((far, t1, t2, t3))
     slab, relay, side = pl.pallas_call(
         functools.partial(slab_kernel, wide),
         out_shape=(
@@ -319,7 +342,7 @@
         compiler_params=params,
         cost_estimate=cost(10**6, 2 * 10**6),
     )(far.reshape(rows, width), scale, shift, own_slab, pair_slab)
-    passed = lax.ppermute(relay, "narrow", pair_relay(narrow))
+    crossed_rows = lax.ppermute(relay, BOTH, cross_narrow(wide, narrow))
     p1, hidden = pl.pallas_call(
         centre_kernel,
         out_shape=(
@@ -330,9 +353,8 @@
         out_specs=(VMEM,) * 2,
         scratch_shapes=[pltpu.VMEM((18 * c1, 4 * width), jnp.bfloat16)],
         compiler_params=params,
-        cost_estimate=cost(2 * 10**9, 4 * 10**6),
+        cost_estimate=cost(10**7, 10**5),
     )(slab, t1)
-    side, p1, hidden = lax.optimization_barrier((side, p1, hidden))
     partner_rows = lax.ppermute(side, "narrow", pair_swap(narrow))
     p2 = pl.pallas_call(
         second_kernel,
@@ -340,10 +362,8 @@
         in_specs=[VMEM] * 2,
         out_specs=VMEM,
         compiler_params=params,
-        cost_estimate=cost(10**9, 2 * 10**6),
+        cost_estimate=cost(10**7, 10**5),
     )(hidden, t2)
-    passed, p1, p2 = lax.optimization_barrier((passed, p1, p2))
-    relayed_rows = lax.ppermute(passed, "narrow", pair_swap(narrow))
 
     def add_side(kernel, out, rows, before):
         return pl.pallas_call(
@@ -356,42 +376,61 @@
                 pltpu.VMEM((12 * c1, 2 * width), jnp.bfloat16),
             ],
             compiler_params=params,
-            cost_estimate=cost(10**9, 4 * 10**6),
+            cost_estimate=cost(10**7, 10**5),
         )(rows, p1, before, t1, t2)
 
     p2 = add_side(partner_kernel, jax.ShapeDtypeStruct(p2.shape, p2.dtype), partner_rows, p2)
-    pooled = add_side(edge_kernel, jax.ShapeDtypeStruct((c2, LANES), jnp.bfloat16), relayed_rows, p2)
+    pooled = add_side(edge_kernel, jax.ShapeDtypeStruct((c2, LANES), jnp.bfloat16), crossed_rows, p2)
+    pooled_far = lax.ppermute(pooled, BOTH, cross_wide(wide, narrow))
     pooled_pair = lax.ppermute(pooled, "wide", pair_swap(wide))
-    pooled_far = lax.ppermute(pooled_pair, "wide", pair_relay_back(wide))
     mine = jnp.stack([pooled, pooled_pair, pooled_far])[None]
+    held, held_places = mine, [0]
+    arrivals = [(mine, [0]), (lax.ppermute(mine, "narrow", pair_swap(narrow)), [1])]
     bit = narrow // 2
     while bit > 1:
-        other = lax.ppermute(mine, "narrow", pair_swap(narrow, bit))
-        mine = jnp.stack([mine, other], axis=1).reshape((-1,) + mine.shape[1:])
+        other = lax.ppermute(held, "narrow", pair_swap(narrow, bit))
+        places = [place ^ bit for place in held_places]
+        arrivals.append((other, places))
+        arrivals.append(
+            (lax.ppermute(other, "narrow", pair_swap(narrow)), [place ^ 1 for place in places])
+        )
+        if bit > 2:
+            held = jnp.concatenate([held, other])
+        held_places = held_places + places
         bit //= 2
-    theirs = lax.ppermute(mine, "narrow", pair_swap(narrow))
     total = narrow * LANES
     products = jax.ShapeDtypeStruct((9 * o3, total), jnp.float32)
-    scratch = [pltpu.VMEM((3 * c2, total // 2), jnp.bfloat16)]
-    first = pl.pallas_call(
-        coarse_first_kernel,
-        out_shape=products,
-        in_specs=[VMEM] * 2,
-        out_specs=VMEM,
-        scratch_shapes=scratch,
-        compiler_params=params,
-        cost_estimate=cost(10**9, 10**6),
-    )(mine, t3)
-    coarse, _ = pl.pallas_call(
-        coarse_kernel,
-        out_shape=(jax.ShapeDtypeStruct((o3, total), jnp.bfloat16), products),
-        in_specs=[VMEM] * 3,
-        out_specs=(VMEM,) * 2,
-        scratch_shapes=scratch,
-        input_output_aliases={2: 1},
-        compiler_params=params,
-        cost_estimate=cost(10**9, 10**6),
-    )(theirs, t3, first)
+    z = None
+    for group in (arrivals[:2], arrivals[2:-1], arrivals[-1:]):
+        if not group:
+            continue
+        places = [place for _, several in group for place in several]
+        operands = [array for array, _ in group] + [t3] + ([] if z is None else [z])
+        scratch = [pltpu.VMEM((3 * c2, len(places) * LANES), jnp.bfloat16)]
+        common = dict(
+            in_specs=[VMEM] * len(operands),
+            scratch_shapes=scratch,
+            compiler_params=params,
+            cost_estimate=cost(10**7, 10**5),
+        )
+        if group[-1] is not arrivals[-1]:
+            z = pl.pallas_call(
+                functools.partial(
+                    first_products_kernel if z is None else more_products_kernel, places
+                ),
+                out_shape=products,
+                out_specs=VMEM,
+                input_output_aliases={} if z is None else {len(operands) - 1: 0},
+                **common,
+            )(*operands)
+        else:
+            coarse, _ = pl.pallas_call(
+                functools.partial(coarse_kernel, places),
+                out_shape=(jax.ShapeDtypeStruct((o3, total), jnp.bfloat16), products),
+                out_specs=(VMEM,) * 2,
+                input_output_aliases={len(operands) - 1: 1},
+                **common,
+            )(*operands)
     return coarse[:, None, :]
 
 

time: 36 us -> 29.5 us (0.82)
  waiting for transfers between devices: 17.9 us -> 7.1 us
  starting transfers between devices: 8.7 us -> 11.6 us
  local copies, waits for them, and re-layouts: 2.16 us -> 3.43 us
    ppermute x6, waiting for transfers between devices: 14.6 us -> 5.22 us  [the longest x1 3.7 us: body(): other = lax.ppermute(held, 'narrow', pair_swap(narrow, bit))]
    ppermute x6, starting transfers between devices: 3.76 us -> 5.55 us  [the longest x1 2.44 us: body(): crossed_rows = lax.ppermute(relay, BOTH, cross_narrow(wide, narrow))]
    unnamed x11, local copies, waits for them, and re-layouts: 2.16 us -> 3.43 us
    ppermute x1, starting transfers between devices: 1.83 us -> 2.98 us  [body(): pooled_pair = lax.ppermute(pooled, 'wide', pair_swap(wide))]
    ppermute x1, waiting for transfers between devices: 1.09 us -> 0.36 us  [body(): pair = lax.ppermute(stored_features, 'wide', pair_swap(wide))]
    ppermute x1, waiting for transfers between devices: 2.18 us -> 1.52 us  [body(): pooled_pair = lax.ppermute(pooled, 'wide', pair_swap(wide))]
    pallas_call x2 -> x3, Pallas kernels: 1.63 us -> 1.83 us  [the longest x1 1.16 us: body(): pl.pallas_call(functools.partial(coarse_kernel, places), out_shape=(jax.S...]
  transfers between devices with their start and end apart: 9 -> 9, of which waited for: 8 -> 6; matrix products, arithmetic and copies ran while one was open for 3% -> 4% of each run, Pallas kernels for 12% -> 15%
where the time goes in v5:
time: 29.5 us; the launch traced here: 29.3 us
  starting transfers between devices  11.6 us (39%)
  Pallas kernels  7.11 us (24%)
  waiting for transfers between devices  7.1 us (24%)
  local copies, waits for them, and re-layouts  3.43 us (12%)
    ppermute x1, waiting for transfers between devices, body(): other = lax.ppermute(held, 'narrow', pair_swap(narrow, bit))  3.7 us
    unnamed x11, local copies, waits for them, and re-layouts  3.43 us
    ppermute x1, starting transfers between devices, body(): pooled_pair = lax.ppermute(pooled, 'wide', pair_swap(wide))  2.98 us
    ppermute x1, starting transfers between devices, body(): pair = lax.ppermute(stored_features, 'wide', pair_swap(wide))  2.97 us
    pallas_call x2, Pallas kernels, add_side(): pl.pallas_call(functools.partial(kernel, narrow), out_shape=out, in_specs...  2.65 us
    ppermute x1, starting transfers between devices, body(): crossed_rows = lax.ppermute(relay, BOTH, cross_narrow(wide, narrow))  2.44 us
    ppermute x1, waiting for transfers between devices, body(): pooled_pair = lax.ppermute(pooled, 'wide', pair_swap(wide))  1.52 us
    ppermute x1, starting transfers between devices, body(): far = lax.ppermute(stored_features, BOTH, cross_wide(wide, narrow))  1.49 us
  transfers between devices with their start and end apart: 9, of which 6 were waited for; matrix products, arithmetic and copies ran while one was open for 4% of the time, Pallas kernels for 15%

profile of v5, /device:TPU:0, one launch (start us, length us, event | category | flops | bytes accessed | tf_op | source)
XLA Modules:
  0.0 29.3 jit_solution(169053342960151968)
XLA Ops:
  0.0 0.0 copy-start
  0.0 0.0 copy-start.1
  0.0 3.0 %collective-permute-start.1 = (bf16[64,2,4,128]{3,2,1,0:T(4,128)(2,1)}, bf16[64,2,4,128]{3,2,1,0:T(4,128)(2,1)S(1)}, u32[]{:S(2)}, u32[]{:S(2)}) collective-permute-start(bf16[64,2,4,128]{3,2,1,0:T(4,128)(2,1)} %param.6), channel_id=1, source_target_pairs={{0,4},{4,0},{8,12},{12,8},{16,20},{20,16},{24,28},{28,24},{1,5},{5... | collective-permute-start | bytes 393224 | tf_op jit(solution)/shard_map/ppermute | solution.py:316
  3.0 1.5 %collective-permute-start = (bf16[64,2,4,128]{3,2,1,0:T(4,128)(2,1)}, bf16[64,2,4,128]{3,2,1,0:T(4,128)(2,1)S(1)}, u32[]{:S(2)}, u32[]{:S(2)}) collective-permute-start(bf16[64,2,4,128]{3,2,1,0:T(4,128)(2,1)} %param.6), channel_id=1, source_target_pairs={{0,2},{1,3},{2,0},{3,1},{4,8},{5,9},{6,10},{7,11},{8,4},{9,5},{10,... | collective-permute-start | bytes 393224 | tf_op jit(solution)/shard_map/ppermute | solution.py:315
  4.5 1.2 %copy.9.w2_ref = bf16[128,1728]{1,0:T(8,128)(2,1)S(1)} copy(bf16[128,1728]{0,1:T(8,128)(2,1)} %param.10) | data formatting | bytes 884736 | tf_op args[4]
  5.7 0.0 copy-start.2
  5.7 0.9 %copy-done.2 = bf16[64,2,4,128]{3,2,1,0:T(4,128)(2,1)S(1)} copy-done((bf16[64,2,4,128]{3,2,1,0:T(4,128)(2,1)S(1)}, bf16[64,2,4,128]{3,2,1,0:T(4,128)(2,1)}, u32[]{:S(2)}) %copy-start.2) | copy-done | bytes 131096
  6.6 0.0 copy-start.3
  6.6 0.7 %copy-done.3 = f32[64]{0:T(128)S(1)} copy-done((f32[64]{0:T(128)S(1)}, f32[64]{0:T(128)}, u32[]{:S(2)}) %copy-start.3) | copy-done | bytes 280
  7.2 0.0 copy-start.4
  7.2 0.7 %copy-done.4 = f32[64]{0:T(128)S(1)} copy-done((f32[64]{0:T(128)S(1)}, f32[64]{0:T(128)}, u32[]{:S(2)}) %copy-start.4) | copy-done | bytes 280
  7.9 0.1 shard_map.65.own_ref
  8.0 0.0 copy-done
  8.0 0.0 copy-done.1
  8.0 0.4 %shard_map.64 = (bf16[256,3456]{1,0:T(8,128)(2,1)S(1)}, bf16[256,2304]{1,0:T(8,128)(2,1)S(1)}, bf16[576,384]{1,0:T(8,128)(2,1)S(1)}) custom-call(bf16[64,1728]{1,0:T(8,128)(2,1)S(1)} %copy-done.1, bf16[128,1728]{1,0:T(8,128)(2,1)S(1)} %copy.9.w2_ref, bf16[64,3456]{1,0:T(8,128)(2,1)S(1)} %copy-done), custom_call_target="tpu_custom_call" | custom-call | flops 1000000 | bytes 4000000 | tf_op jit(solution)/shard_map/pallas_call | solution.py:317
  8.5 0.4 %collective-permute-done.1 = bf16[64,2,4,128]{3,2,1,0:T(4,128)(2,1)S(1)} collective-permute-done((bf16[64,2,4,128]{3,2,1,0:T(4,128)(2,1)}, bf16[64,2,4,128]{3,2,1,0:T(4,128)(2,1)S(1)}, u32[]{:S(2)}, u32[]{:S(2)}) %collective-permute-start.1) | collective-permute-done | bytes 131104 | tf_op jit(solution)/shard_map/ppermute | solution.py:316
  8.9 0.1 shard_map.66.pair_ref
  9.0 0.0 collective-permute-done
  9.0 0.2 shard_map.67
  9.1 0.1 collective-permute-start.3
  9.2 2.4 %collective-permute-start.2 = (bf16[384,256]{1,0:T(8,128)(2,1)S(1)}, bf16[384,256]{1,0:T(8,128)(2,1)S(1)}, u32[]{:S(2)}, u32[]{:S(2)}) collective-permute-start(bf16[384,256]{1,0:T(8,128)(2,1)S(1)} %get-tuple-element.22), channel_id=1, source_target_pairs={{0,4},{1,2},{2,1},{3,7},{4,0},{5,6},{6,5},{7,3},{8,12},{9,10},{10,... | collective-permute-start | bytes 589832 | tf_op jit(solution)/shard_map/ppermute | solution.py:345
  11.7 1.3 %shard_map.68 = (f32[256,512]{1,0:T(8,128)S(1)}, bf16[768,256]{1,0:T(8,128)(2,1)S(1)}) custom-call(bf16[384,512]{1,0:T(8,128)(2,1)S(1)} %get-tuple-element.23.x_ref, bf16[256,3456]{1,0:T(8,128)(2,1)S(1)} %get-tuple-element.24.w1_ref), custom_call_target="tpu_custom_call" | custom-call | flops 10000000 | bytes 100000 | tf_op jit(solution)/shard_map/pallas_call | solution.py:346
  13.0 0.5 %shard_map.69.p2_ref = f32[256,512]{1,0:T(8,128)S(1)} custom-call(bf16[768,256]{1,0:T(8,128)(2,1)S(1)} %get-tuple-element.27.hidden_ref, bf16[256,2304]{1,0:T(8,128)(2,1)S(1)} %get-tuple-element.28.w2_ref), custom_call_target="tpu_custom_call" | custom-call | flops 10000000 | bytes 100000 | tf_op jit(solution)/shard_map/pallas_call | solution.py:359
  13.5 0.0 collective-permute-done.3.rows_ref
  13.5 1.3 %shard_map.70.p2_ref = f32[256,512]{1,0:T(8,128)S(1)} custom-call(bf16[384,256]{1,0:T(8,128)(2,1)S(1)} %collective-permute-done.3.rows_ref, f32[256,512]{1,0:T(8,128)S(1)} %get-tuple-element.25.p1_ref, f32[256,512]{1,0:T(8,128)S(1)} %shard_map.69.p2_ref, bf16[256,3456]{1,0:T(8,128)(2,1)S(1)} %get-tuple-element.24.w1_ref, ...), custom_call_target="tpu_custom_call" | custom-call | flops 10000000 | bytes 100000 | tf_op jit(solution)/shard_map/pallas_call | solution.py:369
  14.8 0.5 %collective-permute-done.2.rows_ref = bf16[384,256]{1,0:T(8,128)(2,1)S(1)} collective-permute-done((bf16[384,256]{1,0:T(8,128)(2,1)S(1)}, bf16[384,256]{1,0:T(8,128)(2,1)S(1)}, u32[]{:S(2)}, u32[]{:S(2)}) %collective-permute-start.2) | collective-permute-done | bytes 196640 | tf_op jit(solution)/shard_map/ppermute | solution.py:345
  15.3 1.4 %shard_map.71 = bf16[128,128]{1,0:T(8,128)(2,1)S(1)} custom-call(bf16[384,256]{1,0:T(8,128)(2,1)S(1)} %collective-permute-done.2.rows_ref, f32[256,512]{1,0:T(8,128)S(1)} %get-tuple-element.25.p1_ref, f32[256,512]{1,0:T(8,128)S(1)} %shard_map.70.p2_ref, bf16[256,3456]{1,0:T(8,128)(2,1)S(1)} %get-tuple-element.24.w1_ref, ...), custom_call_target="tpu_custom_call" | custom-call | flops 10000000 | bytes 100000 | tf_op jit(solution)/shard_map/pallas_call | solution.py:369
  16.7 0.6 %collective-permute-start.5 = (bf16[128,128]{1,0:T(8,128)(2,1)S(1)}, bf16[128,128]{1,0:T(8,128)(2,1)S(1)}, u32[]{:S(2)}, u32[]{:S(2)}) collective-permute-start(bf16[128,128]{1,0:T(8,128)(2,1)S(1)} %shard_map.71), channel_id=1, source_target_pairs={{0,2},{1,3},{2,0},{3,1},{4,8},{5,9},{6,10},{7,11},{8,4},{9,5},{10,... | collective-permute-start | bytes 98312 | tf_op jit(solution)/shard_map/ppermute | solution.py:384
  17.3 3.0 %collective-permute-start.4 = (bf16[128,128]{1,0:T(8,128)(2,1)S(1)}, bf16[128,128]{1,0:T(8,128)(2,1)S(1)}, u32[]{:S(2)}, u32[]{:S(2)}) collective-permute-start(bf16[128,128]{1,0:T(8,128)(2,1)S(1)} %shard_map.71), channel_id=1, source_target_pairs={{0,4},{4,0},{8,12},{12,8},{16,20},{20,16},{24,28},{28,24},{1,5},{5... | collective-permute-start | bytes 98312 | tf_op jit(solution)/shard_map/ppermute | solution.py:385
  20.3 0.4 %collective-permute-done.5 = bf16[128,128]{1,0:T(8,128)(2,1)S(1)} collective-permute-done((bf16[128,128]{1,0:T(8,128)(2,1)S(1)}, bf16[128,128]{1,0:T(8,128)(2,1)S(1)}, u32[]{:S(2)}, u32[]{:S(2)}) %collective-permute-start.5) | collective-permute-done | bytes 32800 | tf_op jit(solution)/shard_map/ppermute | solution.py:384
  20.7 1.5 %collective-permute-done.4 = bf16[128,128]{1,0:T(8,128)(2,1)S(1)} collective-permute-done((bf16[128,128]{1,0:T(8,128)(2,1)S(1)}, bf16[128,128]{1,0:T(8,128)(2,1)S(1)}, u32[]{:S(2)}, u32[]{:S(2)}) %collective-permute-start.4) | collective-permute-done | bytes 32800 | tf_op jit(solution)/shard_map/ppermute | solution.py:385
  22.2 1.0 %collective-permute-start.6 = (bf16[1,3,128,128]{3,2,1,0:T(8,128)(2,1)S(1)}, bf16[1,3,128,128]{3,2,1,0:T(8,128)(2,1)S(1)}, u32[]{:S(2)}, u32[]{:S(2)}) collective-permute-start(bf16[1,3,128,128]{3,2,1,0:T(8,128)(2,1)S(1)} %maximum_bitcast_fusion.refs_0_), channel_id=1, source_target_pairs={{0,2},{1,3},{2,0},{3,1},{4,6},{5,7},{6,4},{7,5},{8,10},{9,11},{10,... | collective-permute-start | bytes 294920 | tf_op jit(solution)/shard_map/ppermute | solution.py:391
  23.2 0.0 collective-permute-start.8
  23.2 3.7 %collective-permute-done.6.refs_0_ = bf16[1,3,128,128]{3,2,1,0:T(8,128)(2,1)S(1)} collective-permute-done((bf16[1,3,128,128]{3,2,1,0:T(8,128)(2,1)S(1)}, bf16[1,3,128,128]{3,2,1,0:T(8,128)(2,1)S(1)}, u32[]{:S(2)}, u32[]{:S(2)}) %collective-permute-start.6) | collective-permute-done | bytes 98336 | tf_op jit(solution)/shard_map/ppermute | solution.py:391
  26.9 0.0 collective-permute-start.7
  26.9 0.0 collective-permute-done.8.refs_1_
  26.9 0.4 %shard_map.72.refs_2_ = f32[576,512]{1,0:T(8,128)S(1)} custom-call(bf16[1,3,128,128]{3,2,1,0:T(8,128)(2,1)S(1)} %maximum_bitcast_fusion.refs_0_, bf16[1,3,128,128]{3,2,1,0:T(8,128)(2,1)S(1)} %collective-permute-done.8.refs_1_, bf16[576,384]{1,0:T(8,128)(2,1)S(1)} %get-tuple-element.29.refs_2_.refs_1_.w3_ref), custom_call_target="tpu_custom_call" | custom-call | flops 10000000 | bytes 100000 | tf_op jit(solution)/shard_map/pallas_call | solution.py:417
  27.3 0.3 %shard_map.73.before_ref = f32[576,512]{1,0:T(8,128)S(1)} custom-call(bf16[1,3,128,128]{3,2,1,0:T(8,128)(2,1)S(1)} %collective-permute-done.6.refs_0_, bf16[576,384]{1,0:T(8,128)(2,1)S(1)} %get-tuple-element.29.refs_2_.refs_1_.w3_ref, f32[576,512]{1,0:T(8,128)S(1)} %shard_map.72.refs_2_), custom_call_target="tpu_custom_call", output_to_operand_aliasing={{}: (2, {})} | custom-call | flops 10000000 | bytes 100000 | tf_op jit(solution)/shard_map/pallas_call | solution.py:417
  27.6 0.6 %collective-permute-done.7.blocks_ref = bf16[1,3,128,128]{3,2,1,0:T(8,128)(2,1)S(1)} collective-permute-done((bf16[1,3,128,128]{3,2,1,0:T(8,128)(2,1)S(1)}, bf16[1,3,128,128]{3,2,1,0:T(8,128)(2,1)S(1)}, u32[]{:S(2)}, u32[]{:S(2)}) %collective-permute-start.7) | collective-permute-done | bytes 98336 | tf_op jit(solution)/shard_map/ppermute | solution.py:395
  28.2 1.2 %shard_map.74 = (bf16[64,512]{1,0:T(8,128)(2,1)}, f32[576,512]{1,0:T(8,128)S(1)}) custom-call(bf16[1,3,128,128]{3,2,1,0:T(8,128)(2,1)S(1)} %collective-permute-done.7.blocks_ref, bf16[576,384]{1,0:T(8,128)(2,1)S(1)} %get-tuple-element.29.refs_2_.refs_1_.w3_ref, f32[576,512]{1,0:T(8,128)S(1)} %shard_map.73.before_ref), custom_call_target="tpu_custom_call", output_to_operand_aliasing={{1}: (2, {})} | custom-call | flops 10000000 | bytes 100000 | tf_op jit(solution)/shard_map/pallas_call | solution.py:427
  (1 shorter events, 0.0 us)
Async XLA Ops:
  0.0 8.0 %copy-start = (bf16[64,3456]{1,0:T(8,128)(2,1)S(1)}, bf16[64,3456]{1,0:T(8,128)(2,1)}, u32[]{:S(2)}) copy-start(bf16[64,3456]{1,0:T(8,128)(2,1)} %w3_ref.1) | copy-start | bytes 1327108
  0.0 8.0 %copy-start.1 = (bf16[64,1728]{1,0:T(8,128)(2,1)S(1)}, bf16[64,1728]{1,0:T(8,128)(2,1)}, u32[]{:S(2)}) copy-start(bf16[64,1728]{1,0:T(8,128)(2,1)} %w1_ref.1) | copy-start | bytes 663556
  0.0 8.8 %collective-permute-start.1 = (bf16[64,2,4,128]{3,2,1,0:T(4,128)(2,1)}, bf16[64,2,4,128]{3,2,1,0:T(4,128)(2,1)S(1)}, u32[]{:S(2)}, u32[]{:S(2)}) collective-permute-start(bf16[64,2,4,128]{3,2,1,0:T(4,128)(2,1)} %param.6), channel_id=1, source_target_pairs={{0,4},{4,0},{8,12},{12,8},{16,20},{20,16},{24,28},{28,24},{1,5},{5... | collective-permute-start | bytes 393224 | tf_op jit(solution)/shard_map/ppermute | solution.py:316
  3.0 6.0 %collective-permute-start = (bf16[64,2,4,128]{3,2,1,0:T(4,128)(2,1)}, bf16[64,2,4,128]{3,2,1,0:T(4,128)(2,1)S(1)}, u32[]{:S(2)}, u32[]{:S(2)}) collective-permute-start(bf16[64,2,4,128]{3,2,1,0:T(4,128)(2,1)} %param.6), channel_id=1, source_target_pairs={{0,2},{1,3},{2,0},{3,1},{4,8},{5,9},{6,10},{7,11},{8,4},{9,5},{10,... | collective-permute-start | bytes 393224 | tf_op jit(solution)/shard_map/ppermute | solution.py:315
  5.7 0.9 %copy-start.2 = (bf16[64,2,4,128]{3,2,1,0:T(4,128)(2,1)S(1)}, bf16[64,2,4,128]{3,2,1,0:T(4,128)(2,1)}, u32[]{:S(2)}) copy-start(bf16[64,2,4,128]{3,2,1,0:T(4,128)(2,1)} %param.6) | copy-start | bytes 393220
  6.6 0.7 %copy-start.3 = (f32[64]{0:T(128)S(1)}, f32[64]{0:T(128)}, u32[]{:S(2)}) copy-start(f32[64]{0:T(128)} %param.7) | copy-start | bytes 772
  7.2 0.7 %copy-start.4 = (f32[64]{0:T(128)S(1)}, f32[64]{0:T(128)}, u32[]{:S(2)}) copy-start(f32[64]{0:T(128)} %param.8) | copy-start | bytes 772
  9.1 4.3 %collective-permute-start.3 = (bf16[384,256]{1,0:T(8,128)(2,1)S(1)}, bf16[384,256]{1,0:T(8,128)(2,1)S(1)}, u32[]{:S(2)}, u32[]{:S(2)}) collective-permute-start(bf16[384,256]{1,0:T(8,128)(2,1)S(1)} %get-tuple-element.26), channel_id=1, source_target_pairs={{0,1},{1,0},{2,3},{3,2},{4,5},{5,4},{6,7},{7,6},{8,9},{9,8},{10,11... | collective-permute-start | bytes 589832 | tf_op jit(solution)/shard_map/ppermute | solution.py:358
  9.2 6.1 %collective-permute-start.2 = (bf16[384,256]{1,0:T(8,128)(2,1)S(1)}, bf16[384,256]{1,0:T(8,128)(2,1)S(1)}, u32[]{:S(2)}, u32[]{:S(2)}) collective-permute-start(bf16[384,256]{1,0:T(8,128)(2,1)S(1)} %get-tuple-element.22), channel_id=1, source_target_pairs={{0,4},{1,2},{2,1},{3,7},{4,0},{5,6},{6,5},{7,3},{8,12},{9,10},{10,... | collective-permute-start | bytes 589832 | tf_op jit(solution)/shard_map/ppermute | solution.py:345
  16.7 4.0 %collective-permute-start.5 = (bf16[128,128]{1,0:T(8,128)(2,1)S(1)}, bf16[128,128]{1,0:T(8,128)(2,1)S(1)}, u32[]{:S(2)}, u32[]{:S(2)}) collective-permute-start(bf16[128,128]{1,0:T(8,128)(2,1)S(1)} %shard_map.71), channel_id=1, source_target_pairs={{0,2},{1,3},{2,0},{3,1},{4,8},{5,9},{6,10},{7,11},{8,4},{9,5},{10,... | collective-permute-start | bytes 98312 | tf_op jit(solution)/shard_map/ppermute | solution.py:384
  17.3 4.9 %collective-permute-start.4 = (bf16[128,128]{1,0:T(8,128)(2,1)S(1)}, bf16[128,128]{1,0:T(8,128)(2,1)S(1)}, u32[]{:S(2)}, u32[]{:S(2)}) collective-permute-start(bf16[128,128]{1,0:T(8,128)(2,1)S(1)} %shard_map.71), channel_id=1, source_target_pairs={{0,4},{4,0},{8,12},{12,8},{16,20},{20,16},{24,28},{28,24},{1,5},{5... | collective-permute-start | bytes 98312 | tf_op jit(solution)/shard_map/ppermute | solution.py:385
  22.2 4.7 %collective-permute-start.6 = (bf16[1,3,128,128]{3,2,1,0:T(8,128)(2,1)S(1)}, bf16[1,3,128,128]{3,2,1,0:T(8,128)(2,1)S(1)}, u32[]{:S(2)}, u32[]{:S(2)}) collective-permute-start(bf16[1,3,128,128]{3,2,1,0:T(8,128)(2,1)S(1)} %maximum_bitcast_fusion.refs_0_), channel_id=1, source_target_pairs={{0,2},{1,3},{2,0},{3,1},{4,6},{5,7},{6,4},{7,5},{8,10},{9,11},{10,... | collective-permute-start | bytes 294920 | tf_op jit(solution)/shard_map/ppermute | solution.py:391
  23.2 3.7 %collective-permute-start.8 = (bf16[1,3,128,128]{3,2,1,0:T(8,128)(2,1)S(1)}, bf16[1,3,128,128]{3,2,1,0:T(8,128)(2,1)S(1)}, u32[]{:S(2)}, u32[]{:S(2)}) collective-permute-start(bf16[1,3,128,128]{3,2,1,0:T(8,128)(2,1)S(1)} %maximum_bitcast_fusion.refs_0_), channel_id=1, source_target_pairs={{0,1},{1,0},{2,3},{3,2},{4,5},{5,4},{6,7},{7,6},{8,9},{9,8},{10,11... | collective-permute-start | bytes 294920 | tf_op jit(solution)/shard_map/ppermute | solution.py:388
  26.9 1.3 %collective-permute-start.7 = (bf16[1,3,128,128]{3,2,1,0:T(8,128)(2,1)S(1)}, bf16[1,3,128,128]{3,2,1,0:T(8,128)(2,1)S(1)}, u32[]{:S(2)}, u32[]{:S(2)}) collective-permute-start(bf16[1,3,128,128]{3,2,1,0:T(8,128)(2,1)S(1)} %collective-permute-done.6.refs_0_), channel_id=1, source_target_pairs={{0,1},{1,0},{2,3},{3,2},{4,5},{5,4},{6,7},{7,6},{8,9},{9,8},{10,11... | collective-permute-start | bytes 294920 | tf_op jit(solution)/shard_map/ppermute | solution.py:395

commit v6 on v5

--- a/solution.py
+++ b/solution.py
@@ -34,12 +34,15 @@
     return steps
 
 
-def cross_narrow(wide, narrow):
+def cross_narrow(wide, narrow, ends_meet):
     steps = []
     for i in range(wide):
         for j in range(narrow):
             target = crossing(j, narrow)
-            end = (i ^ 1) * narrow + j if target is None else i * narrow + target
+            if target is None:
+                end = i * narrow + narrow - 1 - j if ends_meet else (i ^ 1) * narrow + j
+            else:
+                end = i * narrow + target
             steps.append((i * narrow + j, end))
     return steps
 
@@ -130,7 +133,9 @@
     out_ref[block : 2 * block, :] = own_ref[...]
     out_ref[pl.ds(pair_row, block), :] = pair_ref[...]
     half = columns // 2
-    relay_ref[...] = out_ref[:, pl.ds(pl.multiple_of(j_odd * half, half), half)]
+    lane = pl.multiple_of(j_odd * half, half)
+    relay_ref[:block, :] = out_ref[:block, pl.ds(lane, half)]
+    relay_ref[block:, :] = out_ref[2 * block :, pl.ds(lane, half)]
     side_ref[...] = out_ref[:, pl.ds(pl.multiple_of((1 - j_odd) * half, half), half)]
 
 
@@ -180,38 +185,57 @@
     p2_ref[:, 3 * LANES :] = q1[:, LANES:] + q0[:, :LANES]
 
 
-def side_terms(high, keep, rows_ref, p1_ref, w1_ref, w2_ref, taps, hidden):
+def stacked(value):
+    return jnp.concatenate([part.astype(jnp.bfloat16) for part in shifted(value)], axis=0)
+
+
+def side_terms(high, keep, feature, p1_ref, w1_ref, w2_ref):
     span1, span2 = w1_ref.shape[1] // 3, w2_ref.shape[1] // 3
     outer1, outer2 = pl.multiple_of(2 * high * span1, LANES), pl.multiple_of(2 * high * span2, LANES)
-    for k in range(2):
-        at = pl.multiple_of((k + high * (1 - 2 * k)) * LANES, LANES)
-        value = rows_ref[:, k * LANES : (k + 1) * LANES].astype(jnp.float32)
-        spread(value if keep is None else value * keep, taps, at)
-    r = dot(w1_ref[:, pl.ds(outer1, span1)], taps[...])
-    r1 = dot(w1_ref[:, span1 : 2 * span1], taps[:, LANES:])
+    taps = jnp.concatenate([stacked(feature(k)) for k in range(2)], axis=1)
+    r = dot(w1_ref[:, pl.ds(outer1, span1)], taps)
+    r1 = dot(w1_ref[:, span1 : 2 * span1], taps)
+    up = high == 1
     before = p1_ref[:, pl.ds(pl.multiple_of(high * 2 * LANES, LANES), 2 * LANES)]
-    end = jnp.maximum(r[:, :LANES] + r1 + before[:, :LANES], 0.0)
-    spread(end if keep is None else end * keep, hidden, 0)
-    spread(jnp.maximum(r[:, LANES:] + before[:, LANES:], 0.0), hidden, LANES)
-    q = dot(w2_ref[:, pl.ds(outer2, span2)], hidden[...])
-    q1 = dot(w2_ref[:, span2 : 2 * span2], hidden[:, LANES:])
+    end = jnp.where(up, r[:, LANES:] + r1[:, :LANES], r[:, :LANES] + r1[:, LANES:])
+    end = jnp.maximum(end + before[:, :LANES], 0.0)
+    end = stacked(end if keep is None else end * keep)
+    near = jnp.where(up, r[:, :LANES], r[:, LANES:])
+    near = stacked(jnp.maximum(near + before[:, LANES:], 0.0))
+    q = dot(w2_ref[:, pl.ds(outer2, span2)], jnp.concatenate([end, near], axis=1))
+    q1 = dot(w2_ref[:, span2 : 2 * span2], near)
     return q[:, :LANES] + q1, q[:, LANES:]
 
 
-def partner_kernel(narrow, rows_ref, p1_ref, p2_ref, w1_ref, w2_ref, out_ref, taps, hidden):
+def partner_kernel(rows_ref, p1_ref, p2_ref, w1_ref, w2_ref, out_ref):
     high = 1 - lax.rem(lax.axis_index("narrow"), 2)
-    end, near = side_terms(high, None, rows_ref, p1_ref, w1_ref, w2_ref, taps, hidden)
+
+    def feature(k):
+        return rows_ref[:, k * LANES : (k + 1) * LANES].astype(jnp.float32)
+
+    end, near = side_terms(high, None, feature, p1_ref, w1_ref, w2_ref)
     at = pl.multiple_of(high * 2 * LANES, LANES)
     out_ref[...] = p2_ref[...]
     out_ref[:, pl.ds(at, LANES)] += end
     out_ref[:, pl.ds(at + LANES, LANES)] += near
 
 
-def edge_kernel(narrow, rows_ref, p1_ref, p2_ref, w1_ref, w2_ref, out_ref, taps, hidden):
+def edge_kernel(
+    narrow, own_ref, rows_ref, scale_ref, shift_ref, p1_ref, p2_ref, w1_ref, w2_ref, out_ref, staged
+):
     j = lax.axis_index("narrow")
     high = lax.rem(j, 2)
     keep = jnp.where(j == high * (narrow - 1), 0.0, 1.0)
-    end, near = side_terms(high, keep, rows_ref, p1_ref, w1_ref, w2_ref, taps, hidden)
+    staged[...] = own_ref[...].astype(jnp.float32)
+    scale, shift = column(scale_ref) * keep, column(shift_ref) * keep
+    c = scale.shape[0]
+
+    def feature(k):
+        rows = rows_ref[:, k * LANES : (k + 1) * LANES].astype(jnp.float32) * keep
+        own = [staged[pl.ds(2 * d + k, c, stride=4), :] * scale + shift for d in range(2)]
+        return jnp.concatenate([rows[: 2 * c]] + own + [rows[2 * c :]], axis=0)
+
+    end, near = side_terms(high, keep, feature, p1_ref, w1_ref, w2_ref)
     c2 = out_ref.shape[0]
     at = pl.multiple_of(high * 2 * LANES, LANES)
     other = pl.multiple_of((1 - high) * 2 * LANES, LANES)
@@ -326,14 +350,22 @@
         compiler_params=params,
         cost_estimate=cost(10**6, 4 * 10**6),
     )(first_weight, second_weight, third_weight)
-    own_slab = unpack(stored_features)
+    half = height // 2
+    edges = jnp.where(
+        lax.axis_index("narrow") % 2 == 1,
+        stored_features[:, :, half:],
+        stored_features[:, :, :half],
+    )
+    crossed_own = lax.ppermute(edges, BOTH, cross_narrow(wide, narrow, True))
+    pair, raw, scale, shift = lax.optimization_barrier((pair, stored_features, scale, shift))
+    own_slab = unpack(raw)
     pair_slab = unpack(pair)
-    far, t1, t2, t3 = lax.optimization_barrier((far, t1, t2, t3))
+    far, pair_slab, t1, t2, t3 = lax.optimization_barrier((far, pair_slab, t1, t2, t3))
     slab, relay, side = pl.pallas_call(
         functools.partial(slab_kernel, wide),
         out_shape=(
             jax.ShapeDtypeStruct((6 * c1, columns), jnp.bfloat16),
-            jax.ShapeDtypeStruct((6 * c1, columns // 2), jnp.bfloat16),
+            jax.ShapeDtypeStruct((4 * c1, columns // 2), jnp.bfloat16),
             jax.ShapeDtypeStruct((6 * c1, columns // 2), jnp.bfloat16),
         ),
         in_specs=[VMEM] * 5,
@@ -342,7 +374,8 @@
         compiler_params=params,
         cost_estimate=cost(10**6, 2 * 10**6),
     )(far.reshape(rows, width), scale, shift, own_slab, pair_slab)
-    crossed_rows = lax.ppermute(relay, BOTH, cross_narrow(wide, narrow))
+    relay, side, crossed_own = lax.optimization_barrier((relay, side, crossed_own))
+    crossed_rows = lax.ppermute(relay, BOTH, cross_narrow(wide, narrow, False))
     p1, hidden = pl.pallas_call(
         centre_kernel,
         out_shape=(
@@ -365,22 +398,23 @@
         cost_estimate=cost(10**7, 10**5),
     )(hidden, t2)
 
-    def add_side(kernel, out, rows, before):
-        return pl.pallas_call(
-            functools.partial(kernel, narrow),
-            out_shape=out,
-            in_specs=[VMEM] * 5,
-            out_specs=VMEM,
-            scratch_shapes=[
-                pltpu.VMEM((18 * c1, 2 * width), jnp.bfloat16),
-                pltpu.VMEM((12 * c1, 2 * width), jnp.bfloat16),
-            ],
-            compiler_params=params,
-            cost_estimate=cost(10**7, 10**5),
-        )(rows, p1, before, t1, t2)
-
-    p2 = add_side(partner_kernel, jax.ShapeDtypeStruct(p2.shape, p2.dtype), partner_rows, p2)
-    pooled = add_side(edge_kernel, jax.ShapeDtypeStruct((c2, LANES), jnp.bfloat16), crossed_rows, p2)
+    p2 = pl.pallas_call(
+        partner_kernel,
+        out_shape=jax.ShapeDtypeStruct(p2.shape, p2.dtype),
+        in_specs=[VMEM] * 5,
+        out_specs=VMEM,
+        compiler_params=params,
+        cost_estimate=cost(10**7, 10**5),
+    )(partner_rows, p1, p2, t1, t2)
+    pooled = pl.pallas_call(
+        functools.partial(edge_kernel, narrow),
+        out_shape=jax.ShapeDtypeStruct((c2, LANES), jnp.bfloat16),
+        in_specs=[VMEM] * 8,
+        out_specs=VMEM,
+        scratch_shapes=[pltpu.VMEM((rows // 2, width), jnp.float32)],
+        compiler_params=params,
+        cost_estimate=cost(10**7, 10**5),
+    )(crossed_own.reshape(rows // 2, width), crossed_rows, scale, shift, p1, p2, t1, t2)
     pooled_far = lax.ppermute(pooled, BOTH, cross_wide(wide, narrow))
     pooled_pair = lax.ppermute(pooled, "wide", pair_swap(wide))
     mine = jnp.stack([pooled, pooled_pair, pooled_far])[None]

time: 29.5 us -> 28.9 us (0.980)
  local copies, waits for them, and re-layouts: 3.43 us -> 1.24 us
  other arithmetic: 0.01 us -> 1.1 us
  waiting for transfers between devices: 7.1 us -> 8.08 us
  Pallas kernels: 7.11 us -> 6.74 us
    unnamed x11, local copies, waits for them, and re-layouts: 3.43 us -> 1.24 us
    ppermute x1, waiting for transfers between devices: 0.36 us -> 1.51 us  [body(): pair = lax.ppermute(stored_features, 'wide', pair_swap(wide))]
    select_n x0 -> x1, other arithmetic: none -> 1.09 us  [body(): jnp.where(lax.axis_index('narrow') % 2 == 1, stored_features[:, :, half:]...]
    pallas_call x2, Pallas kernels: 2.65 us -> 2.27 us  [the longest x1 1.24 us: body(): pl.pallas_call(functools.partial(edge_kernel, narrow), out_shape=jax.Shap...]
    ppermute x1 -> x2, starting transfers between devices: 2.44 us -> 2.32 us  [the longest x1 2.25 us: body(): crossed_rows = lax.ppermute(relay, BOTH, cross_narrow(wide, narrow, False))]
  transfers between devices with their start and end apart: 9 -> 10, of which waited for: 6 -> 7; matrix products, arithmetic and copies ran while one was open for 4% -> 8% of each run, Pallas kernels for 15% -> 15%
where the time goes in v6:
time: 28.9 us; the launch traced here: 28.7 us
  starting transfers between devices  11.4 us (39%)
  waiting for transfers between devices  8.08 us (28%)
  Pallas kernels  6.74 us (23%)
  local copies, waits for them, and re-layouts  1.24 us (4%)
  other arithmetic  1.1 us (4%)
    ppermute x1, waiting for transfers between devices, body(): other = lax.ppermute(held, 'narrow', pair_swap(narrow, bit))  3.7 us
    ppermute x1, starting transfers between devices, body(): pair = lax.ppermute(stored_features, 'wide', pair_swap(wide))  3.04 us
    ppermute x1, starting transfers between devices, body(): pooled_pair = lax.ppermute(pooled, 'wide', pair_swap(wide))  2.97 us
    ppermute x1, starting transfers between devices, body(): crossed_rows = lax.ppermute(relay, BOTH, cross_narrow(wide, narrow, False))  2.25 us
    ppermute x1, waiting for transfers between devices, body(): pair = lax.ppermute(stored_features, 'wide', pair_swap(wide))  1.51 us
    ppermute x1, waiting for transfers between devices, body(): pooled_pair = lax.ppermute(pooled, 'wide', pair_swap(wide))  1.51 us
    ppermute x1, starting transfers between devices, body(): far = lax.ppermute(stored_features, BOTH, cross_wide(wide, narrow))  1.49 us
    pallas_call x1, Pallas kernels, body(): pl.pallas_call(centre_kernel, out_shape=(jax.ShapeDtypeStruct((4 * c1, 4...  1.32 us
  transfers between devices with their start and end apart: 10, of which 7 were waited for; matrix products, arithmetic and copies ran while one was open for 8% of the time, Pallas kernels for 15%

profile of v6, /device:TPU:0, one launch (start us, length us, event | category | flops | bytes accessed | tf_op | source)
XLA Modules:
  0.0 28.7 jit_solution(10560446846148970994)
XLA Ops:
  0.0 0.0 copy-start.1
  0.0 0.0 copy-start.2
  0.0 0.0 copy-start.4
  0.0 0.0 copy-start.3
  0.0 3.0 %collective-permute-start.1 = (bf16[64,2,4,128]{3,2,1,0:T(4,128)(2,1)}, bf16[64,2,4,128]{3,2,1,0:T(4,128)(2,1)S(1)}, u32[]{:S(2)}, u32[]{:S(2)}) collective-permute-start(bf16[64,2,4,128]{3,2,1,0:T(4,128)(2,1)} %param.6), channel_id=1, source_target_pairs={{0,4},{4,0},{8,12},{12,8},{16,20},{20,16},{24,28},{28,24},{1,5},{5... | collective-permute-start | bytes 393224 | tf_op jit(solution)/shard_map/ppermute | solution.py:340
  3.1 1.5 %collective-permute-start = (bf16[64,2,4,128]{3,2,1,0:T(4,128)(2,1)}, bf16[64,2,4,128]{3,2,1,0:T(4,128)(2,1)S(1)}, u32[]{:S(2)}, u32[]{:S(2)}) collective-permute-start(bf16[64,2,4,128]{3,2,1,0:T(4,128)(2,1)} %param.6), channel_id=1, source_target_pairs={{0,2},{1,3},{2,0},{3,1},{4,8},{5,9},{6,10},{7,11},{8,4},{9,5},{10,... | collective-permute-start | bytes 393224 | tf_op jit(solution)/shard_map/ppermute | solution.py:339
  4.5 1.1 %broadcast_select_fusion = bf16[64,2,2,128]{3,2,1,0:T(2,128)(2,1)S(1)} fusion(pred[]{:T(512)S(6)} %eq.5, bf16[64,2,4,128]{3,2,1,0:T(4,128)(2,1)} %param.6), kind=kLoop, calls=%fused_computation | loop fusion | flops 32768 | bytes 196609 | tf_op jit(solution)/shard_map/jit(_where)/select_n | solution.py:354
  5.6 0.0 copy-start
  5.6 0.1 collective-permute-start.2
  5.7 1.2 %copy.9.w2_ref = bf16[128,1728]{1,0:T(8,128)(2,1)S(1)} copy(bf16[128,1728]{0,1:T(8,128)(2,1)} %param.10) | data formatting | bytes 884736 | tf_op args[4]
  6.9 0.0 copy-done.1
  7.0 0.0 copy-done.2
  7.0 0.4 %shard_map.65 = (bf16[256,3456]{1,0:T(8,128)(2,1)S(1)}, bf16[256,2304]{1,0:T(8,128)(2,1)S(1)}, bf16[576,384]{1,0:T(8,128)(2,1)S(1)}) custom-call(bf16[64,1728]{1,0:T(8,128)(2,1)S(1)} %copy-done.2, bf16[128,1728]{1,0:T(8,128)(2,1)S(1)} %copy.9.w2_ref, bf16[64,3456]{1,0:T(8,128)(2,1)S(1)} %copy-done.1), custom_call_target="tpu_custom_call" | custom-call | flops 1000000 | bytes 4000000 | tf_op jit(solution)/shard_map/pallas_call | solution.py:341
  7.4 1.5 %collective-permute-done.1 = bf16[64,2,4,128]{3,2,1,0:T(4,128)(2,1)S(1)} collective-permute-done((bf16[64,2,4,128]{3,2,1,0:T(4,128)(2,1)}, bf16[64,2,4,128]{3,2,1,0:T(4,128)(2,1)S(1)}, u32[]{:S(2)}, u32[]{:S(2)}) %collective-permute-start.1) | collective-permute-done | bytes 131104 | tf_op jit(solution)/shard_map/ppermute | solution.py:340
  8.9 0.0 copy-done.4
  8.9 0.0 copy-done.3
  8.9 0.1 shard_map.64.pair_ref
  9.1 0.0 collective-permute-done
  9.1 0.0 copy-done
  9.1 0.1 shard_map.66.own_ref
  9.2 0.2 shard_map.67
  9.4 0.3 collective-permute-done.2
  9.6 0.0 collective-permute-start.4
  9.6 2.2 %collective-permute-start.3 = (bf16[256,256]{1,0:T(8,128)(2,1)S(1)}, bf16[256,256]{1,0:T(8,128)(2,1)S(1)}, u32[]{:S(2)}, u32[]{:S(2)}) collective-permute-start(bf16[256,256]{1,0:T(8,128)(2,1)S(1)} %get-tuple-element.38), channel_id=1, source_target_pairs={{0,4},{1,2},{2,1},{3,7},{4,0},{5,6},{6,5},{7,3},{8,12},{9,10},{10,... | collective-permute-start | bytes 393224 | tf_op jit(solution)/shard_map/ppermute | solution.py:378
  11.9 1.3 %shard_map.68 = (f32[256,512]{1,0:T(8,128)S(1)}, bf16[768,256]{1,0:T(8,128)(2,1)S(1)}) custom-call(bf16[384,512]{1,0:T(8,128)(2,1)S(1)} %get-tuple-element.39.x_ref, bf16[256,3456]{1,0:T(8,128)(2,1)S(1)} %get-tuple-element.40.w1_ref), custom_call_target="tpu_custom_call" | custom-call | flops 10000000 | bytes 100000 | tf_op jit(solution)/shard_map/pallas_call | solution.py:379
  13.2 0.5 %shard_map.69.p2_ref = f32[256,512]{1,0:T(8,128)S(1)} custom-call(bf16[768,256]{1,0:T(8,128)(2,1)S(1)} %get-tuple-element.43.hidden_ref, bf16[256,2304]{1,0:T(8,128)(2,1)S(1)} %get-tuple-element.44.w2_ref), custom_call_target="tpu_custom_call" | custom-call | flops 10000000 | bytes 100000 | tf_op jit(solution)/shard_map/pallas_call | solution.py:392
  13.7 0.0 collective-permute-done.4.rows_ref
  13.7 1.0 %shard_map.70.p2_ref = f32[256,512]{1,0:T(8,128)S(1)} custom-call(bf16[384,256]{1,0:T(8,128)(2,1)S(1)} %collective-permute-done.4.rows_ref, f32[256,512]{1,0:T(8,128)S(1)} %get-tuple-element.41.p1_ref, f32[256,512]{1,0:T(8,128)S(1)} %shard_map.69.p2_ref, bf16[256,3456]{1,0:T(8,128)(2,1)S(1)} %get-tuple-element.40.w1_ref, ...), custom_call_target="tpu_custom_call" | custom-call | flops 10000000 | bytes 100000 | tf_op jit(solution)/shard_map/pallas_call | solution.py:401
  14.7 0.1 collective-permute-done.3.rows_ref
  14.8 1.2 %shard_map.71 = bf16[128,128]{1,0:T(8,128)(2,1)S(1)} custom-call(bf16[256,128]{1,0:T(8,128)(2,1)S(1)} %bitcast.16, bf16[256,256]{1,0:T(8,128)(2,1)S(1)} %collective-permute-done.3.rows_ref, f32[1,64]{1,0:T(1,128)S(1)} %bitcast.20, f32[1,64]{1,0:T(1,128)S(1)} %bitcast.24, f32[256,512]{1,0:T(8,128)S(1)} %get-tuple-element.41.p1_ref, ...), custom_call_target="tpu_custom_call" | custom-call | flops 10000000 | bytes 100000 | tf_op jit(solution)/shard_map/pallas_call | solution.py:409
  16.1 0.6 %collective-permute-start.6 = (bf16[128,128]{1,0:T(8,128)(2,1)S(1)}, bf16[128,128]{1,0:T(8,128)(2,1)S(1)}, u32[]{:S(2)}, u32[]{:S(2)}) collective-permute-start(bf16[128,128]{1,0:T(8,128)(2,1)S(1)} %shard_map.71), channel_id=1, source_target_pairs={{0,2},{1,3},{2,0},{3,1},{4,8},{5,9},{6,10},{7,11},{8,4},{9,5},{10,... | collective-permute-start | bytes 98312 | tf_op jit(solution)/shard_map/ppermute | solution.py:418
  16.7 3.0 %collective-permute-start.5 = (bf16[128,128]{1,0:T(8,128)(2,1)S(1)}, bf16[128,128]{1,0:T(8,128)(2,1)S(1)}, u32[]{:S(2)}, u32[]{:S(2)}) collective-permute-start(bf16[128,128]{1,0:T(8,128)(2,1)S(1)} %shard_map.71), channel_id=1, source_target_pairs={{0,4},{4,0},{8,12},{12,8},{16,20},{20,16},{24,28},{28,24},{1,5},{5... | collective-permute-start | bytes 98312 | tf_op jit(solution)/shard_map/ppermute | solution.py:419
  19.7 0.4 %collective-permute-done.6 = bf16[128,128]{1,0:T(8,128)(2,1)S(1)} collective-permute-done((bf16[128,128]{1,0:T(8,128)(2,1)S(1)}, bf16[128,128]{1,0:T(8,128)(2,1)S(1)}, u32[]{:S(2)}, u32[]{:S(2)}) %collective-permute-start.6) | collective-permute-done | bytes 32800 | tf_op jit(solution)/shard_map/ppermute | solution.py:418
  20.1 1.5 %collective-permute-done.5 = bf16[128,128]{1,0:T(8,128)(2,1)S(1)} collective-permute-done((bf16[128,128]{1,0:T(8,128)(2,1)S(1)}, bf16[128,128]{1,0:T(8,128)(2,1)S(1)}, u32[]{:S(2)}, u32[]{:S(2)}) %collective-permute-start.5) | collective-permute-done | bytes 32800 | tf_op jit(solution)/shard_map/ppermute | solution.py:419
  21.6 1.0 %collective-permute-start.7 = (bf16[1,3,128,128]{3,2,1,0:T(8,128)(2,1)S(1)}, bf16[1,3,128,128]{3,2,1,0:T(8,128)(2,1)S(1)}, u32[]{:S(2)}, u32[]{:S(2)}) collective-permute-start(bf16[1,3,128,128]{3,2,1,0:T(8,128)(2,1)S(1)} %maximum_bitcast_fusion.refs_0_), channel_id=1, source_target_pairs={{0,2},{1,3},{2,0},{3,1},{4,6},{5,7},{6,4},{7,5},{8,10},{9,11},{10,... | collective-permute-start | bytes 294920 | tf_op jit(solution)/shard_map/ppermute | solution.py:425
  22.6 0.0 collective-permute-start.9
  22.6 3.7 %collective-permute-done.7.refs_0_ = bf16[1,3,128,128]{3,2,1,0:T(8,128)(2,1)S(1)} collective-permute-done((bf16[1,3,128,128]{3,2,1,0:T(8,128)(2,1)S(1)}, bf16[1,3,128,128]{3,2,1,0:T(8,128)(2,1)S(1)}, u32[]{:S(2)}, u32[]{:S(2)}) %collective-permute-start.7) | collective-permute-done | bytes 98336 | tf_op jit(solution)/shard_map/ppermute | solution.py:425
  26.3 0.0 collective-permute-start.8
  26.3 0.0 collective-permute-done.9.refs_1_
  26.3 0.4 %shard_map.72.refs_2_ = f32[576,512]{1,0:T(8,128)S(1)} custom-call(bf16[1,3,128,128]{3,2,1,0:T(8,128)(2,1)S(1)} %maximum_bitcast_fusion.refs_0_, bf16[1,3,128,128]{3,2,1,0:T(8,128)(2,1)S(1)} %collective-permute-done.9.refs_1_, bf16[576,384]{1,0:T(8,128)(2,1)S(1)} %get-tuple-element.45.refs_2_.refs_1_.w3_ref), custom_call_target="tpu_custom_call" | custom-call | flops 10000000 | bytes 100000 | tf_op jit(solution)/shard_map/pallas_call | solution.py:451
  26.7 0.3 %shard_map.73.before_ref = f32[576,512]{1,0:T(8,128)S(1)} custom-call(bf16[1,3,128,128]{3,2,1,0:T(8,128)(2,1)S(1)} %collective-permute-done.7.refs_0_, bf16[576,384]{1,0:T(8,128)(2,1)S(1)} %get-tuple-element.45.refs_2_.refs_1_.w3_ref, f32[576,512]{1,0:T(8,128)S(1)} %shard_map.72.refs_2_), custom_call_target="tpu_custom_call", output_to_operand_aliasing={{}: (2, {})} | custom-call | flops 10000000 | bytes 100000 | tf_op jit(solution)/shard_map/pallas_call | solution.py:451
  27.0 0.6 %collective-permute-done.8.blocks_ref = bf16[1,3,128,128]{3,2,1,0:T(8,128)(2,1)S(1)} collective-permute-done((bf16[1,3,128,128]{3,2,1,0:T(8,128)(2,1)S(1)}, bf16[1,3,128,128]{3,2,1,0:T(8,128)(2,1)S(1)}, u32[]{:S(2)}, u32[]{:S(2)}) %collective-permute-start.8) | collective-permute-done | bytes 98336 | tf_op jit(solution)/shard_map/ppermute | solution.py:429
  27.6 1.2 %shard_map.74 = (bf16[64,512]{1,0:T(8,128)(2,1)}, f32[576,512]{1,0:T(8,128)S(1)}) custom-call(bf16[1,3,128,128]{3,2,1,0:T(8,128)(2,1)S(1)} %collective-permute-done.8.blocks_ref, bf16[576,384]{1,0:T(8,128)(2,1)S(1)} %get-tuple-element.45.refs_2_.refs_1_.w3_ref, f32[576,512]{1,0:T(8,128)S(1)} %shard_map.73.before_ref), custom_call_target="tpu_custom_call", output_to_operand_aliasing={{1}: (2, {})} | custom-call | flops 10000000 | bytes 100000 | tf_op jit(solution)/shard_map/pallas_call | solution.py:461
  (1 shorter events, 0.0 us)
Async XLA Ops:
  0.0 6.9 %copy-start.1 = (bf16[64,3456]{1,0:T(8,128)(2,1)S(1)}, bf16[64,3456]{1,0:T(8,128)(2,1)}, u32[]{:S(2)}) copy-start(bf16[64,3456]{1,0:T(8,128)(2,1)} %w3_ref.1) | copy-start | bytes 1327108
  0.0 7.0 %copy-start.2 = (bf16[64,1728]{1,0:T(8,128)(2,1)S(1)}, bf16[64,1728]{1,0:T(8,128)(2,1)}, u32[]{:S(2)}) copy-start(bf16[64,1728]{1,0:T(8,128)(2,1)} %w1_ref.1) | copy-start | bytes 663556
  0.0 8.9 %copy-start.4 = (f32[64]{0:T(128)S(1)}, f32[64]{0:T(128)}, u32[]{:S(2)}) copy-start(f32[64]{0:T(128)} %param.8) | copy-start | bytes 772
  0.0 8.9 %copy-start.3 = (f32[64]{0:T(128)S(1)}, f32[64]{0:T(128)}, u32[]{:S(2)}) copy-start(f32[64]{0:T(128)} %param.7) | copy-start | bytes 772
  0.0 8.9 %collective-permute-start.1 = (bf16[64,2,4,128]{3,2,1,0:T(4,128)(2,1)}, bf16[64,2,4,128]{3,2,1,0:T(4,128)(2,1)S(1)}, u32[]{:S(2)}, u32[]{:S(2)}) collective-permute-start(bf16[64,2,4,128]{3,2,1,0:T(4,128)(2,1)} %param.6), channel_id=1, source_target_pairs={{0,4},{4,0},{8,12},{12,8},{16,20},{20,16},{24,28},{28,24},{1,5},{5... | collective-permute-start | bytes 393224 | tf_op jit(solution)/shard_map/ppermute | solution.py:340
  3.1 6.0 %collective-permute-start = (bf16[64,2,4,128]{3,2,1,0:T(4,128)(2,1)}, bf16[64,2,4,128]{3,2,1,0:T(4,128)(2,1)S(1)}, u32[]{:S(2)}, u32[]{:S(2)}) collective-permute-start(bf16[64,2,4,128]{3,2,1,0:T(4,128)(2,1)} %param.6), channel_id=1, source_target_pairs={{0,2},{1,3},{2,0},{3,1},{4,8},{5,9},{6,10},{7,11},{8,4},{9,5},{10,... | collective-permute-start | bytes 393224 | tf_op jit(solution)/shard_map/ppermute | solution.py:339
  5.6 3.4 %copy-start = (bf16[64,2,4,128]{3,2,1,0:T(4,128)(2,1)S(1)}, bf16[64,2,4,128]{3,2,1,0:T(4,128)(2,1)}, u32[]{:S(2)}) copy-start(bf16[64,2,4,128]{3,2,1,0:T(4,128)(2,1)} %param.6) | copy-start | bytes 393220
  5.6 4.0 %collective-permute-start.2 = (bf16[64,2,2,128]{3,2,1,0:T(2,128)(2,1)S(1)}, bf16[64,2,2,128]{3,2,1,0:T(2,128)(2,1)S(1)}, u32[]{:S(2)}, u32[]{:S(2)}) collective-permute-start(bf16[64,2,2,128]{3,2,1,0:T(2,128)(2,1)S(1)} %broadcast_select_fusion), channel_id=1, source_target_pairs={{0,3},{1,2},{2,1},{3,0},{4,7},{5,6},{6,5},{7,4},{8,11},{9,10},{10,... | collective-permute-start | bytes 196616 | tf_op jit(solution)/shard_map/ppermute | solution.py:359
  9.6 4.1 %collective-permute-start.4 = (bf16[384,256]{1,0:T(8,128)(2,1)S(1)}, bf16[384,256]{1,0:T(8,128)(2,1)S(1)}, u32[]{:S(2)}, u32[]{:S(2)}) collective-permute-start(bf16[384,256]{1,0:T(8,128)(2,1)S(1)} %get-tuple-element.42), channel_id=1, source_target_pairs={{0,1},{1,0},{2,3},{3,2},{4,5},{5,4},{6,7},{7,6},{8,9},{9,8},{10,11... | collective-permute-start | bytes 589832 | tf_op jit(solution)/shard_map/ppermute | solution.py:391
  9.6 5.2 %collective-permute-start.3 = (bf16[256,256]{1,0:T(8,128)(2,1)S(1)}, bf16[256,256]{1,0:T(8,128)(2,1)S(1)}, u32[]{:S(2)}, u32[]{:S(2)}) collective-permute-start(bf16[256,256]{1,0:T(8,128)(2,1)S(1)} %get-tuple-element.38), channel_id=1, source_target_pairs={{0,4},{1,2},{2,1},{3,7},{4,0},{5,6},{6,5},{7,3},{8,12},{9,10},{10,... | collective-permute-start | bytes 393224 | tf_op jit(solution)/shard_map/ppermute | solution.py:378
  16.1 4.0 %collective-permute-start.6 = (bf16[128,128]{1,0:T(8,128)(2,1)S(1)}, bf16[128,128]{1,0:T(8,128)(2,1)S(1)}, u32[]{:S(2)}, u32[]{:S(2)}) collective-permute-start(bf16[128,128]{1,0:T(8,128)(2,1)S(1)} %shard_map.71), channel_id=1, source_target_pairs={{0,2},{1,3},{2,0},{3,1},{4,8},{5,9},{6,10},{7,11},{8,4},{9,5},{10,... | collective-permute-start | bytes 98312 | tf_op jit(solution)/shard_map/ppermute | solution.py:418
  16.7 4.9 %collective-permute-start.5 = (bf16[128,128]{1,0:T(8,128)(2,1)S(1)}, bf16[128,128]{1,0:T(8,128)(2,1)S(1)}, u32[]{:S(2)}, u32[]{:S(2)}) collective-permute-start(bf16[128,128]{1,0:T(8,128)(2,1)S(1)} %shard_map.71), channel_id=1, source_target_pairs={{0,4},{4,0},{8,12},{12,8},{16,20},{20,16},{24,28},{28,24},{1,5},{5... | collective-permute-start | bytes 98312 | tf_op jit(solution)/shard_map/ppermute | solution.py:419
  21.6 4.7 %collective-permute-start.7 = (bf16[1,3,128,128]{3,2,1,0:T(8,128)(2,1)S(1)}, bf16[1,3,128,128]{3,2,1,0:T(8,128)(2,1)S(1)}, u32[]{:S(2)}, u32[]{:S(2)}) collective-permute-start(bf16[1,3,128,128]{3,2,1,0:T(8,128)(2,1)S(1)} %maximum_bitcast_fusion.refs_0_), channel_id=1, source_target_pairs={{0,2},{1,3},{2,0},{3,1},{4,6},{5,7},{6,4},{7,5},{8,10},{9,11},{10,... | collective-permute-start | bytes 294920 | tf_op jit(solution)/shard_map/ppermute | solution.py:425
  22.6 3.7 %collective-permute-start.9 = (bf16[1,3,128,128]{3,2,1,0:T(8,128)(2,1)S(1)}, bf16[1,3,128,128]{3,2,1,0:T(8,128)(2,1)S(1)}, u32[]{:S(2)}, u32[]{:S(2)}) collective-permute-start(bf16[1,3,128,128]{3,2,1,0:T(8,128)(2,1)S(1)} %maximum_bitcast_fusion.refs_0_), channel_id=1, source_target_pairs={{0,1},{1,0},{2,3},{3,2},{4,5},{5,4},{6,7},{7,6},{8,9},{9,8},{10,11... | collective-permute-start | bytes 294920 | tf_op jit(solution)/shard_map/ppermute | solution.py:422
  26.3 1.3 %collective-permute-start.8 = (bf16[1,3,128,128]{3,2,1,0:T(8,128)(2,1)S(1)}, bf16[1,3,128,128]{3,2,1,0:T(8,128)(2,1)S(1)}, u32[]{:S(2)}, u32[]{:S(2)}) collective-permute-start(bf16[1,3,128,128]{3,2,1,0:T(8,128)(2,1)S(1)} %collective-permute-done.7.refs_0_), channel_id=1, source_target_pairs={{0,1},{1,0},{2,3},{3,2},{4,5},{5,4},{6,7},{7,6},{8,9},{9,8},{10,11... | collective-permute-start | bytes 294920 | tf_op jit(solution)/shard_map/ppermute | solution.py:429

commit v7 on v6

--- a/solution.py
+++ b/solution.py
@@ -24,7 +24,7 @@
 
 
 def cross_wide(wide, narrow):
-    bit = 2 if narrow % 4 == 0 else 1
+    bit = 1
     steps = []
     for i in range(wide):
         for j in range(narrow):
@@ -98,40 +98,29 @@
     return jnp.sum(jnp.where(here, jnp.broadcast_to(row, square), 0.0), axis=1, keepdims=True)
 
 
-def unpack_kernel(raw_ref, scale_ref, shift_ref, out_ref, staged):
-    c = scale_ref.shape[1]
-    depth, height = out_ref.shape[0] // c, out_ref.shape[1] // LANES
-    staged[...] = raw_ref[...].astype(jnp.float32)
-    scale, shift = column(scale_ref), column(shift_ref)
-    for d in range(depth):
-        for h in range(height):
-            rows = staged[pl.ds(d * height + h, c, stride=depth * height), :]
-            out_ref[d * c : (d + 1) * c, h * LANES : (h + 1) * LANES] = (
-                rows * scale + shift
-            ).astype(jnp.bfloat16)
-
-
 def slab_kernel(
-    wide, raw_ref, scale_ref, shift_ref, own_ref, pair_ref, out_ref, relay_ref, side_ref, staged
+    wide, own_ref, pair_ref, far_ref, scale_ref, shift_ref, out_ref, relay_ref, side_ref, staged
 ):
     i, j = lax.axis_index("wide"), lax.axis_index("narrow")
     i_odd, j_odd = lax.rem(i, 2), lax.rem(j, 2)
-    block, columns = own_ref.shape
+    block, columns = out_ref.shape[0] // 3, out_ref.shape[1]
     c = scale_ref.shape[1]
     depth, height = block // c, columns // LANES
-    far_row = pl.multiple_of(2 * i_odd * block, block)
-    pair_row = pl.multiple_of((2 - 2 * i_odd) * block, block)
     keep = jnp.where(i == i_odd * (wide - 1), 0.0, 1.0)
-    staged[...] = raw_ref[...].astype(jnp.float32)
-    scale, shift = column(scale_ref) * keep, column(shift_ref) * keep
-    for d in range(depth):
-        for h in range(height):
-            rows = staged[pl.ds(d * height + h, c, stride=depth * height), :]
-            out_ref[
-                pl.ds(pl.multiple_of(far_row + d * c, c), c), h * LANES : (h + 1) * LANES
-            ] = (rows * scale + shift).astype(jnp.bfloat16)
-    out_ref[block : 2 * block, :] = own_ref[...]
-    out_ref[pl.ds(pair_row, block), :] = pair_ref[...]
+    scale, shift = column(scale_ref), column(shift_ref)
+    size = own_ref.shape[0]
+    for n, ref in enumerate((own_ref, pair_ref, far_ref)):
+        staged[n * size : (n + 1) * size, :] = ref[...].astype(jnp.float32)
+        slot = (1, 2 - 2 * i_odd, 2 * i_odd)[n]
+        gain, offset = (scale * keep, shift * keep) if n == 2 else (scale, shift)
+        for d in range(depth):
+            for h in range(height):
+                start = n * size + d * height + h
+                value = staged[pl.ds(start, c, stride=depth * height), :] * gain + offset
+                row = slot * block + d * c
+                rows = slice(row, row + c) if n == 0 else pl.ds(pl.multiple_of(row, c), c)
+                out_ref[rows, h * LANES : (h + 1) * LANES] = value.astype(jnp.bfloat16)
+
     half = columns // 2
     lane = pl.multiple_of(j_odd * half, half)
     relay_ref[:block, :] = out_ref[:block, pl.ds(lane, half)]
@@ -160,24 +149,27 @@
     return [ref[:, b * span : (b + 1) * span] for b in range(3)]
 
 
-def centre_kernel(x_ref, w1_ref, p1_ref, hidden_ref, taps):
-    spread(x_ref[...], taps, 0)
+def beside(*parts):
+    return jnp.concatenate(parts, axis=1)
+
+
+def part(ref, k):
+    return ref[:, k * LANES : (k + 1) * LANES]
+
+
+def centre_kernel(x_ref, w1_ref, w2_ref, p1_ref, p2_ref):
+    taps = [stacked(part(x_ref, k).astype(jnp.float32)) for k in range(4)]
     first = thirds(w1_ref)
-    columns = jnp.concatenate(
-        [taps[:, b * LANES : (b + 2) * LANES] for b in range(3)], axis=0
-    )
-    spread(jnp.maximum(dot(w1_ref[...], columns), 0.0), hidden_ref, 0)
-    r0 = dot(first[0], tile(taps, 2, 3))
-    r1 = dot(first[1], tile(taps, 0, 3))
-    r2 = dot(first[2], tile(taps, 0, 1))
+    pairs = jnp.concatenate([beside(taps[b], taps[b + 1]) for b in range(3)], axis=0)
+    inner = jnp.maximum(dot(w1_ref[...], pairs), 0.0)
+    both = beside(stacked(inner[:, :LANES]), stacked(inner[:, LANES:]))
+    r0 = dot(first[0], beside(taps[2], taps[3]))
+    r1 = dot(first[1], beside(taps[0], taps[3]))
+    r2 = dot(first[2], beside(taps[0], taps[1]))
     p1_ref[:, 0:LANES] = r2[:, :LANES]
     p1_ref[:, LANES : 2 * LANES] = r2[:, LANES:] + r1[:, :LANES]
     p1_ref[:, 2 * LANES : 3 * LANES] = r0[:, LANES:]
     p1_ref[:, 3 * LANES :] = r1[:, LANES:] + r0[:, :LANES]
-
-
-def second_kernel(hidden_ref, w2_ref, p2_ref):
-    both = hidden_ref[...]
     q0, q1, q2 = (dot(w, both) for w in thirds(w2_ref))
     p2_ref[:, 0:LANES] = q2[:, :LANES]
     p2_ref[:, LANES : 2 * LANES] = q2[:, LANES:] + q1[:, :LANES]
@@ -324,17 +316,6 @@
 
     def cost(flops, size):
         return pl.CostEstimate(flops=flops, bytes_accessed=size, transcendentals=0)
-
-    def unpack(block):
-        return pl.pallas_call(
-            unpack_kernel,
-            out_shape=jax.ShapeDtypeStruct((depth * c1, columns), jnp.bfloat16),
-            in_specs=[VMEM] * 3,
-            out_specs=VMEM,
-            scratch_shapes=[pltpu.VMEM((rows, width), jnp.float32)],
-            compiler_params=params,
-            cost_estimate=cost(10**6, 10**6),
-        )(block.reshape(rows, width), scale, shift)
 
     far = lax.ppermute(stored_features, BOTH, cross_wide(wide, narrow))
     pair = lax.ppermute(stored_features, "wide", pair_swap(wide))
@@ -358,9 +339,8 @@
     )
     crossed_own = lax.ppermute(edges, BOTH, cross_narrow(wide, narrow, True))
     pair, raw, scale, shift = lax.optimization_barrier((pair, stored_features, scale, shift))
-    own_slab = unpack(raw)
-    pair_slab = unpack(pair)
-    far, pair_slab, t1, t2, t3 = lax.optimization_barrier((far, pair_slab, t1, t2, t3))
+    pair_rows = pair.reshape(rows, width)
+    far, pair_rows, t1, t2, t3 = lax.optimization_barrier((far, pair_rows, t1, t2, t3))
     slab, relay, side = pl.pallas_call(
         functools.partial(slab_kernel, wide),
         out_shape=(
@@ -370,34 +350,24 @@
         ),
         in_specs=[VMEM] * 5,
         out_specs=(VMEM,) * 3,
-        scratch_shapes=[pltpu.VMEM((rows, width), jnp.float32)],
+        scratch_shapes=[pltpu.VMEM((3 * rows, width), jnp.float32)],
         compiler_params=params,
         cost_estimate=cost(10**6, 2 * 10**6),
-    )(far.reshape(rows, width), scale, shift, own_slab, pair_slab)
+    )(raw.reshape(rows, width), pair_rows, far.reshape(rows, width), scale, shift)
     relay, side, crossed_own = lax.optimization_barrier((relay, side, crossed_own))
     crossed_rows = lax.ppermute(relay, BOTH, cross_narrow(wide, narrow, False))
-    p1, hidden = pl.pallas_call(
+    p1, p2 = pl.pallas_call(
         centre_kernel,
         out_shape=(
             jax.ShapeDtypeStruct((4 * c1, 4 * width), jnp.float32),
-            jax.ShapeDtypeStruct((12 * c1, 2 * width), jnp.bfloat16),
+            jax.ShapeDtypeStruct((2 * c2, 4 * width), jnp.float32),
         ),
-        in_specs=[VMEM] * 2,
+        in_specs=[VMEM] * 3,
         out_specs=(VMEM,) * 2,
-        scratch_shapes=[pltpu.VMEM((18 * c1, 4 * width), jnp.bfloat16)],
         compiler_params=params,
         cost_estimate=cost(10**7, 10**5),
-    )(slab, t1)
+    )(slab, t1, t2)
     partner_rows = lax.ppermute(side, "narrow", pair_swap(narrow))
-    p2 = pl.pallas_call(
-        second_kernel,
-        out_shape=jax.ShapeDtypeStruct((2 * c2, 4 * width), jnp.float32),
-        in_specs=[VMEM] * 2,
-        out_specs=VMEM,
-        compiler_params=params,
-        cost_estimate=cost(10**7, 10**5),
-    )(hidden, t2)
-
     p2 = pl.pallas_call(
         partner_kernel,
         out_shape=jax.ShapeDtypeStruct(p2.shape, p2.dtype),

time: 28.9 us -> 28.8 us (level)
  starting transfers between devices: 11.4 us -> 11.8 us
    ppermute x1, starting transfers between devices: 0.07 us -> 1.68 us  [body(): crossed_own = lax.ppermute(edges, BOTH, cross_narrow(wide, narrow, True))]
    ppermute x1, starting transfers between devices: 1.49 us -> 0.01 us  [body(): far = lax.ppermute(stored_features, BOTH, cross_wide(wide, narrow))]
    pallas_call x3 -> x0, Pallas kernels: 0.7 us -> none  [the longest x1 0.48 us: body(): pl.pallas_call(second_kernel, out_shape=jax.ShapeDtypeStruct((2 * c2, 4 *...]
    ppermute x1, starting transfers between devices: 2.97 us -> 3.53 us  [body(): pooled_pair = lax.ppermute(pooled, 'wide', pair_swap(wide))]
    ppermute x1, starting transfers between devices: 0.63 us -> 0.07 us  [body(): pooled_far = lax.ppermute(pooled, BOTH, cross_wide(wide, narrow))]
    pallas_call x1, Pallas kernels: 1.32 us -> 1.7 us  [body(): pl.pallas_call(centre_kernel, out_shape=(jax.ShapeDtypeStruct((4 * c1, 4...]
    ppermute x1, waiting for transfers between devices: 1.51 us -> 1.89 us  [body(): pooled_pair = lax.ppermute(pooled, 'wide', pair_swap(wide))]
    ppermute x1, waiting for transfers between devices: 0.38 us -> 0.01 us  [body(): pooled_far = lax.ppermute(pooled, BOTH, cross_wide(wide, narrow))]
  transfers between devices with their start and end apart: 10 -> 10, of which waited for: 7 -> 5; matrix products, arithmetic and copies ran while one was open for 8% -> 8% of each run, Pallas kernels for 15% -> 14%
where the time goes in v7:
time: 28.8 us; the launch traced here: 28.6 us
  starting transfers between devices  11.8 us (41%)
  waiting for transfers between devices  7.83 us (27%)
  Pallas kernels  6.52 us (23%)
  local copies, waits for them, and re-layouts  1.23 us (4%)
  other arithmetic  1.1 us (4%)
    ppermute x1, waiting for transfers between devices, body(): other = lax.ppermute(held, 'narrow', pair_swap(narrow, bit))  3.7 us
    ppermute x1, starting transfers between devices, body(): pooled_pair = lax.ppermute(pooled, 'wide', pair_swap(wide))  3.53 us
    ppermute x1, starting transfers between devices, body(): pair = lax.ppermute(stored_features, 'wide', pair_swap(wide))  3.05 us
    ppermute x1, starting transfers between devices, body(): crossed_rows = lax.ppermute(relay, BOTH, cross_narrow(wide, narrow, False))  2.45 us
    ppermute x1, waiting for transfers between devices, body(): pooled_pair = lax.ppermute(pooled, 'wide', pair_swap(wide))  1.89 us
    pallas_call x1, Pallas kernels, body(): pl.pallas_call(centre_kernel, out_shape=(jax.ShapeDtypeStruct((4 * c1, 4...  1.7 us
    ppermute x1, starting transfers between devices, body(): crossed_own = lax.ppermute(edges, BOTH, cross_narrow(wide, narrow, True))  1.68 us
    ppermute x1, waiting for transfers between devices, body(): pair = lax.ppermute(stored_features, 'wide', pair_swap(wide))  1.42 us
  transfers between devices with their start and end apart: 10, of which 5 were waited for; matrix products, arithmetic and copies ran while one was open for 8% of the time, Pallas kernels for 14%

profile of v7, /device:TPU:0, one launch (start us, length us, event | category | flops | bytes accessed | tf_op | source)
XLA Modules:
  0.0 28.6 jit_solution(560714532432066937)
XLA Ops:
  0.0 0.0 copy-start
  0.0 0.0 copy-start.1
  0.0 0.0 copy-start.2
  0.0 0.0 copy-start.4
  0.0 0.0 copy-start.3
  0.0 3.0 %collective-permute-start = (bf16[64,2,4,128]{3,2,1,0:T(4,128)(2,1)}, bf16[64,2,4,128]{3,2,1,0:T(4,128)(2,1)S(1)}, u32[]{:S(2)}, u32[]{:S(2)}) collective-permute-start(bf16[64,2,4,128]{3,2,1,0:T(4,128)(2,1)} %param.6), channel_id=1, source_target_pairs={{0,4},{4,0},{8,12},{12,8},{16,20},{20,16},{24,28},{28,24},{1,5},{5... | collective-permute-start | bytes 393224 | tf_op jit(solution)/shard_map/ppermute | solution.py:321
  3.1 0.0 collective-permute-start.1
  3.1 1.1 %broadcast_select_fusion = bf16[64,2,2,128]{3,2,1,0:T(2,128)(2,1)S(1)} fusion(pred[]{:T(512)S(6)} %eq.5, bf16[64,2,4,128]{3,2,1,0:T(4,128)(2,1)} %param.6), kind=kLoop, calls=%fused_computation | loop fusion | flops 32768 | bytes 196609 | tf_op jit(solution)/shard_map/jit(_where)/select_n | solution.py:335
  4.2 1.7 %collective-permute-start.2 = (bf16[64,2,2,128]{3,2,1,0:T(2,128)(2,1)S(1)}, bf16[64,2,2,128]{3,2,1,0:T(2,128)(2,1)S(1)}, u32[]{:S(2)}, u32[]{:S(2)}) collective-permute-start(bf16[64,2,2,128]{3,2,1,0:T(2,128)(2,1)S(1)} %broadcast_select_fusion), channel_id=1, source_target_pairs={{0,3},{1,2},{2,1},{3,0},{4,7},{5,6},{6,5},{7,4},{8,11},{9,10},{10,... | collective-permute-start | bytes 196616 | tf_op jit(solution)/shard_map/ppermute | solution.py:340
  5.8 1.2 %copy.9.w2_ref = bf16[128,1728]{1,0:T(8,128)(2,1)S(1)} copy(bf16[128,1728]{0,1:T(8,128)(2,1)} %param.10) | data formatting | bytes 884736 | tf_op args[4]
  7.0 0.0 copy-done.1
  7.1 0.0 copy-done.2
  7.1 0.4 %shard_map.64 = (bf16[256,3456]{1,0:T(8,128)(2,1)S(1)}, bf16[256,2304]{1,0:T(8,128)(2,1)S(1)}, bf16[576,384]{1,0:T(8,128)(2,1)S(1)}) custom-call(bf16[64,1728]{1,0:T(8,128)(2,1)S(1)} %copy-done.2, bf16[128,1728]{1,0:T(8,128)(2,1)S(1)} %copy.9.w2_ref, bf16[64,3456]{1,0:T(8,128)(2,1)S(1)} %copy-done.1), custom_call_target="tpu_custom_call" | custom-call | flops 1000000 | bytes 4000000 | tf_op jit(solution)/shard_map/pallas_call | solution.py:322
  7.5 1.4 %collective-permute-done = bf16[64,2,4,128]{3,2,1,0:T(4,128)(2,1)S(1)} collective-permute-done((bf16[64,2,4,128]{3,2,1,0:T(4,128)(2,1)}, bf16[64,2,4,128]{3,2,1,0:T(4,128)(2,1)S(1)}, u32[]{:S(2)}, u32[]{:S(2)}) %collective-permute-start) | collective-permute-done | bytes 131104 | tf_op jit(solution)/shard_map/ppermute | solution.py:321
  8.9 0.0 collective-permute-done.1
  8.9 0.0 copy-done
  8.9 0.0 copy-done.4
  9.0 0.0 copy-done.3
  9.0 0.3 shard_map.65
  9.2 0.0 collective-permute-done.2
  9.2 0.1 collective-permute-start.4
  9.3 2.4 %collective-permute-start.3 = (bf16[256,256]{1,0:T(8,128)(2,1)S(1)}, bf16[256,256]{1,0:T(8,128)(2,1)S(1)}, u32[]{:S(2)}, u32[]{:S(2)}) collective-permute-start(bf16[256,256]{1,0:T(8,128)(2,1)S(1)} %get-tuple-element.38), channel_id=1, source_target_pairs={{0,4},{1,2},{2,1},{3,7},{4,0},{5,6},{6,5},{7,3},{8,12},{9,10},{10,... | collective-permute-start | bytes 393224 | tf_op jit(solution)/shard_map/ppermute | solution.py:358
  11.8 1.7 %shard_map.66 = (f32[256,512]{1,0:T(8,128)S(1)}, f32[256,512]{1,0:T(8,128)S(1)}) custom-call(bf16[384,512]{1,0:T(8,128)(2,1)S(1)} %get-tuple-element.39.x_ref, bf16[256,3456]{1,0:T(8,128)(2,1)S(1)} %get-tuple-element.40.w1_ref, bf16[256,2304]{1,0:T(8,128)(2,1)S(1)} %get-tuple-element.41.w2_ref), custom_call_target="tpu_custom_call" | custom-call | flops 10000000 | bytes 100000 | tf_op jit(solution)/shard_map/pallas_call | solution.py:359
  13.5 0.0 collective-permute-done.4.rows_ref
  13.5 1.0 %shard_map.67.p2_ref = f32[256,512]{1,0:T(8,128)S(1)} custom-call(bf16[384,256]{1,0:T(8,128)(2,1)S(1)} %collective-permute-done.4.rows_ref, f32[256,512]{1,0:T(8,128)S(1)} %get-tuple-element.42.p1_ref, f32[256,512]{1,0:T(8,128)S(1)} %get-tuple-element.44.p2_ref, bf16[256,3456]{1,0:T(8,128)(2,1)S(1)} %get-tuple-element.40.w1_ref, ...), custom_call_target="tpu_custom_call" | custom-call | flops 10000000 | bytes 100000 | tf_op jit(solution)/shard_map/pallas_call | solution.py:371
  14.5 0.2 collective-permute-done.3.rows_ref
  14.7 1.2 %shard_map.68 = bf16[128,128]{1,0:T(8,128)(2,1)S(1)} custom-call(bf16[256,128]{1,0:T(8,128)(2,1)S(1)} %bitcast.16, bf16[256,256]{1,0:T(8,128)(2,1)S(1)} %collective-permute-done.3.rows_ref, f32[1,64]{1,0:T(1,128)S(1)} %bitcast.18, f32[1,64]{1,0:T(1,128)S(1)} %bitcast.20, f32[256,512]{1,0:T(8,128)S(1)} %get-tuple-element.42.p1_ref, ...), custom_call_target="tpu_custom_call" | custom-call | flops 10000000 | bytes 100000 | tf_op jit(solution)/shard_map/pallas_call | solution.py:379
  16.0 0.1 collective-permute-start.6
  16.0 3.5 %collective-permute-start.5 = (bf16[128,128]{1,0:T(8,128)(2,1)S(1)}, bf16[128,128]{1,0:T(8,128)(2,1)S(1)}, u32[]{:S(2)}, u32[]{:S(2)}) collective-permute-start(bf16[128,128]{1,0:T(8,128)(2,1)S(1)} %shard_map.68), channel_id=1, source_target_pairs={{0,4},{4,0},{8,12},{12,8},{16,20},{20,16},{24,28},{28,24},{1,5},{5... | collective-permute-start | bytes 98312 | tf_op jit(solution)/shard_map/ppermute | solution.py:389
  19.6 0.0 collective-permute-done.6
  19.6 1.9 %collective-permute-done.5 = bf16[128,128]{1,0:T(8,128)(2,1)S(1)} collective-permute-done((bf16[128,128]{1,0:T(8,128)(2,1)S(1)}, bf16[128,128]{1,0:T(8,128)(2,1)S(1)}, u32[]{:S(2)}, u32[]{:S(2)}) %collective-permute-start.5) | collective-permute-done | bytes 32800 | tf_op jit(solution)/shard_map/ppermute | solution.py:389
  21.5 1.0 %collective-permute-start.7 = (bf16[1,3,128,128]{3,2,1,0:T(8,128)(2,1)S(1)}, bf16[1,3,128,128]{3,2,1,0:T(8,128)(2,1)S(1)}, u32[]{:S(2)}, u32[]{:S(2)}) collective-permute-start(bf16[1,3,128,128]{3,2,1,0:T(8,128)(2,1)S(1)} %maximum_bitcast_fusion.refs_0_), channel_id=1, source_target_pairs={{0,2},{1,3},{2,0},{3,1},{4,6},{5,7},{6,4},{7,5},{8,10},{9,11},{10,... | collective-permute-start | bytes 294920 | tf_op jit(solution)/shard_map/ppermute | solution.py:395
  22.5 0.0 collective-permute-start.9
  22.5 3.7 %collective-permute-done.7.refs_0_ = bf16[1,3,128,128]{3,2,1,0:T(8,128)(2,1)S(1)} collective-permute-done((bf16[1,3,128,128]{3,2,1,0:T(8,128)(2,1)S(1)}, bf16[1,3,128,128]{3,2,1,0:T(8,128)(2,1)S(1)}, u32[]{:S(2)}, u32[]{:S(2)}) %collective-permute-start.7) | collective-permute-done | bytes 98336 | tf_op jit(solution)/shard_map/ppermute | solution.py:395
  26.2 0.0 collective-permute-start.8
  26.2 0.0 collective-permute-done.9.refs_1_
  26.2 0.4 %shard_map.69.refs_2_ = f32[576,512]{1,0:T(8,128)S(1)} custom-call(bf16[1,3,128,128]{3,2,1,0:T(8,128)(2,1)S(1)} %maximum_bitcast_fusion.refs_0_, bf16[1,3,128,128]{3,2,1,0:T(8,128)(2,1)S(1)} %collective-permute-done.9.refs_1_, bf16[576,384]{1,0:T(8,128)(2,1)S(1)} %get-tuple-element.45.refs_2_.refs_1_.w3_ref), custom_call_target="tpu_custom_call" | custom-call | flops 10000000 | bytes 100000 | tf_op jit(solution)/shard_map/pallas_call | solution.py:421
  26.6 0.3 %shard_map.70.before_ref = f32[576,512]{1,0:T(8,128)S(1)} custom-call(bf16[1,3,128,128]{3,2,1,0:T(8,128)(2,1)S(1)} %collective-permute-done.7.refs_0_, bf16[576,384]{1,0:T(8,128)(2,1)S(1)} %get-tuple-element.45.refs_2_.refs_1_.w3_ref, f32[576,512]{1,0:T(8,128)S(1)} %shard_map.69.refs_2_), custom_call_target="tpu_custom_call", output_to_operand_aliasing={{}: (2, {})} | custom-call | flops 10000000 | bytes 100000 | tf_op jit(solution)/shard_map/pallas_call | solution.py:421
  26.9 0.6 %collective-permute-done.8.blocks_ref = bf16[1,3,128,128]{3,2,1,0:T(8,128)(2,1)S(1)} collective-permute-done((bf16[1,3,128,128]{3,2,1,0:T(8,128)(2,1)S(1)}, bf16[1,3,128,128]{3,2,1,0:T(8,128)(2,1)S(1)}, u32[]{:S(2)}, u32[]{:S(2)}) %collective-permute-start.8) | collective-permute-done | bytes 98336 | tf_op jit(solution)/shard_map/ppermute | solution.py:399
  27.5 1.2 %shard_map.71 = (bf16[64,512]{1,0:T(8,128)(2,1)}, f32[576,512]{1,0:T(8,128)S(1)}) custom-call(bf16[1,3,128,128]{3,2,1,0:T(8,128)(2,1)S(1)} %collective-permute-done.8.blocks_ref, bf16[576,384]{1,0:T(8,128)(2,1)S(1)} %get-tuple-element.45.refs_2_.refs_1_.w3_ref, f32[576,512]{1,0:T(8,128)S(1)} %shard_map.70.before_ref), custom_call_target="tpu_custom_call", output_to_operand_aliasing={{1}: (2, {})} | custom-call | flops 10000000 | bytes 100000 | tf_op jit(solution)/shard_map/pallas_call | solution.py:431
  (1 shorter events, 0.0 us)
Async XLA Ops:
  0.0 8.9 %copy-start = (bf16[64,2,4,128]{3,2,1,0:T(4,128)(2,1)S(1)}, bf16[64,2,4,128]{3,2,1,0:T(4,128)(2,1)}, u32[]{:S(2)}) copy-start(bf16[64,2,4,128]{3,2,1,0:T(4,128)(2,1)} %param.6) | copy-start | bytes 393220
  0.0 7.0 %copy-start.1 = (bf16[64,3456]{1,0:T(8,128)(2,1)S(1)}, bf16[64,3456]{1,0:T(8,128)(2,1)}, u32[]{:S(2)}) copy-start(bf16[64,3456]{1,0:T(8,128)(2,1)} %w3_ref.1) | copy-start | bytes 1327108
  0.0 7.1 %copy-start.2 = (bf16[64,1728]{1,0:T(8,128)(2,1)S(1)}, bf16[64,1728]{1,0:T(8,128)(2,1)}, u32[]{:S(2)}) copy-start(bf16[64,1728]{1,0:T(8,128)(2,1)} %w1_ref.1) | copy-start | bytes 663556
  0.0 8.9 %copy-start.4 = (f32[64]{0:T(128)S(1)}, f32[64]{0:T(128)}, u32[]{:S(2)}) copy-start(f32[64]{0:T(128)} %param.8) | copy-start | bytes 772
  0.0 8.9 %copy-start.3 = (f32[64]{0:T(128)S(1)}, f32[64]{0:T(128)}, u32[]{:S(2)}) copy-start(f32[64]{0:T(128)} %param.7) | copy-start | bytes 772
  0.0 8.9 %collective-permute-start = (bf16[64,2,4,128]{3,2,1,0:T(4,128)(2,1)}, bf16[64,2,4,128]{3,2,1,0:T(4,128)(2,1)S(1)}, u32[]{:S(2)}, u32[]{:S(2)}) collective-permute-start(bf16[64,2,4,128]{3,2,1,0:T(4,128)(2,1)} %param.6), channel_id=1, source_target_pairs={{0,4},{4,0},{8,12},{12,8},{16,20},{20,16},{24,28},{28,24},{1,5},{5... | collective-permute-start | bytes 393224 | tf_op jit(solution)/shard_map/ppermute | solution.py:321
  3.1 5.9 %collective-permute-start.1 = (bf16[64,2,4,128]{3,2,1,0:T(4,128)(2,1)}, bf16[64,2,4,128]{3,2,1,0:T(4,128)(2,1)S(1)}, u32[]{:S(2)}, u32[]{:S(2)}) collective-permute-start(bf16[64,2,4,128]{3,2,1,0:T(4,128)(2,1)} %param.6), channel_id=1, source_target_pairs={{0,1},{1,0},{2,3},{3,2},{4,8},{5,9},{6,10},{7,11},{8,4},{9,5},{10,... | collective-permute-start | bytes 393224 | tf_op jit(solution)/shard_map/ppermute | solution.py:320
  4.2 5.1 %collective-permute-start.2 = (bf16[64,2,2,128]{3,2,1,0:T(2,128)(2,1)S(1)}, bf16[64,2,2,128]{3,2,1,0:T(2,128)(2,1)S(1)}, u32[]{:S(2)}, u32[]{:S(2)}) collective-permute-start(bf16[64,2,2,128]{3,2,1,0:T(2,128)(2,1)S(1)} %broadcast_select_fusion), channel_id=1, source_target_pairs={{0,3},{1,2},{2,1},{3,0},{4,7},{5,6},{6,5},{7,4},{8,11},{9,10},{10,... | collective-permute-start | bytes 196616 | tf_op jit(solution)/shard_map/ppermute | solution.py:340
  9.2 4.2 %collective-permute-start.4 = (bf16[384,256]{1,0:T(8,128)(2,1)S(1)}, bf16[384,256]{1,0:T(8,128)(2,1)S(1)}, u32[]{:S(2)}, u32[]{:S(2)}) collective-permute-start(bf16[384,256]{1,0:T(8,128)(2,1)S(1)} %get-tuple-element.43), channel_id=1, source_target_pairs={{0,1},{1,0},{2,3},{3,2},{4,5},{5,4},{6,7},{7,6},{8,9},{9,8},{10,11... | collective-permute-start | bytes 589832 | tf_op jit(solution)/shard_map/ppermute | solution.py:370
  9.3 5.4 %collective-permute-start.3 = (bf16[256,256]{1,0:T(8,128)(2,1)S(1)}, bf16[256,256]{1,0:T(8,128)(2,1)S(1)}, u32[]{:S(2)}, u32[]{:S(2)}) collective-permute-start(bf16[256,256]{1,0:T(8,128)(2,1)S(1)} %get-tuple-element.38), channel_id=1, source_target_pairs={{0,4},{1,2},{2,1},{3,7},{4,0},{5,6},{6,5},{7,3},{8,12},{9,10},{10,... | collective-permute-start | bytes 393224 | tf_op jit(solution)/shard_map/ppermute | solution.py:358
  16.0 3.6 %collective-permute-start.6 = (bf16[128,128]{1,0:T(8,128)(2,1)S(1)}, bf16[128,128]{1,0:T(8,128)(2,1)S(1)}, u32[]{:S(2)}, u32[]{:S(2)}) collective-permute-start(bf16[128,128]{1,0:T(8,128)(2,1)S(1)} %shard_map.68), channel_id=1, source_target_pairs={{0,1},{1,0},{2,3},{3,2},{4,8},{5,9},{6,10},{7,11},{8,4},{9,5},{10,... | collective-permute-start | bytes 98312 | tf_op jit(solution)/shard_map/ppermute | solution.py:388
  16.0 5.4 %collective-permute-start.5 = (bf16[128,128]{1,0:T(8,128)(2,1)S(1)}, bf16[128,128]{1,0:T(8,128)(2,1)S(1)}, u32[]{:S(2)}, u32[]{:S(2)}) collective-permute-start(bf16[128,128]{1,0:T(8,128)(2,1)S(1)} %shard_map.68), channel_id=1, source_target_pairs={{0,4},{4,0},{8,12},{12,8},{16,20},{20,16},{24,28},{28,24},{1,5},{5... | collective-permute-start | bytes 98312 | tf_op jit(solution)/shard_map/ppermute | solution.py:389
  21.5 4.7 %collective-permute-start.7 = (bf16[1,3,128,128]{3,2,1,0:T(8,128)(2,1)S(1)}, bf16[1,3,128,128]{3,2,1,0:T(8,128)(2,1)S(1)}, u32[]{:S(2)}, u32[]{:S(2)}) collective-permute-start(bf16[1,3,128,128]{3,2,1,0:T(8,128)(2,1)S(1)} %maximum_bitcast_fusion.refs_0_), channel_id=1, source_target_pairs={{0,2},{1,3},{2,0},{3,1},{4,6},{5,7},{6,4},{7,5},{8,10},{9,11},{10,... | collective-permute-start | bytes 294920 | tf_op jit(solution)/shard_map/ppermute | solution.py:395
  22.5 3.7 %collective-permute-start.9 = (bf16[1,3,128,128]{3,2,1,0:T(8,128)(2,1)S(1)}, bf16[1,3,128,128]{3,2,1,0:T(8,128)(2,1)S(1)}, u32[]{:S(2)}, u32[]{:S(2)}) collective-permute-start(bf16[1,3,128,128]{3,2,1,0:T(8,128)(2,1)S(1)} %maximum_bitcast_fusion.refs_0_), channel_id=1, source_target_pairs={{0,1},{1,0},{2,3},{3,2},{4,5},{5,4},{6,7},{7,6},{8,9},{9,8},{10,11... | collective-permute-start | bytes 294920 | tf_op jit(solution)/shard_map/ppermute | solution.py:392
  26.2 1.3 %collective-permute-start.8 = (bf16[1,3,128,128]{3,2,1,0:T(8,128)(2,1)S(1)}, bf16[1,3,128,128]{3,2,1,0:T(8,128)(2,1)S(1)}, u32[]{:S(2)}, u32[]{:S(2)}) collective-permute-start(bf16[1,3,128,128]{3,2,1,0:T(8,128)(2,1)S(1)} %collective-permute-done.7.refs_0_), channel_id=1, source_target_pairs={{0,1},{1,0},{2,3},{3,2},{4,5},{5,4},{6,7},{7,6},{8,9},{9,8},{10,11... | collective-permute-start | bytes 294920 | tf_op jit(solution)/shard_map/ppermute | solution.py:399

commit v8 on v7

--- a/solution.py
+++ b/solution.py
@@ -332,10 +332,8 @@
         cost_estimate=cost(10**6, 4 * 10**6),
     )(first_weight, second_weight, third_weight)
     half = height // 2
-    edges = jnp.where(
-        lax.axis_index("narrow") % 2 == 1,
-        stored_features[:, :, half:],
-        stored_features[:, :, :half],
+    edges = lax.dynamic_slice_in_dim(
+        stored_features, lax.axis_index("narrow") % 2 * half, half, axis=2
     )
     crossed_own = lax.ppermute(edges, BOTH, cross_narrow(wide, narrow, True))
     pair, raw, scale, shift = lax.optimization_barrier((pair, stored_features, scale, shift))

time: 28.8 us -> 28.8 us (level)
  other arithmetic: 1.1 us -> 0.01 us
  local copies, waits for them, and re-layouts: 1.23 us -> 2.24 us
    select_n x1 -> x0, other arithmetic: 1.08 us -> none  [body(): jnp.where(lax.axis_index('narrow') % 2 == 1, stored_features[:, :, half:]...]
    dynamic_slice x0 -> x1, local copies, waits for them, and re-layouts: none -> 1.01 us  [body(): lax.dynamic_slice_in_dim(stored_features, lax.axis_index('narrow') % 2 *...]
where the time goes in v8:
time: 28.8 us; the launch traced here: 28.6 us
  starting transfers between devices  11.8 us (41%)
  waiting for transfers between devices  7.94 us (28%)
  Pallas kernels  6.52 us (23%)
  local copies, waits for them, and re-layouts  2.24 us (8%)
    ppermute x1, waiting for transfers between devices, body(): other = lax.ppermute(held, 'narrow', pair_swap(narrow, bit))  3.7 us
    ppermute x1, starting transfers between devices, body(): pooled_pair = lax.ppermute(pooled, 'wide', pair_swap(wide))  3.53 us
    ppermute x1, starting transfers between devices, body(): pair = lax.ppermute(stored_features, 'wide', pair_swap(wide))  3.05 us
    ppermute x1, starting transfers between devices, body(): crossed_rows = lax.ppermute(relay, BOTH, cross_narrow(wide, narrow, False))  2.45 us
    ppermute x1, waiting for transfers between devices, body(): pooled_pair = lax.ppermute(pooled, 'wide', pair_swap(wide))  1.89 us
    pallas_call x1, Pallas kernels, body(): pl.pallas_call(centre_kernel, out_shape=(jax.ShapeDtypeStruct((4 * c1, 4...  1.7 us
    ppermute x1, starting transfers between devices, body(): crossed_own = lax.ppermute(edges, BOTH, cross_narrow(wide, narrow, True))  1.64 us
    ppermute x1, waiting for transfers between devices, body(): pair = lax.ppermute(stored_features, 'wide', pair_swap(wide))  1.54 us
  transfers between devices with their start and end apart: 10, of which 5 were waited for; matrix products, arithmetic and copies ran while one was open for 8% of the time, Pallas kernels for 14%

profile of v8, /device:TPU:0, one launch (start us, length us, event | category | flops | bytes accessed | tf_op | source)
XLA Modules:
  0.0 28.6 jit_solution(16493921705734072815)
XLA Ops:
  0.0 0.0 copy-start.1
  0.0 0.0 copy-start
  0.0 0.0 copy-start.2
  0.0 0.0 copy-start.4
  0.0 0.0 copy-start.3
  0.0 3.0 %collective-permute-start = (bf16[64,2,4,128]{3,2,1,0:T(4,128)(2,1)}, bf16[64,2,4,128]{3,2,1,0:T(4,128)(2,1)S(1)}, u32[]{:S(2)}, u32[]{:S(2)}) collective-permute-start(bf16[64,2,4,128]{3,2,1,0:T(4,128)(2,1)} %param.6), channel_id=1, source_target_pairs={{0,4},{4,0},{8,12},{12,8},{16,20},{20,16},{24,28},{28,24},{1,5},{5... | collective-permute-start | bytes 393224 | tf_op jit(solution)/shard_map/ppermute | solution.py:321
  3.1 0.0 collective-permute-start.1
  3.1 1.0 %constant_dynamic-slice_fusion = bf16[64,2,2,128]{3,2,1,0:T(2,128)(2,1)S(1)} fusion(bf16[64,2,4,128]{3,2,1,0:T(4,128)(2,1)} %param.6, s32[]{:T(128)S(6)} %select_n.11), kind=kLoop, calls=%fused_computation.1 | loop fusion | bytes 131076 | tf_op jit(solution)/shard_map/dynamic_slice | solution.py:335
  4.1 1.6 %collective-permute-start.2 = (bf16[64,2,2,128]{3,2,1,0:T(2,128)(2,1)S(1)}, bf16[64,2,2,128]{3,2,1,0:T(2,128)(2,1)S(1)}, u32[]{:S(2)}, u32[]{:S(2)}) collective-permute-start(bf16[64,2,2,128]{3,2,1,0:T(2,128)(2,1)S(1)} %constant_dynamic-slice_fusion), channel_id=1, source_target_pairs={{0,3},{1,2},{2,1},{3,0},{4,7},{5,6},{6,5},{7,4},{8,11},{9,10},{10,... | collective-permute-start | bytes 196616 | tf_op jit(solution)/shard_map/ppermute | solution.py:338
  5.7 1.2 %copy.9.w2_ref = bf16[128,1728]{1,0:T(8,128)(2,1)S(1)} copy(bf16[128,1728]{0,1:T(8,128)(2,1)} %param.10) | data formatting | bytes 884736 | tf_op args[4]
  6.9 0.0 copy-done
  6.9 0.0 copy-done.2
  7.0 0.4 %shard_map.64 = (bf16[256,3456]{1,0:T(8,128)(2,1)S(1)}, bf16[256,2304]{1,0:T(8,128)(2,1)S(1)}, bf16[576,384]{1,0:T(8,128)(2,1)S(1)}) custom-call(bf16[64,1728]{1,0:T(8,128)(2,1)S(1)} %copy-done.2, bf16[128,1728]{1,0:T(8,128)(2,1)S(1)} %copy.9.w2_ref, bf16[64,3456]{1,0:T(8,128)(2,1)S(1)} %copy-done), custom_call_target="tpu_custom_call" | custom-call | flops 1000000 | bytes 4000000 | tf_op jit(solution)/shard_map/pallas_call | solution.py:322
  7.4 1.5 %collective-permute-done = bf16[64,2,4,128]{3,2,1,0:T(4,128)(2,1)S(1)} collective-permute-done((bf16[64,2,4,128]{3,2,1,0:T(4,128)(2,1)}, bf16[64,2,4,128]{3,2,1,0:T(4,128)(2,1)S(1)}, u32[]{:S(2)}, u32[]{:S(2)}) %collective-permute-start) | collective-permute-done | bytes 131104 | tf_op jit(solution)/shard_map/ppermute | solution.py:321
  8.9 0.0 collective-permute-done.1
  8.9 0.0 copy-done.1
  8.9 0.0 copy-done.4
  9.0 0.0 copy-done.3
  9.0 0.3 shard_map.65
  9.2 0.0 collective-permute-done.2
  9.2 0.1 collective-permute-start.4
  9.3 2.4 %collective-permute-start.3 = (bf16[256,256]{1,0:T(8,128)(2,1)S(1)}, bf16[256,256]{1,0:T(8,128)(2,1)S(1)}, u32[]{:S(2)}, u32[]{:S(2)}) collective-permute-start(bf16[256,256]{1,0:T(8,128)(2,1)S(1)} %get-tuple-element.38), channel_id=1, source_target_pairs={{0,4},{1,2},{2,1},{3,7},{4,0},{5,6},{6,5},{7,3},{8,12},{9,10},{10,... | collective-permute-start | bytes 393224 | tf_op jit(solution)/shard_map/ppermute | solution.py:356
  11.8 1.7 %shard_map.66 = (f32[256,512]{1,0:T(8,128)S(1)}, f32[256,512]{1,0:T(8,128)S(1)}) custom-call(bf16[384,512]{1,0:T(8,128)(2,1)S(1)} %get-tuple-element.39.x_ref, bf16[256,3456]{1,0:T(8,128)(2,1)S(1)} %get-tuple-element.40.w1_ref, bf16[256,2304]{1,0:T(8,128)(2,1)S(1)} %get-tuple-element.41.w2_ref), custom_call_target="tpu_custom_call" | custom-call | flops 10000000 | bytes 100000 | tf_op jit(solution)/shard_map/pallas_call | solution.py:357
  13.5 0.0 collective-permute-done.4.rows_ref
  13.5 1.0 %shard_map.67.p2_ref = f32[256,512]{1,0:T(8,128)S(1)} custom-call(bf16[384,256]{1,0:T(8,128)(2,1)S(1)} %collective-permute-done.4.rows_ref, f32[256,512]{1,0:T(8,128)S(1)} %get-tuple-element.42.p1_ref, f32[256,512]{1,0:T(8,128)S(1)} %get-tuple-element.44.p2_ref, bf16[256,3456]{1,0:T(8,128)(2,1)S(1)} %get-tuple-element.40.w1_ref, ...), custom_call_target="tpu_custom_call" | custom-call | flops 10000000 | bytes 100000 | tf_op jit(solution)/shard_map/pallas_call | solution.py:369
  14.5 0.2 collective-permute-done.3.rows_ref
  14.7 1.2 %shard_map.68 = bf16[128,128]{1,0:T(8,128)(2,1)S(1)} custom-call(bf16[256,128]{1,0:T(8,128)(2,1)S(1)} %bitcast.16, bf16[256,256]{1,0:T(8,128)(2,1)S(1)} %collective-permute-done.3.rows_ref, f32[1,64]{1,0:T(1,128)S(1)} %bitcast.18, f32[1,64]{1,0:T(1,128)S(1)} %bitcast.20, f32[256,512]{1,0:T(8,128)S(1)} %get-tuple-element.42.p1_ref, ...), custom_call_target="tpu_custom_call" | custom-call | flops 10000000 | bytes 100000 | tf_op jit(solution)/shard_map/pallas_call | solution.py:377
  16.0 0.1 collective-permute-start.6
  16.0 3.5 %collective-permute-start.5 = (bf16[128,128]{1,0:T(8,128)(2,1)S(1)}, bf16[128,128]{1,0:T(8,128)(2,1)S(1)}, u32[]{:S(2)}, u32[]{:S(2)}) collective-permute-start(bf16[128,128]{1,0:T(8,128)(2,1)S(1)} %shard_map.68), channel_id=1, source_target_pairs={{0,4},{4,0},{8,12},{12,8},{16,20},{20,16},{24,28},{28,24},{1,5},{5... | collective-permute-start | bytes 98312 | tf_op jit(solution)/shard_map/ppermute | solution.py:387
  19.6 0.0 collective-permute-done.6
  19.6 1.9 %collective-permute-done.5 = bf16[128,128]{1,0:T(8,128)(2,1)S(1)} collective-permute-done((bf16[128,128]{1,0:T(8,128)(2,1)S(1)}, bf16[128,128]{1,0:T(8,128)(2,1)S(1)}, u32[]{:S(2)}, u32[]{:S(2)}) %collective-permute-start.5) | collective-permute-done | bytes 32800 | tf_op jit(solution)/shard_map/ppermute | solution.py:387
  21.5 1.0 %collective-permute-start.7 = (bf16[1,3,128,128]{3,2,1,0:T(8,128)(2,1)S(1)}, bf16[1,3,128,128]{3,2,1,0:T(8,128)(2,1)S(1)}, u32[]{:S(2)}, u32[]{:S(2)}) collective-permute-start(bf16[1,3,128,128]{3,2,1,0:T(8,128)(2,1)S(1)} %maximum_bitcast_fusion.refs_0_), channel_id=1, source_target_pairs={{0,2},{1,3},{2,0},{3,1},{4,6},{5,7},{6,4},{7,5},{8,10},{9,11},{10,... | collective-permute-start | bytes 294920 | tf_op jit(solution)/shard_map/ppermute | solution.py:393
  22.5 0.0 collective-permute-start.9
  22.5 3.7 %collective-permute-done.7.refs_0_ = bf16[1,3,128,128]{3,2,1,0:T(8,128)(2,1)S(1)} collective-permute-done((bf16[1,3,128,128]{3,2,1,0:T(8,128)(2,1)S(1)}, bf16[1,3,128,128]{3,2,1,0:T(8,128)(2,1)S(1)}, u32[]{:S(2)}, u32[]{:S(2)}) %collective-permute-start.7) | collective-permute-done | bytes 98336 | tf_op jit(solution)/shard_map/ppermute | solution.py:393
  26.2 0.0 collective-permute-start.8
  26.2 0.0 collective-permute-done.9.refs_1_
  26.2 0.4 %shard_map.69.refs_2_ = f32[576,512]{1,0:T(8,128)S(1)} custom-call(bf16[1,3,128,128]{3,2,1,0:T(8,128)(2,1)S(1)} %maximum_bitcast_fusion.refs_0_, bf16[1,3,128,128]{3,2,1,0:T(8,128)(2,1)S(1)} %collective-permute-done.9.refs_1_, bf16[576,384]{1,0:T(8,128)(2,1)S(1)} %get-tuple-element.45.refs_2_.refs_1_.w3_ref), custom_call_target="tpu_custom_call" | custom-call | flops 10000000 | bytes 100000 | tf_op jit(solution)/shard_map/pallas_call | solution.py:419
  26.6 0.3 %shard_map.70.before_ref = f32[576,512]{1,0:T(8,128)S(1)} custom-call(bf16[1,3,128,128]{3,2,1,0:T(8,128)(2,1)S(1)} %collective-permute-done.7.refs_0_, bf16[576,384]{1,0:T(8,128)(2,1)S(1)} %get-tuple-element.45.refs_2_.refs_1_.w3_ref, f32[576,512]{1,0:T(8,128)S(1)} %shard_map.69.refs_2_), custom_call_target="tpu_custom_call", output_to_operand_aliasing={{}: (2, {})} | custom-call | flops 10000000 | bytes 100000 | tf_op jit(solution)/shard_map/pallas_call | solution.py:419
  26.9 0.6 %collective-permute-done.8.blocks_ref = bf16[1,3,128,128]{3,2,1,0:T(8,128)(2,1)S(1)} collective-permute-done((bf16[1,3,128,128]{3,2,1,0:T(8,128)(2,1)S(1)}, bf16[1,3,128,128]{3,2,1,0:T(8,128)(2,1)S(1)}, u32[]{:S(2)}, u32[]{:S(2)}) %collective-permute-start.8) | collective-permute-done | bytes 98336 | tf_op jit(solution)/shard_map/ppermute | solution.py:397
  27.5 1.2 %shard_map.71 = (bf16[64,512]{1,0:T(8,128)(2,1)}, f32[576,512]{1,0:T(8,128)S(1)}) custom-call(bf16[1,3,128,128]{3,2,1,0:T(8,128)(2,1)S(1)} %collective-permute-done.8.blocks_ref, bf16[576,384]{1,0:T(8,128)(2,1)S(1)} %get-tuple-element.45.refs_2_.refs_1_.w3_ref, f32[576,512]{1,0:T(8,128)S(1)} %shard_map.70.before_ref), custom_call_target="tpu_custom_call", output_to_operand_aliasing={{1}: (2, {})} | custom-call | flops 10000000 | bytes 100000 | tf_op jit(solution)/shard_map/pallas_call | solution.py:429
  (1 shorter events, 0.0 us)
Async XLA Ops:
  0.0 8.9 %copy-start.1 = (bf16[64,2,4,128]{3,2,1,0:T(4,128)(2,1)S(1)}, bf16[64,2,4,128]{3,2,1,0:T(4,128)(2,1)}, u32[]{:S(2)}) copy-start(bf16[64,2,4,128]{3,2,1,0:T(4,128)(2,1)} %param.6) | copy-start | bytes 393220
  0.0 6.9 %copy-start = (bf16[64,3456]{1,0:T(8,128)(2,1)S(1)}, bf16[64,3456]{1,0:T(8,128)(2,1)}, u32[]{:S(2)}) copy-start(bf16[64,3456]{1,0:T(8,128)(2,1)} %w3_ref.1) | copy-start | bytes 1327108
  0.0 6.9 %copy-start.2 = (bf16[64,1728]{1,0:T(8,128)(2,1)S(1)}, bf16[64,1728]{1,0:T(8,128)(2,1)}, u32[]{:S(2)}) copy-start(bf16[64,1728]{1,0:T(8,128)(2,1)} %w1_ref.1) | copy-start | bytes 663556
  0.0 8.9 %copy-start.4 = (f32[64]{0:T(128)S(1)}, f32[64]{0:T(128)}, u32[]{:S(2)}) copy-start(f32[64]{0:T(128)} %param.8) | copy-start | bytes 772
  0.0 8.9 %copy-start.3 = (f32[64]{0:T(128)S(1)}, f32[64]{0:T(128)}, u32[]{:S(2)}) copy-start(f32[64]{0:T(128)} %param.7) | copy-start | bytes 772
  0.0 8.9 %collective-permute-start = (bf16[64,2,4,128]{3,2,1,0:T(4,128)(2,1)}, bf16[64,2,4,128]{3,2,1,0:T(4,128)(2,1)S(1)}, u32[]{:S(2)}, u32[]{:S(2)}) collective-permute-start(bf16[64,2,4,128]{3,2,1,0:T(4,128)(2,1)} %param.6), channel_id=1, source_target_pairs={{0,4},{4,0},{8,12},{12,8},{16,20},{20,16},{24,28},{28,24},{1,5},{5... | collective-permute-start | bytes 393224 | tf_op jit(solution)/shard_map/ppermute | solution.py:321
  3.1 5.9 %collective-permute-start.1 = (bf16[64,2,4,128]{3,2,1,0:T(4,128)(2,1)}, bf16[64,2,4,128]{3,2,1,0:T(4,128)(2,1)S(1)}, u32[]{:S(2)}, u32[]{:S(2)}) collective-permute-start(bf16[64,2,4,128]{3,2,1,0:T(4,128)(2,1)} %param.6), channel_id=1, source_target_pairs={{0,1},{1,0},{2,3},{3,2},{4,8},{5,9},{6,10},{7,11},{8,4},{9,5},{10,... | collective-permute-start | bytes 393224 | tf_op jit(solution)/shard_map/ppermute | solution.py:320
  4.1 5.2 %collective-permute-start.2 = (bf16[64,2,2,128]{3,2,1,0:T(2,128)(2,1)S(1)}, bf16[64,2,2,128]{3,2,1,0:T(2,128)(2,1)S(1)}, u32[]{:S(2)}, u32[]{:S(2)}) collective-permute-start(bf16[64,2,2,128]{3,2,1,0:T(2,128)(2,1)S(1)} %constant_dynamic-slice_fusion), channel_id=1, source_target_pairs={{0,3},{1,2},{2,1},{3,0},{4,7},{5,6},{6,5},{7,4},{8,11},{9,10},{10,... | collective-permute-start | bytes 196616 | tf_op jit(solution)/shard_map/ppermute | solution.py:338
  9.2 4.2 %collective-permute-start.4 = (bf16[384,256]{1,0:T(8,128)(2,1)S(1)}, bf16[384,256]{1,0:T(8,128)(2,1)S(1)}, u32[]{:S(2)}, u32[]{:S(2)}) collective-permute-start(bf16[384,256]{1,0:T(8,128)(2,1)S(1)} %get-tuple-element.43), channel_id=1, source_target_pairs={{0,1},{1,0},{2,3},{3,2},{4,5},{5,4},{6,7},{7,6},{8,9},{9,8},{10,11... | collective-permute-start | bytes 589832 | tf_op jit(solution)/shard_map/ppermute | solution.py:368
  9.3 5.4 %collective-permute-start.3 = (bf16[256,256]{1,0:T(8,128)(2,1)S(1)}, bf16[256,256]{1,0:T(8,128)(2,1)S(1)}, u32[]{:S(2)}, u32[]{:S(2)}) collective-permute-start(bf16[256,256]{1,0:T(8,128)(2,1)S(1)} %get-tuple-element.38), channel_id=1, source_target_pairs={{0,4},{1,2},{2,1},{3,7},{4,0},{5,6},{6,5},{7,3},{8,12},{9,10},{10,... | collective-permute-start | bytes 393224 | tf_op jit(solution)/shard_map/ppermute | solution.py:356
  16.0 3.6 %collective-permute-start.6 = (bf16[128,128]{1,0:T(8,128)(2,1)S(1)}, bf16[128,128]{1,0:T(8,128)(2,1)S(1)}, u32[]{:S(2)}, u32[]{:S(2)}) collective-permute-start(bf16[128,128]{1,0:T(8,128)(2,1)S(1)} %shard_map.68), channel_id=1, source_target_pairs={{0,1},{1,0},{2,3},{3,2},{4,8},{5,9},{6,10},{7,11},{8,4},{9,5},{10,... | collective-permute-start | bytes 98312 | tf_op jit(solution)/shard_map/ppermute | solution.py:386
  16.0 5.4 %collective-permute-start.5 = (bf16[128,128]{1,0:T(8,128)(2,1)S(1)}, bf16[128,128]{1,0:T(8,128)(2,1)S(1)}, u32[]{:S(2)}, u32[]{:S(2)}) collective-permute-start(bf16[128,128]{1,0:T(8,128)(2,1)S(1)} %shard_map.68), channel_id=1, source_target_pairs={{0,4},{4,0},{8,12},{12,8},{16,20},{20,16},{24,28},{28,24},{1,5},{5... | collective-permute-start | bytes 98312 | tf_op jit(solution)/shard_map/ppermute | solution.py:387
  21.5 4.7 %collective-permute-start.7 = (bf16[1,3,128,128]{3,2,1,0:T(8,128)(2,1)S(1)}, bf16[1,3,128,128]{3,2,1,0:T(8,128)(2,1)S(1)}, u32[]{:S(2)}, u32[]{:S(2)}) collective-permute-start(bf16[1,3,128,128]{3,2,1,0:T(8,128)(2,1)S(1)} %maximum_bitcast_fusion.refs_0_), channel_id=1, source_target_pairs={{0,2},{1,3},{2,0},{3,1},{4,6},{5,7},{6,4},{7,5},{8,10},{9,11},{10,... | collective-permute-start | bytes 294920 | tf_op jit(solution)/shard_map/ppermute | solution.py:393
  22.5 3.7 %collective-permute-start.9 = (bf16[1,3,128,128]{3,2,1,0:T(8,128)(2,1)S(1)}, bf16[1,3,128,128]{3,2,1,0:T(8,128)(2,1)S(1)}, u32[]{:S(2)}, u32[]{:S(2)}) collective-permute-start(bf16[1,3,128,128]{3,2,1,0:T(8,128)(2,1)S(1)} %maximum_bitcast_fusion.refs_0_), channel_id=1, source_target_pairs={{0,1},{1,0},{2,3},{3,2},{4,5},{5,4},{6,7},{7,6},{8,9},{9,8},{10,11... | collective-permute-start | bytes 294920 | tf_op jit(solution)/shard_map/ppermute | solution.py:390
  26.2 1.3 %collective-permute-start.8 = (bf16[1,3,128,128]{3,2,1,0:T(8,128)(2,1)S(1)}, bf16[1,3,128,128]{3,2,1,0:T(8,128)(2,1)S(1)}, u32[]{:S(2)}, u32[]{:S(2)}) collective-permute-start(bf16[1,3,128,128]{3,2,1,0:T(8,128)(2,1)S(1)} %collective-permute-done.7.refs_0_), channel_id=1, source_target_pairs={{0,1},{1,0},{2,3},{3,2},{4,5},{5,4},{6,7},{7,6},{8,9},{9,8},{10,11... | collective-permute-start | bytes 294920 | tf_op jit(solution)/shard_map/ppermute | solution.py:397
